TPU v7x, 512 devices: a whole 4x4x16 slice. The times are simulated.
512 devices in a mesh: replica: 64 (over z_lo, x, core), fsdp: 8 (over y, z_hi).
Axes of the slice: x: 4, y: 4, z: 16 (z_hi: 2, z_lo: 8; z = z_hi * 8 + z_lo), core: 2. Of those that a mesh axis runs over, the one named last changes fastest.
Arguments:
- hidden_in: bfloat16 [131072, 7168], P(('replica', 'fsdp')), may hold values from -6 to 6
- norm_gain: float32 [7168], replicated, may hold values from 0.5 to 1.5
- proj_weight: bfloat16 [7168, 512], P('fsdp'), may hold values from -0.0625 to 0.0625
- replica_params: bfloat16 [64, 7168, 512], P('replica', 'fsdp'), may hold values from -120 to 120, as said below
- outer_params: float32 [7168, 512], P(('fsdp', 'replica')), may hold values from -6 to 6
- momentum: float32 [7168, 512], P(('fsdp', 'replica')), may hold values from -6 to 6
Outputs:
- projected: bfloat16 [131072, 512], P(('replica', 'fsdp'))
- new_outer: float32 [7168, 512], P(('fsdp', 'replica'))
- new_momentum: float32 [7168, 512], P(('fsdp', 'replica'))
Inputs may be any that keep to these rules, and one draw needn't show every extreme that they name: `replica_params`: finite values of varying size.
All inputs are finite; a program needn't handle non-finite values.
Results may differ from a plain program's by a relative error of at most 0.0049.
Values may be sent and summed in bfloat16 or wider, within the bound.
No kernel may reach another device: no remote copies, remote signals or barrier semaphores. Data moves between devices by JAX's collectives and lax.ppermute only.
A program may use at most 64 MiB of HBM per device.

v0:
```python
import jax
import jax.numpy as jnp
from jax import lax
from jax.sharding import PartitionSpec as P

D = 7168
KV = 512


OUTER_LR = 0.7
MOMENTUM_DECAY = 0.9
CLIP_RATIO = 0.25


def on_device(hidden_in, norm_gain, proj_weight, replica_params, outer_params, momentum):
    values = hidden_in.astype(jnp.float32)
    scaled = lax.rsqrt(jnp.mean(values * values, axis=1, keepdims=True) + 1e-05)
    normed = (values * scaled * norm_gain).astype(jnp.bfloat16)
    keys_total = jnp.dot(
        normed,
        lax.all_gather(proj_weight, "fsdp", axis=0, tiled=True),
        preferred_element_type=jnp.float32,
    )
    projected = keys_total.astype(jnp.bfloat16)
    local_params = replica_params[0].astype(jnp.float32)
    share_rows = outer_params.shape[0]
    whole_sum = lax.psum(local_params, "replica")
    first_row = lax.axis_index("replica") * share_rows
    summed = lax.dynamic_slice_in_dim(whole_sum, first_row, share_rows, 0)
    delta = outer_params - summed / lax.axis_size("replica")
    squares = lax.psum(jnp.sum(delta * delta), ("replica", "fsdp"))
    length = jnp.sqrt(squares)
    factor = jnp.minimum(1.0, CLIP_RATIO * jnp.sqrt(jnp.float32(D * KV)) / (length + 1e-06))
    clipped = factor * delta
    new_momentum = MOMENTUM_DECAY * momentum + clipped
    new_outer = outer_params - OUTER_LR * (clipped + MOMENTUM_DECAY * new_momentum)
    return (projected, new_outer, new_momentum)


def solution(mesh):
    in_specs = (
        P(("replica", "fsdp"), None),
        P(),
        P("fsdp", None),
        P("replica", "fsdp", None),
        P(("fsdp", "replica"), None),
        P(("fsdp", "replica"), None),
    )
    out_specs = (
        P(("replica", "fsdp"), None),
        P(("fsdp", "replica"), None),
        P(("fsdp", "replica"), None),
    )
    return jax.shard_map(
        on_device, mesh=mesh, in_specs=in_specs, out_specs=out_specs, check_vma=False
    )
```

profile of v0, /device:TPU:1, one launch (start us, length us, event | category | flops | bytes accessed | tf_op | source)
XLA Modules:
  0.0 1141.1 jit_solution(1452082678008156838)
XLA Ops:
  8.0 0.0 copy-start
  8.0 0.0 copy-start.1
  8.0 0.0 copy-start.2
  8.0 0.0 all-reduce.2.cloned.1.call-start
  8.1 2.7 bitcast_convert_fusion
  10.8 0.0 all-reduce.2.cloned.1.call-update
  10.8 0.0 all-gather.2.cloned.1.call-start
  10.8 0.5 all-gather.2.cloned.1.call-update
  11.4 2.9 fusion
  14.2 1004.1 %all-reduce.2.cloned.1.call-done = f32[896,512]{1,0:T(8,128)} async-done(((f32[896,512]{1,0:T(8,128)}), f32[896,512]{1,0:T(8,128)}) %all-reduce.2.cloned.1.call-update) | async-done | bytes 1835024 | tf_op jit(solution)/shard_map/psum | solution.py:27
  1018.3 0.0 copy-done
  1018.3 1.4 multiply_reduce_fusion
  1019.7 104.7 %psum.15 = f32[]{:T(128)} all-reduce(f32[]{:T(128)} %multiply_reduce_fusion), channel_id=1, replica_groups=mesh['replica'=64,'fsdp'=8] {'replica','fsdp'}, use_global_device_ids=true, to_apply=%region_3.0 | all-reduce | flops 1 | bytes 8 | tf_op jit(solution)/shard_map/psum | solution.py:31
  1125.2 0.0 copy-done.1
  1125.2 1.4 multiply_subtract_fusion
  1126.7 0.0 all-gather.2.cloned.1.call-done
  1126.7 0.0 copy-done.2
  1126.7 7.0 fusion.7
  (1 shorter events, 0.0 us)
Async XLA Ops:
  8.0 1010.3 %copy-start = (f32[14,512]{1,0:T(8,128)S(1)}, f32[14,512]{1,0:T(8,128)}, u32[]{:S(2)}) copy-start(f32[14,512]{1,0:T(8,128)} %param.10) | copy-start | bytes 86020
  8.0 1117.2 %copy-start.1 = (f32[14,512]{1,0:T(8,128)S(1)}, f32[14,512]{1,0:T(8,128)}, u32[]{:S(2)}) copy-start(f32[14,512]{1,0:T(8,128)} %param.11) | copy-start | bytes 86020
  8.0 1118.7 %copy-start.2 = (f32[7168]{0:T(1024)S(1)}, f32[7168]{0:T(1024)}, u32[]{:S(2)}) copy-start(f32[7168]{0:T(1024)} %param.7) | copy-start | bytes 86020
  8.0 1010.3 %all-reduce.2.cloned.1.call-start = ((), (), s32[]{:S(2)}) async-start(), calls=%async_computation.1 | async-start | bytes 3670016 | tf_op jit(solution)/shard_map/psum | solution.py:27
  10.8 1115.9 %all-gather.2.cloned.1.call-start = ((), (), s32[]{:S(2)}) async-start(), calls=%async_computation | async-start | bytes 8257536 | tf_op jit(solution)/shard_map/all_gather | solution.py:21
Sparse Core Ops, SparseCore 0:
  11.8 1006.4 all-reduce.1
Sparse Core Ops, SparseCore 1:
  14.5 253.2 all-gather.1
where the time goes:
time: 1140 us
  waiting for transfers between devices  1000 us (88%)
  blocking collectives  105 us (9%)
  between operations  16.3 us (1%)
    psum x1, waiting for transfers between devices, on_device(): whole_sum = lax.psum(local_params, 'replica')  1000 us
    psum x1, blocking collectives, on_device(): squares = lax.psum(jnp.sum(delta * delta), ('replica', 'fsdp'))  105 us
  transfers between devices with their start and end apart: 2, of which 1 were waited for; matrix products, arithmetic and copies ran while one was open for 1% of the time, Pallas kernels for 0%

commit v1 on v0

v1 whole, which is shorter than its diff:
```python
import functools

import jax
import jax.numpy as jnp
from jax import lax
from jax.experimental import pallas as pl
from jax.experimental.pallas import tpu as pltpu
from jax.sharding import Mesh, PartitionSpec as P

D = 7168
KV = 512

OUTER_LR = 0.7
MOMENTUM_DECAY = 0.9
CLIP_RATIO = 0.25

NAMES = ("z_lo", "x", "core", "y", "z_hi")
SIZES = (8, 4, 2, 4, 2)
N_REPLICA = 64
SHARE = 14
ROWS = 896
PIECE = 112
LANES = 128
F32 = jnp.float32
BF16 = jnp.bfloat16
VMEM = pl.BlockSpec(memory_space=pltpu.VMEM)
PARAMS = pltpu.CompilerParams(vmem_limit_bytes=48 * 1024 * 1024)


def call(body, name, out, n_in, scratch=()):
    many = isinstance(out, (tuple, list))
    return pl.pallas_call(
        body,
        name=name,
        out_shape=out,
        in_specs=[VMEM] * n_in,
        out_specs=[VMEM] * len(out) if many else VMEM,
        scratch_shapes=list(scratch),
        compiler_params=PARAMS,
    )


def regroup_body(src, out, wide, grouped):
    wide[...] = src[...].astype(F32)
    for xc in range(8):
        for z in range(8):
            first = PIECE * z + SHARE * xc
            grouped[xc, SHARE * z : SHARE * (z + 1), :] = wide[first : first + SHARE, :]
        out[xc] = grouped[xc].astype(BF16)


def first_sum_body(parts, out, total):
    total[...] = functools.reduce(lambda a, b: a + b, [parts[i].astype(F32) for i in range(8)])
    for z in range(8):
        for j in range(4):
            out[z, SHARE * j : SHARE * (j + 1), :] = total[SHARE * z : SHARE * (z + 1), LANES * j : LANES * (j + 1)]


def second_sum_body(parts, outer, delta, squares, total):
    total[...] = functools.reduce(lambda a, b: a + b, [parts[i] for i in range(8)])
    for j in range(4):
        cols = slice(LANES * j, LANES * (j + 1))
        delta[:, cols] = outer[:, cols] - total[SHARE * j : SHARE * (j + 1), :] / N_REPLICA
    d = delta[...]
    line = jnp.sum(d * d, axis=0, keepdims=True)
    line = line[:, :128] + line[:, 128:256] + line[:, 256:384] + line[:, 384:]
    squares[...] = jnp.broadcast_to(line[None], squares.shape)


def spread_sum_body(parts, out):
    out[...] = jnp.broadcast_to(jnp.sum(parts[...], axis=0, keepdims=True), out.shape)


def update_body(parts, delta, outer, momentum, new_outer, new_momentum):
    lanes = jnp.sum(parts[...], axis=0)[:1]
    length = jnp.sqrt(jnp.sum(lanes, axis=1, keepdims=True))
    limit = CLIP_RATIO * jnp.sqrt(jnp.full((1, 1), D * KV, F32))
    factor = jnp.minimum(1.0, limit / (length + 1e-06))
    clipped = factor * delta[...]
    moved = MOMENTUM_DECAY * momentum[...] + clipped
    new_momentum[...] = moved
    new_outer[...] = outer[...] - OUTER_LR * (clipped + MOMENTUM_DECAY * moved)


def norm_body(hidden, gain, out):
    values = hidden[...].astype(F32)
    scaled = lax.rsqrt(jnp.mean(values * values, axis=1, keepdims=True) + 1e-05)
    out[...] = (values * scaled * gain[...]).astype(BF16)


def norm(hidden, gain):
    rows, block = hidden.shape[0], 32
    return pl.pallas_call(
        norm_body,
        name="norm",
        grid=(rows // block,),
        out_shape=jax.ShapeDtypeStruct(hidden.shape, BF16),
        in_specs=[pl.BlockSpec((block, D), lambda i: (i, 0)), pl.BlockSpec((1, D), lambda i: (0, 0))],
        out_specs=pl.BlockSpec((block, D), lambda i: (i, 0)),
        compiler_params=PARAMS,
        cost_estimate=pl.CostEstimate(flops=5 * rows * D, bytes_accessed=4 * rows * D, transcendentals=rows),
    )(hidden, gain)


def project_body(half, left, right, own, other, out, total):
    @pl.when(pl.program_id(0) == 0)
    def _():
        total[...] = jnp.zeros_like(total)

    total[...] += jnp.dot(left[...], own[...], preferred_element_type=F32) + jnp.dot(
        right[...], other[...], preferred_element_type=F32
    )

    @pl.when(pl.program_id(0) == pl.num_programs(0) - 1)
    def _():
        out[...] = total[...].astype(BF16)


def project(half, normed, own, other):
    rows, cols = normed.shape[0], own.shape[1]
    return pl.pallas_call(
        project_body,
        name="project",
        out_shape=jax.ShapeDtypeStruct((rows, cols), BF16),
        grid_spec=pltpu.PrefetchScalarGridSpec(
            num_scalar_prefetch=1,
            grid=(4,),
            in_specs=[
                pl.BlockSpec((rows, ROWS), lambda y, h: (0, 2 * y + h[0])),
                pl.BlockSpec((rows, ROWS), lambda y, h: (0, 2 * y + 1 - h[0])),
                pl.BlockSpec((ROWS, cols), lambda y, h: (y, 0)),
                pl.BlockSpec((ROWS, cols), lambda y, h: (y, 0)),
            ],
            out_specs=pl.BlockSpec((rows, cols), lambda y, h: (0, 0)),
            scratch_shapes=[pltpu.VMEM((rows, cols), F32)],
        ),
        compiler_params=PARAMS,
        cost_estimate=pl.CostEstimate(
            flops=2 * rows * D * cols, bytes_accessed=2 * (D * cols + rows * D), transcendentals=0
        ),
    )(half, normed, normed, own, other)


def on_device(hidden_in, norm_gain, proj_weight, replica_params, outer_params, momentum):
    share = outer_params.shape
    f32 = lambda *dims: jax.ShapeDtypeStruct(dims, F32)
    grouped = call(
        regroup_body, "regroup", jax.ShapeDtypeStruct((8, PIECE, KV), BF16), 1,
        [pltpu.VMEM((ROWS, KV), F32), pltpu.VMEM((8, PIECE, KV), F32)],
    )(replica_params[0])
    grouped = lax.all_to_all(grouped, ("x", "core"), 0, 0)
    pieces = call(first_sum_body, "first_sum", f32(8, 56, LANES), 1, [pltpu.VMEM((PIECE, KV), F32)])(grouped)
    pieces = lax.all_to_all(pieces, "z_lo", 0, 0)
    delta, squares = call(
        second_sum_body, "second_sum", (f32(*share), f32(32, 8, LANES)), 2, [pltpu.VMEM((56, LANES), F32)]
    )(pieces, outer_params)
    squares = lax.all_to_all(squares, ("y", "x", "core"), 0, 0)
    squares = call(spread_sum_body, "spread_sum", f32(16, 8, LANES), 1)(squares)
    squares = lax.all_to_all(squares, ("z_lo", "z_hi"), 0, 0)
    new_outer, new_momentum = call(update_body, "update", (f32(*share), f32(*share)), 4)(
        squares, delta, outer_params, momentum
    )

    place = lax.axis_index("x") * 2 + lax.axis_index("core")
    half = lax.axis_index("z_hi")
    mine = lax.dynamic_slice_in_dim(proj_weight, place * PIECE, PIECE, 0)
    mirror = [(2 * z + h, 2 * (7 - z) + 1 - h) for z in range(8) for h in range(2)]
    theirs = lax.ppermute(mine, ("z_lo", "z_hi"), mirror)
    own = lax.all_gather(mine, ("y", "x", "core"), axis=0, tiled=True)
    other = lax.all_gather(theirs, ("y", "x", "core"), axis=0, tiled=True)
    normed = norm(hidden_in, norm_gain.reshape(1, -1))
    projected = project(half.astype(jnp.int32).reshape(1), normed, own, other)
    return (projected, new_outer, new_momentum)


def solution(mesh):
    inner = Mesh(mesh.devices.reshape(SIZES), NAMES)
    replica, fsdp = NAMES[:3], NAMES[3:]
    in_specs = (
        P(replica + fsdp, None),
        P(),
        P(fsdp, None),
        P(replica, fsdp, None),
        P(fsdp + replica, None),
        P(fsdp + replica, None),
    )
    out_specs = (
        P(replica + fsdp, None),
        P(fsdp + replica, None),
        P(fsdp + replica, None),
    )
    return jax.shard_map(
        on_device, mesh=inner, in_specs=in_specs, out_specs=out_specs, check_vma=False
    )
```

time: 1140 us -> 159 us (0.14)
  waiting for transfers between devices: 1000 us -> 49 us
  blocking collectives: 105 us -> 54.2 us
  starting transfers between devices: 0.08 us -> 19.5 us
  Pallas kernels: 0 us -> 13.8 us
    psum x1 -> x0, waiting for transfers between devices: 1000 us -> none  [on_device(): whole_sum = lax.psum(local_params, 'replica')]
    psum x1 -> x0, blocking collectives: 105 us -> none  [on_device(): squares = lax.psum(jnp.sum(delta * delta), ('replica', 'fsdp'))]
    all_to_all x0 -> x3, blocking collectives: none -> 54.2 us  [the longest x1 19.5 us: on_device(): grouped = lax.all_to_all(grouped, ('x', 'core'), 0, 0)]
    all_gather x1 -> x2, waiting for transfers between devices: 0.01 us -> 33.6 us  [the longest x1 33.6 us: on_device(): other = lax.all_gather(theirs, ('y', 'x', 'core'), axis=0, tiled=True)]
    pallas_call x0 -> x7, Pallas kernels: none -> 13.8 us  [the longest x1 6.26 us: project(): pl.pallas_call(project_body, name='project', out_shape=jax.ShapeDtypeStru...]
    ppermute x0 -> x1, starting transfers between devices: none -> 12 us  [on_device(): theirs = lax.ppermute(mine, ('z_lo', 'z_hi'), mirror)]
  transfers between devices with their start and end apart: 2 -> 4, of which waited for: 1 -> 3; matrix products, arithmetic and copies ran while one was open for 1% -> 0% of each run, Pallas kernels for 0% -> 5%
where the time goes in v1:
time: 159 us; the launch traced here: 158 us
  blocking collectives  54.2 us (34%)
  waiting for transfers between devices  49 us (31%)
  starting transfers between devices  19.5 us (12%)
  between operations  14.1 us (9%)
  Pallas kernels  13.8 us (9%)
  local copies, waits for them, and re-layouts  7.53 us (5%)
    all_gather x1, waiting for transfers between devices, on_device(): other = lax.all_gather(theirs, ('y', 'x', 'core'), axis=0, tiled=True)  33.6 us
    all_to_all x1, blocking collectives, on_device(): grouped = lax.all_to_all(grouped, ('x', 'core'), 0, 0)  19.5 us
    all_to_all x1, blocking collectives, on_device(): pieces = lax.all_to_all(pieces, 'z_lo', 0, 0)  17.7 us
    all_to_all x1, blocking collectives, on_device(): squares = lax.all_to_all(squares, ('y', 'x', 'core'), 0, 0)  16.9 us
    ppermute x1, starting transfers between devices, on_device(): theirs = lax.ppermute(mine, ('z_lo', 'z_hi'), mirror)  12 us
    ppermute x1, waiting for transfers between devices, on_device(): theirs = lax.ppermute(mine, ('z_lo', 'z_hi'), mirror)  10.8 us
    all_to_all x1, starting transfers between devices, on_device(): squares = lax.all_to_all(squares, ('z_lo', 'z_hi'), 0, 0)  7.47 us
    unnamed x16, local copies, waits for them, and re-layouts  6.88 us
  transfers between devices with their start and end apart: 4, of which 3 were waited for; matrix products, arithmetic and copies ran while one was open for 0% of the time, Pallas kernels for 5%

profile of v1, /device:TPU:1, one launch (start us, length us, event | category | flops | bytes accessed | tf_op | source)
XLA Modules:
  0.0 158.2 jit_solution(3928121974901874870)
XLA Ops:
  7.2 0.0 copy-start
  7.2 0.0 copy-start.4
  7.2 0.0 copy-start.6
  7.2 0.0 all-gather.3.cloned.1.call-start
  7.3 1.1 copy-done
  8.4 0.7 constant_dynamic-slice_fusion
  9.0 0.0 all-gather.3.cloned.1.call-update
  9.0 0.0 all-gather.5.cloned.1.call-start
  9.1 12.0 %collective-permute-start = (bf16[112,512]{1,0:T(8,128)(2,1)}, bf16[112,512]{1,0:T(8,128)(2,1)S(1)}, u32[]{:S(2)}, u32[]{:S(2)}) collective-permute-start(bf16[112,512]{1,0:T(8,128)(2,1)} %constant_dynamic-slice_fusion), channel_id=1, source_target_pairs={{0,449},{1,448},{64,385},{65,384},{128,321},{129,320},{192,257},{1... | collective-permute-start | bytes 344072 | tf_op jit(solution)/shard_map/ppermute | solution.py:168
  21.0 10.8 %collective-permute-done = bf16[112,512]{1,0:T(8,128)(2,1)S(1)} collective-permute-done((bf16[112,512]{1,0:T(8,128)(2,1)}, bf16[112,512]{1,0:T(8,128)(2,1)S(1)}, u32[]{:S(2)}, u32[]{:S(2)}) %collective-permute-start) | collective-permute-done | bytes 114720 | tf_op jit(solution)/shard_map/ppermute | solution.py:168
  31.8 0.6 copy-done.7
  32.4 0.0 all-gather.5.cloned.1.call-update
  32.5 0.0 copy-start.3
  32.5 1.2 copy-done.3
  33.6 0.4 regroup.1
  34.0 19.5 %all_to_all.20.parts = bf16[8,112,512]{2,1,0:T(8,128)(2,1)S(1)} all-to-all(bf16[8,112,512]{2,1,0:T(8,128)(2,1)S(1)} %regroup.1), channel_id=1, replica_groups=mesh['z_lo'=8,'x'=4,'core'=2,'y'=4,'z_hi'=2] {'x','core'}, dimensions={0} | all-to-all | bytes 1835008 | tf_op jit(solution)/shard_map/all_to_all | solution.py:151
  53.5 0.2 first_sum.1
  53.7 17.7 %all_to_all.21.parts = f32[8,56,128]{2,1,0:T(8,128)S(1)} all-to-all(f32[8,56,128]{2,1,0:T(8,128)S(1)} %first_sum.1), channel_id=1, replica_groups=mesh['z_lo'=8,'x'=4,'core'=2,'y'=4,'z_hi'=2] {'z_lo'}, dimensions={0} | all-to-all | bytes 458752 | tf_op jit(solution)/shard_map/all_to_all | solution.py:153
  71.5 0.0 copy-done.4
  71.5 16.9 %all_to_all.22.parts = f32[32,8,128]{2,1,0:T(8,128)S(1)} all-to-all(f32[32,8,128]{2,1,0:T(8,128)S(1)} %get-tuple-element.7), channel_id=1, replica_groups=mesh['z_lo'=8,'x'=4,'core'=2,'y'=4,'z_hi'=2] {'y','x','core'}, dimensions={0} | all-to-all | bytes 262144 | tf_op jit(solution)/shard_map/all_to_all | solution.py:157
  88.5 0.7 spread_sum.1
  89.1 7.5 %all-to-all-start.3 = ((f32[16,8,128]{2,1,0:T(8,128)}), f32[16,8,128]{2,1,0:T(8,128)S(1)}, u32[]{:S(2)}, u32[]{:S(2)}) async-start(f32[16,8,128]{2,1,0:T(8,128)} %spread_sum.1), calls=%async_computation.3 | async-start | bytes 131072 | tf_op jit(solution)/shard_map/all_to_all | solution.py:159
  96.6 0.0 copy-done.6
  96.6 0.0 copy-start.5
  96.6 5.6 %norm.1.left.right = bf16[256,7168]{1,0:T(8,128)(2,1)S(1)} custom-call(bf16[256,7168]{1,0:T(8,128)(2,1)} %hidden.1, f32[1,7168]{1,0:T(1,128)S(1)} %bitcast.4), custom_call_target="tpu_custom_call" | custom-call | flops 9175040 | bytes 7340032 | tf_op jit(solution)/shard_map/norm/pallas_call | solution.py:93
  102.2 0.0 copy-start.1
  102.2 1.9 %copy-done.1 = bf16[256,7168]{1,0:T(8,128)(2,1)} copy-done((bf16[256,7168]{1,0:T(8,128)(2,1)}, bf16[256,7168]{1,0:T(8,128)(2,1)S(1)}, u32[]{:S(2)}) %copy-start.1) | copy-done | bytes 3670040
  104.1 4.6 %all-to-all-done.3.parts = f32[16,8,128]{2,1,0:T(8,128)S(1)} async-done(((f32[16,8,128]{2,1,0:T(8,128)}), f32[16,8,128]{2,1,0:T(8,128)S(1)}, u32[]{:S(2)}, u32[]{:S(2)}) %all-to-all-start.3) | async-done | bytes 65568 | tf_op jit(solution)/shard_map/all_to_all | solution.py:159
  108.7 0.7 update.1
  109.5 33.6 %all-gather.5.cloned.1.call-done.other = bf16[3584,512]{1,0:T(8,128)(2,1)} async-done(((bf16[112,512]{1,0:T(8,128)(2,1)}), bf16[3584,512]{1,0:T(8,128)(2,1)}) %all-gather.5.cloned.1.call-update) | async-done | bytes 3670032 | tf_op jit(solution)/shard_map/all_gather | solution.py:170
  143.1 2.0 %copy-done.2 = bf16[256,7168]{1,0:T(8,128)(2,1)S(1)} copy-done((bf16[256,7168]{1,0:T(8,128)(2,1)S(1)}, bf16[256,7168]{1,0:T(8,128)(2,1)}, u32[]{:S(2)}) %copy-start.2) | copy-done | bytes 3670040
  145.1 6.3 %project.1 = bf16[256,512]{1,0:T(8,128)(2,1)} custom-call(s32[1]{0:T(128)} %bitcast.half, bf16[256,7168]{1,0:T(8,128)(2,1)S(1)} %copy-done.2, bf16[256,7168]{1,0:T(8,128)(2,1)S(1)} %copy-done.2, bf16[3584,512]{1,0:T(8,128)(2,1)} %all-gather.3.cloned.1.call-done.own, bf16[3584,512]{1,0:T(8,128)(2,1)} %all-gather.5.cloned.1.call-done.other), custom_call_target="tpu_custom_call" | custom-call | flops 1879048192 | bytes 11010048 | tf_op jit(solution)/shard_map/project/pallas_call | solution.py:121
  (5 shorter events, 0.1 us)
Async XLA Ops:
  7.2 1.2 copy-start
  7.2 64.3 %copy-start.4 = (f32[14,512]{1,0:T(8,128)S(1)}, f32[14,512]{1,0:T(8,128)}, u32[]{:S(2)}) copy-start(f32[14,512]{1,0:T(8,128)} %outer.3) | copy-start | bytes 86020
  7.2 89.4 %copy-start.6 = (f32[7168]{0:T(1024)S(1)}, f32[7168]{0:T(1024)}, u32[]{:S(2)}) copy-start(f32[7168]{0:T(1024)} %param.7) | copy-start | bytes 86020
  7.2 102.3 %all-gather.3.cloned.1.call-start = ((), (), s32[]{:S(2)}) async-start(), calls=%async_computation.4 | async-start | bytes 3784704 | tf_op jit(solution)/shard_map/all_gather | solution.py:169
  9.0 134.1 %all-gather.5.cloned.1.call-start = ((), (), s32[]{:S(2)}) async-start(), calls=%async_computation.5 | async-start | bytes 3784704 | tf_op jit(solution)/shard_map/all_gather | solution.py:170
  9.1 22.7 %collective-permute-start = (bf16[112,512]{1,0:T(8,128)(2,1)}, bf16[112,512]{1,0:T(8,128)(2,1)S(1)}, u32[]{:S(2)}, u32[]{:S(2)}) collective-permute-start(bf16[112,512]{1,0:T(8,128)(2,1)} %constant_dynamic-slice_fusion), channel_id=1, source_target_pairs={{0,449},{1,448},{64,385},{65,384},{128,321},{129,320},{192,257},{1... | collective-permute-start | bytes 344072 | tf_op jit(solution)/shard_map/ppermute | solution.py:168
  31.8 0.6 copy-start.7
  32.5 1.2 copy-start.3
  89.1 19.6 %all-to-all-start.3 = ((f32[16,8,128]{2,1,0:T(8,128)}), f32[16,8,128]{2,1,0:T(8,128)S(1)}, u32[]{:S(2)}, u32[]{:S(2)}) async-start(f32[16,8,128]{2,1,0:T(8,128)} %spread_sum.1), calls=%async_computation.3 | async-start | bytes 131072 | tf_op jit(solution)/shard_map/all_to_all | solution.py:159
  96.6 12.1 %copy-start.5 = (f32[14,512]{1,0:T(8,128)S(1)}, f32[14,512]{1,0:T(8,128)}, u32[]{:S(2)}) copy-start(f32[14,512]{1,0:T(8,128)} %momentum.1) | copy-start | bytes 86020
  102.2 1.9 %copy-start.1 = (bf16[256,7168]{1,0:T(8,128)(2,1)}, bf16[256,7168]{1,0:T(8,128)(2,1)S(1)}, u32[]{:S(2)}) copy-start(bf16[256,7168]{1,0:T(8,128)(2,1)S(1)} %norm.1.left.right) | copy-start | bytes 11010052
  143.1 2.0 %copy-start.2 = (bf16[256,7168]{1,0:T(8,128)(2,1)S(1)}, bf16[256,7168]{1,0:T(8,128)(2,1)}, u32[]{:S(2)}) copy-start(bf16[256,7168]{1,0:T(8,128)(2,1)} %copy-done.1) | copy-start | bytes 11010052
Sparse Core Ops, SparseCore 0:
  11.7 67.9 all-gather.2
  82.8 60.2 all-gather.4

commit v2 on v1

v2 whole, which is shorter than its diff:
```python
import functools

import jax
import jax.numpy as jnp
from jax import lax
from jax.experimental import pallas as pl
from jax.experimental.pallas import tpu as pltpu
from jax.sharding import Mesh, PartitionSpec as P

D = 7168
KV = 512

OUTER_LR = 0.7
MOMENTUM_DECAY = 0.9
CLIP_RATIO = 0.25

NAMES = ("z_lo", "x", "core", "y", "z_hi")
SIZES = (8, 4, 2, 4, 2)
N_REPLICA = 64
SHARE = 14
ROWS = 896
PIECE = 112
LANES = 128
F32 = jnp.float32
BF16 = jnp.bfloat16
VMEM = pl.BlockSpec(memory_space=pltpu.VMEM)
PARAMS = pltpu.CompilerParams(vmem_limit_bytes=48 * 1024 * 1024)


LONG = pl.CostEstimate(flops=0, bytes_accessed=2**32, transcendentals=0)


def call(body, name, out, args, after=(), through=(), scratch=(), first=VMEM, cost=None):
    out = tuple(out) + tuple(jax.ShapeDtypeStruct(a.shape, a.dtype) for a in through)
    anywhere = pl.BlockSpec(memory_space=pl.ANY)
    given, kept = len(args) + len(after), len(out) - len(through)
    return pl.pallas_call(
        body,
        name=name,
        out_shape=out,
        in_specs=[first] + [VMEM] * (len(args) - 1) + [anywhere] * (len(after) + len(through)),
        out_specs=[VMEM] * kept + [anywhere] * len(through),
        scratch_shapes=list(scratch),
        input_output_aliases={given + i: kept + i for i in range(len(through))},
        compiler_params=PARAMS,
        cost_estimate=cost,
    )(*args, *after, *through)


def regroup_body(src, out, wide, grouped):
    wide[...] = src[...].astype(F32)
    for xc in range(8):
        for z in range(8):
            first = PIECE * z + SHARE * xc
            grouped[xc, SHARE * z : SHARE * (z + 1), :] = wide[first : first + SHARE, :]
        out[xc] = grouped[xc].astype(BF16)


def cut_body(place, weight, after, own, mine):
    rows, cols = mine.shape
    own[...] = weight[:, pl.ds(pl.multiple_of(place[0] * cols, cols), cols)]
    mine[...] = own[pl.ds(pl.multiple_of(place[1] * rows, rows), rows), :]


def first_sum_body(parts, *rest):
    out, total = rest[-2:]
    total[...] = functools.reduce(lambda a, b: a + b, [parts[i].astype(F32) for i in range(8)])
    for z in range(8):
        for j in range(4):
            out[z, SHARE * j : SHARE * (j + 1), :] = total[SHARE * z : SHARE * (z + 1), LANES * j : LANES * (j + 1)]


def lay_body(*refs):
    count = refs[-1].shape[0]
    for i in range(count):
        refs[-1][i] = refs[i][...]


def hold_body(given, after, out):
    out[...] = given[...]


def second_sum_body(parts, outer, *rest):
    delta, squares, total = rest[-3:]
    total[...] = functools.reduce(lambda a, b: a + b, [parts[i] for i in range(8)])
    for j in range(4):
        cols = slice(LANES * j, LANES * (j + 1))
        delta[:, cols] = outer[:, cols] - total[SHARE * j : SHARE * (j + 1), :] / N_REPLICA
    d = delta[...]
    line = jnp.sum(d * d, axis=0, keepdims=True)
    line = line[:, :128] + line[:, 128:256] + line[:, 256:384] + line[:, 384:]
    squares[...] = jnp.broadcast_to(line[None], squares.shape)


def spread_sum_body(parts, *rest):
    out = rest[-4]
    out[...] = jnp.broadcast_to(jnp.sum(parts[...], axis=0, keepdims=True), out.shape)


def update_body(parts, delta, outer, momentum, new_outer, new_momentum):
    lanes = jnp.sum(parts[...], axis=0)[:1]
    length = jnp.sqrt(jnp.sum(lanes, axis=1, keepdims=True))
    limit = CLIP_RATIO * jnp.sqrt(jnp.full((1, 1), D * KV, F32))
    factor = jnp.minimum(1.0, limit / (length + 1e-06))
    clipped = factor * delta[...]
    moved = MOMENTUM_DECAY * momentum[...] + clipped
    new_momentum[...] = moved
    new_outer[...] = outer[...] - OUTER_LR * (clipped + MOMENTUM_DECAY * moved)


def scale_body(hidden, after, out):
    squares = jnp.zeros((hidden.shape[0], LANES), F32)
    for first in range(0, D, LANES):
        values = hidden[:, first : first + LANES].astype(F32)
        squares += values * values
    scaled = lax.rsqrt(jnp.sum(squares, axis=1, keepdims=True) / D + 1e-05)
    out[...] = jnp.broadcast_to(scaled, out.shape)


def norm_body(hidden, gain, scaled, after, out):
    scale = scaled[...]
    for first in range(0, D, LANES):
        cols = slice(first, first + LANES)
        out[:, cols] = (hidden[:, cols].astype(F32) * scale * gain[:, cols]).astype(BF16)


def by_rows(body, name, width, dtype, hidden, args, after):
    rows, block = hidden.shape[0], 32
    return pl.pallas_call(
        body,
        name=name,
        grid=(rows // block,),
        out_shape=jax.ShapeDtypeStruct((rows, width), dtype),
        in_specs=[pl.BlockSpec((block, D), lambda i: (i, 0))]
        + [
            pl.BlockSpec((1, D), lambda i: (0, 0)) if a.shape[0] == 1 else pl.BlockSpec((block, a.shape[1]), lambda i: (i, 0))
            for a in args
        ]
        + [pl.BlockSpec(memory_space=pl.ANY)],
        out_specs=pl.BlockSpec((block, width), lambda i: (i, 0)),
        compiler_params=PARAMS,
        cost_estimate=LONG,
    )(hidden, *args, after)


DOT = functools.partial(jnp.dot, preferred_element_type=F32)


def project_body(order, near_own, far_own, near_other, far_other, early, late, first, second, third, fourth, near, far, weights, near_sum, far_sum):
    step = pl.program_id(0)

    @pl.when(step == 0)
    def _():
        near_sum[...] = jnp.zeros_like(near_sum)
        far_sum[...] = jnp.zeros_like(far_sum)

    rows = first.shape[1]
    for k, piece in enumerate((first, second, third, fourth)):
        weights[pl.ds(pl.multiple_of(order[8 + k] * rows, rows), rows), :] = piece[0] if k < 2 else piece[0, 0]

    def add(own):
        near_sum[...] += DOT(near_own[...], own) + DOT(near_other[...], weights[...])
        far_sum[...] += DOT(far_own[...], own) + DOT(far_other[...], weights[...])

    pl.when(step < 2)(lambda: add(early[0]))
    pl.when(step >= 2)(lambda: add(late[0]))

    @pl.when(step == pl.num_programs(0) - 1)
    def _():
        near[...] = near_sum[...].astype(BF16)
        far[...] = far_sum[...].astype(BF16)


def project(order, normed, far_normed, early, late, quad, quad_next, quad_late):
    rows, cols = normed.shape[0], early.shape[2]
    out = jax.ShapeDtypeStruct((rows, cols), BF16)
    own = pl.BlockSpec((rows, ROWS), lambda j, o: (0, o[j]))
    other = pl.BlockSpec((rows, ROWS), lambda j, o: (0, o[4 + j]))
    whole = pl.BlockSpec((rows, cols), lambda j, o: (0, 0))
    piece = pl.BlockSpec((1, ROWS // 4, cols), lambda j, o: (j, 0, 0))
    return pl.pallas_call(
        project_body,
        name="project",
        out_shape=(out, out),
        grid_spec=pltpu.PrefetchScalarGridSpec(
            num_scalar_prefetch=1,
            grid=(4,),
            in_specs=[
                own, own, other, other,
                pl.BlockSpec((1, ROWS, cols), lambda j, o: (jnp.minimum(j, 1), 0, 0)),
                pl.BlockSpec((1, ROWS, cols), lambda j, o: (jnp.maximum(j - 2, 0), 0, 0)),
                piece, piece,
                pl.BlockSpec((1, 1, ROWS // 4, cols), lambda j, o: (0, j, 0, 0)),
                pl.BlockSpec((1, 1, ROWS // 4, cols), lambda j, o: (1, j, 0, 0)),
            ],
            out_specs=(whole, whole),
            scratch_shapes=[pltpu.VMEM((ROWS, cols), BF16)] + [pltpu.VMEM((rows, cols), F32)] * 2,
        ),
        compiler_params=PARAMS,
        cost_estimate=pl.CostEstimate(
            flops=4 * rows * D * cols, bytes_accessed=2 * (D * cols + 2 * rows * D), transcendentals=0
        ),
    )(order, normed, far_normed, normed, far_normed, early, late, quad, quad_next, quad_late, quad_late)


def join_body(core, near, far, out):
    cols = near.shape[1]

    @pl.when(core[0] == 0)
    def _():
        out[:, :cols] = near[...]
        out[:, cols:] = far[...]

    @pl.when(core[0] == 1)
    def _():
        out[:, :cols] = far[...]
        out[:, cols:] = near[...]


def join(core, near, far):
    rows, cols = near.shape
    return pl.pallas_call(
        join_body,
        name="join",
        out_shape=jax.ShapeDtypeStruct((rows, 2 * cols), BF16),
        in_specs=[pl.BlockSpec(memory_space=pltpu.SMEM), VMEM, VMEM],
        out_specs=VMEM,
        compiler_params=PARAMS,
    )(core, near, far)


def exchange(array, axis, second):
    flips = (3, 1) if second else (1, 3)
    names = tuple(name for name in NAMES if name in (axis, "core"))
    number = lambda i, c: 2 * i + c if names[1] == "core" else 4 * c + i
    pairs = [(number(i, c), number(i ^ flips[c], c)) for i in range(4) for c in range(2)]
    return lax.ppermute(array, names, pairs)


SHIFTS = (1, 3, 2)


def spread(array, axis):
    return [lax.ppermute(array, axis, [(i, (i + s) % 4) for i in range(4)]) for s in SHIFTS]


def order_of(place, core):
    near = place ^ (1 + 2 * core)
    return [place, near, near ^ 2, place ^ 2]


def on_device(hidden_in, norm_gain, proj_weight, replica_params, outer_params, momentum):
    share, rows, cols = outer_params.shape, proj_weight.shape[0], KV // 2
    array = lambda dtype, *dims: jax.ShapeDtypeStruct(dims, dtype)
    x, y, core, half = [lax.axis_index(name).astype(jnp.int32) for name in ("x", "y", "core", "z_hi")]
    swap = [(0, 1), (1, 0)]

    (grouped,) = call(
        regroup_body, "regroup", (array(BF16, 8, PIECE, KV),), (replica_params[0],),
        scratch=[pltpu.VMEM((ROWS, KV), F32), pltpu.VMEM((8, PIECE, KV), F32)],
    )
    own, mine = call(
        cut_body, "cut", (array(BF16, rows, cols), array(BF16, rows // 4, cols)),
        (jnp.stack([core, x]), proj_weight), (grouped,), first=pl.BlockSpec(memory_space=pltpu.SMEM),
    )
    grouped = lax.all_to_all(grouped, ("x", "core"), 0, 0)
    mirror = [(2 * z + h, 2 * (7 - z) + 1 - h) for z in range(8) for h in range(2)]
    other = lax.ppermute(mine, ("z_lo", "z_hi"), mirror)
    own_next = exchange(own, "y", False)
    (pieces,) = call(
        first_sum_body, "first_sum", (array(F32, 8, 56, LANES),), (grouped,), (own_next, other), scratch=[pltpu.VMEM((PIECE, KV), F32)]
    )
    pieces_in = lax.all_to_all(pieces, "z_lo", 0, 0)
    scaled = by_rows(scale_body, "scale", LANES, F32, hidden_in, (), pieces)
    (other,) = call(hold_body, "hold", (array(BF16, *other.shape),), (other,), (pieces,), cost=LONG)
    others = [other] + spread(other, "y")
    (early,) = call(lay_body, "pair", (array(BF16, 2, rows, cols),), (own, own_next), (pieces,), cost=LONG)
    late = exchange(early, "y", True)
    delta, squares = call(
        second_sum_body, "second_sum", (array(F32, *share), array(F32, 32, 8, LANES)),
        (pieces_in, outer_params), (*others[1:], late, scaled), (), [pltpu.VMEM((56, LANES), F32)],
    )
    squares = lax.all_to_all(squares, ("y", "x", "core"), 0, 0)
    (other,) = call(lay_body, "lay", (array(BF16, 4, rows // 4, cols),), tuple(others), (delta,), cost=LONG)
    other_next = exchange(other, "x", False)
    normed = by_rows(norm_body, "norm", D, BF16, hidden_in, (norm_gain.reshape(1, -1), scaled), delta)
    squares, normed, other, other_next = call(
        spread_sum_body, "spread_sum", (array(F32, 16, 8, LANES),), (squares,), (), (normed, other, other_next)
    )
    far_normed = lax.ppermute(normed, "core", swap)
    other_late = exchange(jnp.stack([other, other_next]), "x", True)
    squares = lax.all_to_all(squares, ("z_lo", "z_hi"), 0, 0)
    ys, other_ys, xs = order_of(y, core), [(y - s) % 4 for s in (0,) + SHIFTS], order_of(x, core)
    order = jnp.stack([2 * k + half for k in ys] + [2 * k + 1 - half for k in other_ys] + xs)
    near, far = project(order, normed, far_normed, early, late, other, other_next, other_late)
    far = lax.ppermute(far, "core", swap)
    new_outer, new_momentum = call(
        update_body, "update", (array(F32, *share), array(F32, *share)), (squares, delta, outer_params, momentum)
    )
    projected = join(core.reshape(1), near, far)
    return (projected, new_outer, new_momentum)


def solution(mesh):
    inner = Mesh(mesh.devices.reshape(SIZES), NAMES)
    replica, fsdp = NAMES[:3], NAMES[3:]
    in_specs = (
        P(replica + fsdp, None),
        P(),
        P(fsdp, None),
        P(replica, fsdp, None),
        P(fsdp + replica, None),
        P(fsdp + replica, None),
    )
    out_specs = (
        P(replica + fsdp, None),
        P(fsdp + replica, None),
        P(fsdp + replica, None),
    )
    return jax.shard_map(
        on_device, mesh=inner, in_specs=in_specs, out_specs=out_specs, check_vma=False
    )
```

time: 159 us -> 110 us (0.69)
  blocking collectives: 54.2 us -> 0 us
  starting transfers between devices: 19.5 us -> 67.7 us
  waiting for transfers between devices: 49 us -> 15 us
  between operations: 14.1 us -> 0.92 us
  Pallas kernels: 13.8 us -> 20.2 us
  local copies, waits for them, and re-layouts: 7.53 us -> 3.31 us
    all_to_all x3 -> x0, blocking collectives: 54.2 us -> none  [the longest x1 19.5 us: on_device(): grouped = lax.all_to_all(grouped, ('x', 'core'), 0, 0)]
    all_gather x2 -> x0, waiting for transfers between devices: 33.6 us -> none  [the longest x1 33.6 us: on_device(): other = lax.all_gather(theirs, ('y', 'x', 'core'), axis=0, tiled=True)]
    ppermute x1 -> x10, starting transfers between devices: 12 us -> 36.3 us  [the longest x4 11.2 us: exchange(): return lax.ppermute(array, names, pairs)]
    all_to_all x0 -> x3, starting transfers between devices: none -> 21.7 us  [the longest x1 10.3 us: on_device(): grouped = lax.all_to_all(grouped, ('x', 'core'), 0, 0)]
    pallas_call x7 -> x13, Pallas kernels: 13.8 us -> 20.2 us  [the longest x2 8.28 us: by_rows(): pl.pallas_call(body, name=name, grid=(rows // block,), out_shape=jax.Shap...]
    all_to_all x1, waiting for transfers between devices: 4.64 us -> 0.01 us  [on_device(): squares = lax.all_to_all(squares, ('z_lo', 'z_hi'), 0, 0)]
    unnamed x16 -> x12, local copies, waits for them, and re-layouts: 6.88 us -> 3.22 us
    ppermute x1 -> x10, waiting for transfers between devices: 10.8 us -> 14 us  [the longest x1 9.8 us: on_device(): other = lax.ppermute(mine, ('z_lo', 'z_hi'), mirror)]
  transfers between devices with their start and end apart: 4 -> 14, of which waited for: 3 -> 5; matrix products, arithmetic and copies ran while one was open for 0% -> 1% of each run, Pallas kernels for 5% -> 15%
where the time goes in v2:
time: 110 us; the launch traced here: 108 us
  starting transfers between devices  67.7 us (62%)
  Pallas kernels  20.2 us (18%)
  waiting for transfers between devices  15 us (14%)
  local copies, waits for them, and re-layouts  3.31 us (3%)
  other arithmetic  1.18 us (1%)
    ppermute x4, starting transfers between devices, exchange(): return lax.ppermute(array, names, pairs)  11.2 us
    all_to_all x1, starting transfers between devices, on_device(): grouped = lax.all_to_all(grouped, ('x', 'core'), 0, 0)  10.3 us
    ppermute x1, waiting for transfers between devices, on_device(): other = lax.ppermute(mine, ('z_lo', 'z_hi'), mirror)  9.8 us
    all_to_all x1, starting transfers between devices, on_device(): squares = lax.all_to_all(squares, ('z_lo', 'z_hi'), 0, 0)  9.66 us
    ppermute x3, starting transfers between devices, spread(): lax.ppermute(array, axis, [(i, (i + s) % 4) for i in range(4)])  9.43 us
    ppermute x1, starting transfers between devices, on_device(): other = lax.ppermute(mine, ('z_lo', 'z_hi'), mirror)  9.31 us
    pallas_call x2, Pallas kernels, by_rows(): pl.pallas_call(body, name=name, grid=(rows // block,), out_shape=jax.Shap...  8.28 us
    pallas_call x1, Pallas kernels, project(): pl.pallas_call(project_body, name='project', out_shape=(out, out), grid_s...  6.18 us
  transfers between devices with their start and end apart: 14, of which 5 were waited for; matrix products, arithmetic and copies ran while one was open for 1% of the time, Pallas kernels for 15%

profile of v2, /device:TPU:1, one launch (start us, length us, event | category | flops | bytes accessed | tf_op | source)
XLA Modules:
  0.0 108.2 jit_solution(9953491507677755206)
XLA Ops:
  0.6 1.2 %copy-done.1 = bf16[1,896,512]{2,1,0:T(8,128)(2,1)S(1)} copy-done((bf16[1,896,512]{2,1,0:T(8,128)(2,1)S(1)}, bf16[1,896,512]{2,1,0:T(8,128)(2,1)}, u32[]{:S(2)}) %copy-start.1) | copy-done | bytes 917528
  1.8 1.3 %regroup.1.after = bf16[8,112,512]{2,1,0:T(8,128)(2,1)} custom-call(bf16[896,512]{1,0:T(8,128)(2,1)S(1)} %bitcast.19), custom_call_target="tpu_custom_call" | custom-call | tf_op jit(solution)/shard_map/regroup/pallas_call | solution.py:37
  3.1 10.3 %all-to-all-start = ((bf16[8,112,512]{2,1,0:T(8,128)(2,1)}), bf16[8,112,512]{2,1,0:T(8,128)(2,1)S(1)}, u32[]{:S(2)}, u32[]{:S(2)}) async-start(bf16[8,112,512]{2,1,0:T(8,128)(2,1)} %regroup.1.after), calls=%async_computation | async-start | bytes 1835008 | tf_op jit(solution)/shard_map/all_to_all | solution.py:266
  13.5 0.6 cut.1
  14.1 1.9 %collective-permute-start = (bf16[896,256]{1,0:T(8,128)(2,1)S(1)}, bf16[896,256]{1,0:T(8,128)(2,1)S(1)}, u32[]{:S(2)}, u32[]{:S(2)}) collective-permute-start(bf16[896,256]{1,0:T(8,128)(2,1)S(1)} %get-tuple-element.15.refs_0_), channel_id=1, source_target_pairs={{0,2},{8,14},{2,0},{10,12},{4,6},{12,10},{6,4},{14,8},{1,3},{9,15}... | collective-permute-start | bytes 1376264 | tf_op jit(solution)/shard_map/ppermute | solution.py:237
  16.1 9.3 %collective-permute-start.1 = (bf16[224,256]{1,0:T(8,128)(2,1)S(1)}, bf16[224,256]{1,0:T(8,128)(2,1)S(1)}, u32[]{:S(2)}, u32[]{:S(2)}) collective-permute-start(bf16[224,256]{1,0:T(8,128)(2,1)S(1)} %get-tuple-element.16), channel_id=1, source_target_pairs={{0,449},{1,448},{64,385},{65,384},{128,321},{129,320},{192,257},{1... | collective-permute-start | bytes 344072 | tf_op jit(solution)/shard_map/ppermute | solution.py:268
  25.4 9.8 %collective-permute-done.1.rest_1_.given = bf16[224,256]{1,0:T(8,128)(2,1)S(1)} collective-permute-done((bf16[224,256]{1,0:T(8,128)(2,1)S(1)}, bf16[224,256]{1,0:T(8,128)(2,1)S(1)}, u32[]{:S(2)}, u32[]{:S(2)}) %collective-permute-start.1) | collective-permute-done | bytes 114720 | tf_op jit(solution)/shard_map/ppermute | solution.py:268
  35.2 0.9 first_sum.1.after.refs_2_
  36.1 2.1 %collective-permute-start.5 = (bf16[2,896,256]{2,1,0:T(8,128)(2,1)S(1)}, bf16[2,896,256]{2,1,0:T(8,128)(2,1)S(1)}, u32[]{:S(2)}, u32[]{:S(2)}) collective-permute-start(bf16[2,896,256]{2,1,0:T(8,128)(2,1)S(1)} %pair.1.early), channel_id=1, source_target_pairs={{0,6},{8,10},{2,4},{10,8},{4,2},{12,14},{6,0},{14,12},{1,7},{9,11}... | collective-permute-start | bytes 2752520 | tf_op jit(solution)/shard_map/ppermute | solution.py:237
  38.2 6.0 %all-to-all-start.1 = ((f32[8,56,128]{2,1,0:T(8,128)}), f32[8,56,128]{2,1,0:T(8,128)S(1)}, u32[]{:S(2)}, u32[]{:S(2)}) async-start(f32[8,56,128]{2,1,0:T(8,128)} %first_sum.1.after.refs_2_), calls=%async_computation.1 | async-start | bytes 458752 | tf_op jit(solution)/shard_map/all_to_all | solution.py:273
  44.2 3.6 %collective-permute-start.4 = (bf16[224,256]{1,0:T(8,128)(2,1)S(1)}, bf16[224,256]{1,0:T(8,128)(2,1)S(1)}, u32[]{:S(2)}, u32[]{:S(2)}) collective-permute-start(bf16[224,256]{1,0:T(8,128)(2,1)S(1)} %hold.1.refs_0_), channel_id=1, source_target_pairs={{0,4},{2,6},{4,0},{6,2},{1,5},{3,7},{5,1},{7,3},{8,12},{10,14},{12... | collective-permute-start | bytes 344072 | tf_op jit(solution)/shard_map/ppermute | solution.py:244
  47.8 4.0 %collective-permute-start.3 = (bf16[224,256]{1,0:T(8,128)(2,1)S(1)}, bf16[224,256]{1,0:T(8,128)(2,1)S(1)}, u32[]{:S(2)}, u32[]{:S(2)}) collective-permute-start(bf16[224,256]{1,0:T(8,128)(2,1)S(1)} %hold.1.refs_0_), channel_id=1, source_target_pairs={{0,6},{2,0},{4,2},{6,4},{1,7},{3,1},{5,3},{7,5},{8,14},{10,8},{12,... | collective-permute-start | bytes 344072 | tf_op jit(solution)/shard_map/ppermute | solution.py:244
  51.8 1.9 %collective-permute-start.2 = (bf16[224,256]{1,0:T(8,128)(2,1)S(1)}, bf16[224,256]{1,0:T(8,128)(2,1)S(1)}, u32[]{:S(2)}, u32[]{:S(2)}) collective-permute-start(bf16[224,256]{1,0:T(8,128)(2,1)S(1)} %hold.1.refs_0_), channel_id=1, source_target_pairs={{0,2},{2,4},{4,6},{6,0},{1,3},{3,5},{5,7},{7,1},{8,10},{10,12},{12... | collective-permute-start | bytes 344072 | tf_op jit(solution)/shard_map/ppermute | solution.py:244
  53.7 2.0 %copy-done = bf16[256,7168]{1,0:T(8,128)(2,1)S(1)} copy-done((bf16[256,7168]{1,0:T(8,128)(2,1)S(1)}, bf16[256,7168]{1,0:T(8,128)(2,1)}, u32[]{:S(2)}) %copy-start) | copy-done | bytes 3670040
  55.7 1.6 %scale.1.rest_4_.scaled = f32[256,128]{1,0:T(8,128)S(1)} custom-call(bf16[256,7168]{1,0:T(8,128)(2,1)S(1)} %copy-done, f32[8,56,128]{2,1,0:T(8,128)} %first_sum.1.after.refs_2_), custom_call_target="tpu_custom_call" | custom-call | bytes 4294967296 | tf_op jit(solution)/shard_map/scale/pallas_call | solution.py:129
  57.3 1.5 %collective-permute-done.2.rest_0_.refs_1_ = bf16[224,256]{1,0:T(8,128)(2,1)S(1)} collective-permute-done((bf16[224,256]{1,0:T(8,128)(2,1)S(1)}, bf16[224,256]{1,0:T(8,128)(2,1)S(1)}, u32[]{:S(2)}, u32[]{:S(2)}) %collective-permute-start.2) | collective-permute-done | bytes 114720 | tf_op jit(solution)/shard_map/ppermute | solution.py:244
  58.8 0.7 second_sum.1
  59.6 4.9 %collective-permute-start.6 = (bf16[4,224,256]{2,1,0:T(8,128)(2,1)S(1)}, bf16[4,224,256]{2,1,0:T(8,128)(2,1)S(1)}, u32[]{:S(2)}, u32[]{:S(2)}) collective-permute-start(bf16[4,224,256]{2,1,0:T(8,128)(2,1)S(1)} %lay.1.rest_1_), channel_id=1, source_target_pairs={{0,16},{8,56},{16,0},{24,40},{32,48},{40,24},{48,32},{56,8},{1,17}... | collective-permute-start | bytes 1376264 | tf_op jit(solution)/shard_map/ppermute | solution.py:237
  64.4 5.4 %all-to-all-start.2 = ((f32[32,8,128]{2,1,0:T(8,128)}), f32[32,8,128]{2,1,0:T(8,128)S(1)}, u32[]{:S(2)}, u32[]{:S(2)}) async-start(f32[32,8,128]{2,1,0:T(8,128)} %get-tuple-element.17), calls=%async_computation.2 | async-start | bytes 262144 | tf_op jit(solution)/shard_map/all_to_all | solution.py:283
  69.8 6.7 %norm.1.rest_0_ = bf16[256,7168]{1,0:T(8,128)(2,1)} custom-call(bf16[256,7168]{1,0:T(8,128)(2,1)} %hidden.3, f32[1,7168]{1,0:T(1,128)S(1)} %bitcast.20, f32[256,128]{1,0:T(8,128)S(1)} %scale.1.rest_4_.scaled, f32[14,512]{1,0:T(8,128)S(1)} %get-tuple-element.18.after.refs_4_.delta), custom_call_target="tpu_custom_call" | custom-call | bytes 4294967296 | tf_op jit(solution)/shard_map/norm/pallas_call | solution.py:129
  76.5 0.9 all-to-all-done.2.parts
  77.4 0.7 spread_sum.1
  78.1 2.3 %collective-permute-start.7 = (bf16[256,7168]{1,0:T(8,128)(2,1)}, bf16[256,7168]{1,0:T(8,128)(2,1)}, u32[]{:S(2)}, u32[]{:S(2)}) collective-permute-start(bf16[256,7168]{1,0:T(8,128)(2,1)} %get-tuple-element.19.near_own.near_other), channel_id=1, source_target_pairs={{0,8},{8,0},{1,9},{9,1},{2,10},{10,2},{3,11},{11,3},{4,12},{12,4},... | collective-permute-start | bytes 11010056 | tf_op jit(solution)/shard_map/ppermute | solution.py:290
  80.4 1.1 %pad_maximum_fusion = bf16[2,4,224,256]{3,2,1,0:T(8,128)(2,1)} fusion(bf16[1,4,224,256]{3,2,1,0:T(8,128)(2,1)S(1)} %bitcast.18, bf16[1,4,224,256]{3,2,1,0:T(8,128)(2,1)S(1)} %bitcast.17), kind=kLoop, calls=%fused_computation | loop fusion | flops 458752 | bytes 1835008 | tf_op jit(solution)/shard_map/stack | solution.py:291
  81.5 2.3 %collective-permute-start.8 = (bf16[2,4,224,256]{3,2,1,0:T(8,128)(2,1)}, bf16[2,4,224,256]{3,2,1,0:T(8,128)(2,1)}, u32[]{:S(2)}, u32[]{:S(2)}) collective-permute-start(bf16[2,4,224,256]{3,2,1,0:T(8,128)(2,1)} %pad_maximum_fusion), channel_id=1, source_target_pairs={{0,48},{8,24},{16,32},{24,8},{32,16},{40,56},{48,0},{56,40},{1,49}... | collective-permute-start | bytes 2752520 | tf_op jit(solution)/shard_map/ppermute | solution.py:237
  84.0 9.7 %all-to-all-start.3 = ((f32[16,8,128]{2,1,0:T(8,128)}), f32[16,8,128]{2,1,0:T(8,128)S(1)}, u32[]{:S(2)}, u32[]{:S(2)}) async-start(f32[16,8,128]{2,1,0:T(8,128)} %get-tuple-element.24), calls=%async_computation.3 | async-start | bytes 131072 | tf_op jit(solution)/shard_map/all_to_all | solution.py:292
  93.7 2.6 %collective-permute-done.8.third.fourth = bf16[2,4,224,256]{3,2,1,0:T(8,128)(2,1)} collective-permute-done((bf16[2,4,224,256]{3,2,1,0:T(8,128)(2,1)}, bf16[2,4,224,256]{3,2,1,0:T(8,128)(2,1)}, u32[]{:S(2)}, u32[]{:S(2)}) %collective-permute-start.8) | collective-permute-done | bytes 917536 | tf_op jit(solution)/shard_map/ppermute | solution.py:237
  96.3 6.2 %project.1 = (bf16[256,256]{1,0:T(8,128)(2,1)S(1)}, bf16[256,256]{1,0:T(8,128)(2,1)S(1)}) custom-call(s32[12]{0:T(128)S(1)} %stack.65.order, bf16[256,7168]{1,0:T(8,128)(2,1)} %get-tuple-element.19.near_own.near_other, bf16[256,7168]{1,0:T(8,128)(2,1)} %collective-permute-done.7.far_own.far_other, bf16[256,7168]{1,0:T(8,128)(2,1)} %get-tuple-element.19.near_own.near_other, ...), custom_call_target="tpu_custom_call" | custom-call | flops 1879048192 | bytes 11010048 | tf_op jit(solution)/shard_map/project/pallas_call | solution.py:181
  102.5 4.1 %collective-permute-start.9 = (bf16[256,256]{1,0:T(8,128)(2,1)S(1)}, bf16[256,256]{1,0:T(8,128)(2,1)S(1)}, u32[]{:S(2)}, u32[]{:S(2)}) collective-permute-start(bf16[256,256]{1,0:T(8,128)(2,1)S(1)} %get-tuple-element.23), channel_id=1, source_target_pairs={{0,8},{8,0},{1,9},{9,1},{2,10},{10,2},{3,11},{11,3},{4,12},{12,4},... | collective-permute-start | bytes 393224 | tf_op jit(solution)/shard_map/ppermute | solution.py:296
  106.6 0.7 update.1
  107.3 0.2 collective-permute-done.9.far
  107.5 0.7 join.1
  (24 shorter events, 0.3 us)
Async XLA Ops:
  0.6 1.2 %copy-start.1 = (bf16[1,896,512]{2,1,0:T(8,128)(2,1)S(1)}, bf16[1,896,512]{2,1,0:T(8,128)(2,1)}, u32[]{:S(2)}) copy-start(bf16[1,896,512]{2,1,0:T(8,128)(2,1)} %param.9) | copy-start | bytes 2752516
  1.8 11.7 %copy-start.2 = (bf16[896,512]{1,0:T(8,128)(2,1)S(1)}, bf16[896,512]{1,0:T(8,128)(2,1)}, u32[]{:S(2)}) copy-start(bf16[896,512]{1,0:T(8,128)(2,1)} %weight.1) | copy-start | bytes 2752516
  3.1 32.1 %all-to-all-start = ((bf16[8,112,512]{2,1,0:T(8,128)(2,1)}), bf16[8,112,512]{2,1,0:T(8,128)(2,1)S(1)}, u32[]{:S(2)}, u32[]{:S(2)}) async-start(bf16[8,112,512]{2,1,0:T(8,128)(2,1)} %regroup.1.after), calls=%async_computation | async-start | bytes 1835008 | tf_op jit(solution)/shard_map/all_to_all | solution.py:266
  14.1 21.0 %collective-permute-start = (bf16[896,256]{1,0:T(8,128)(2,1)S(1)}, bf16[896,256]{1,0:T(8,128)(2,1)S(1)}, u32[]{:S(2)}, u32[]{:S(2)}) collective-permute-start(bf16[896,256]{1,0:T(8,128)(2,1)S(1)} %get-tuple-element.15.refs_0_), channel_id=1, source_target_pairs={{0,2},{8,14},{2,0},{10,12},{4,6},{12,10},{6,4},{14,8},{1,3},{9,15}... | collective-permute-start | bytes 1376264 | tf_op jit(solution)/shard_map/ppermute | solution.py:237
  16.1 19.1 %collective-permute-start.1 = (bf16[224,256]{1,0:T(8,128)(2,1)S(1)}, bf16[224,256]{1,0:T(8,128)(2,1)S(1)}, u32[]{:S(2)}, u32[]{:S(2)}) collective-permute-start(bf16[224,256]{1,0:T(8,128)(2,1)S(1)} %get-tuple-element.16), channel_id=1, source_target_pairs={{0,449},{1,448},{64,385},{65,384},{128,321},{129,320},{192,257},{1... | collective-permute-start | bytes 344072 | tf_op jit(solution)/shard_map/ppermute | solution.py:268
  36.1 22.7 %copy-start.3 = (f32[14,512]{1,0:T(8,128)S(1)}, f32[14,512]{1,0:T(8,128)}, u32[]{:S(2)}) copy-start(f32[14,512]{1,0:T(8,128)} %outer.3) | copy-start | bytes 86020
  36.1 22.7 %collective-permute-start.5 = (bf16[2,896,256]{2,1,0:T(8,128)(2,1)S(1)}, bf16[2,896,256]{2,1,0:T(8,128)(2,1)S(1)}, u32[]{:S(2)}, u32[]{:S(2)}) collective-permute-start(bf16[2,896,256]{2,1,0:T(8,128)(2,1)S(1)} %pair.1.early), channel_id=1, source_target_pairs={{0,6},{8,10},{2,4},{10,8},{4,2},{12,14},{6,0},{14,12},{1,7},{9,11}... | collective-permute-start | bytes 2752520 | tf_op jit(solution)/shard_map/ppermute | solution.py:237
  38.2 20.6 %all-to-all-start.1 = ((f32[8,56,128]{2,1,0:T(8,128)}), f32[8,56,128]{2,1,0:T(8,128)S(1)}, u32[]{:S(2)}, u32[]{:S(2)}) async-start(f32[8,56,128]{2,1,0:T(8,128)} %first_sum.1.after.refs_2_), calls=%async_computation.1 | async-start | bytes 458752 | tf_op jit(solution)/shard_map/all_to_all | solution.py:273
  44.2 25.6 %copy-start.5 = (f32[7168]{0:T(1024)S(1)}, f32[7168]{0:T(1024)}, u32[]{:S(2)}) copy-start(f32[7168]{0:T(1024)} %param.7) | copy-start | bytes 86020
  44.2 13.1 %collective-permute-start.4 = (bf16[224,256]{1,0:T(8,128)(2,1)S(1)}, bf16[224,256]{1,0:T(8,128)(2,1)S(1)}, u32[]{:S(2)}, u32[]{:S(2)}) collective-permute-start(bf16[224,256]{1,0:T(8,128)(2,1)S(1)} %hold.1.refs_0_), channel_id=1, source_target_pairs={{0,4},{2,6},{4,0},{6,2},{1,5},{3,7},{5,1},{7,3},{8,12},{10,14},{12... | collective-permute-start | bytes 344072 | tf_op jit(solution)/shard_map/ppermute | solution.py:244
  47.8 9.5 %collective-permute-start.3 = (bf16[224,256]{1,0:T(8,128)(2,1)S(1)}, bf16[224,256]{1,0:T(8,128)(2,1)S(1)}, u32[]{:S(2)}, u32[]{:S(2)}) collective-permute-start(bf16[224,256]{1,0:T(8,128)(2,1)S(1)} %hold.1.refs_0_), channel_id=1, source_target_pairs={{0,6},{2,0},{4,2},{6,4},{1,7},{3,1},{5,3},{7,5},{8,14},{10,8},{12,... | collective-permute-start | bytes 344072 | tf_op jit(solution)/shard_map/ppermute | solution.py:244
  51.8 7.0 %collective-permute-start.2 = (bf16[224,256]{1,0:T(8,128)(2,1)S(1)}, bf16[224,256]{1,0:T(8,128)(2,1)S(1)}, u32[]{:S(2)}, u32[]{:S(2)}) collective-permute-start(bf16[224,256]{1,0:T(8,128)(2,1)S(1)} %hold.1.refs_0_), channel_id=1, source_target_pairs={{0,2},{2,4},{4,6},{6,0},{1,3},{3,5},{5,7},{7,1},{8,10},{10,12},{12... | collective-permute-start | bytes 344072 | tf_op jit(solution)/shard_map/ppermute | solution.py:244
  53.7 2.0 %copy-start = (bf16[256,7168]{1,0:T(8,128)(2,1)S(1)}, bf16[256,7168]{1,0:T(8,128)(2,1)}, u32[]{:S(2)}) copy-start(bf16[256,7168]{1,0:T(8,128)(2,1)} %hidden.3) | copy-start | bytes 11010052
  59.6 17.9 %collective-permute-start.6 = (bf16[4,224,256]{2,1,0:T(8,128)(2,1)S(1)}, bf16[4,224,256]{2,1,0:T(8,128)(2,1)S(1)}, u32[]{:S(2)}, u32[]{:S(2)}) collective-permute-start(bf16[4,224,256]{2,1,0:T(8,128)(2,1)S(1)} %lay.1.rest_1_), channel_id=1, source_target_pairs={{0,16},{8,56},{16,0},{24,40},{32,48},{40,24},{48,32},{56,8},{1,17}... | collective-permute-start | bytes 1376264 | tf_op jit(solution)/shard_map/ppermute | solution.py:237
  64.4 13.0 %all-to-all-start.2 = ((f32[32,8,128]{2,1,0:T(8,128)}), f32[32,8,128]{2,1,0:T(8,128)S(1)}, u32[]{:S(2)}, u32[]{:S(2)}) async-start(f32[32,8,128]{2,1,0:T(8,128)} %get-tuple-element.17), calls=%async_computation.2 | async-start | bytes 262144 | tf_op jit(solution)/shard_map/all_to_all | solution.py:283
  78.1 18.2 %collective-permute-start.7 = (bf16[256,7168]{1,0:T(8,128)(2,1)}, bf16[256,7168]{1,0:T(8,128)(2,1)}, u32[]{:S(2)}, u32[]{:S(2)}) collective-permute-start(bf16[256,7168]{1,0:T(8,128)(2,1)} %get-tuple-element.19.near_own.near_other), channel_id=1, source_target_pairs={{0,8},{8,0},{1,9},{9,1},{2,10},{10,2},{3,11},{11,3},{4,12},{12,4},... | collective-permute-start | bytes 11010056 | tf_op jit(solution)/shard_map/ppermute | solution.py:290
  81.5 14.7 %collective-permute-start.8 = (bf16[2,4,224,256]{3,2,1,0:T(8,128)(2,1)}, bf16[2,4,224,256]{3,2,1,0:T(8,128)(2,1)}, u32[]{:S(2)}, u32[]{:S(2)}) collective-permute-start(bf16[2,4,224,256]{3,2,1,0:T(8,128)(2,1)} %pad_maximum_fusion), channel_id=1, source_target_pairs={{0,48},{8,24},{16,32},{24,8},{32,16},{40,56},{48,0},{56,40},{1,49}... | collective-permute-start | bytes 2752520 | tf_op jit(solution)/shard_map/ppermute | solution.py:237
  84.0 22.5 %all-to-all-start.3 = ((f32[16,8,128]{2,1,0:T(8,128)}), f32[16,8,128]{2,1,0:T(8,128)S(1)}, u32[]{:S(2)}, u32[]{:S(2)}) async-start(f32[16,8,128]{2,1,0:T(8,128)} %get-tuple-element.24), calls=%async_computation.3 | async-start | bytes 131072 | tf_op jit(solution)/shard_map/all_to_all | solution.py:292
  93.7 12.9 %copy-start.4 = (f32[14,512]{1,0:T(8,128)S(1)}, f32[14,512]{1,0:T(8,128)}, u32[]{:S(2)}) copy-start(f32[14,512]{1,0:T(8,128)} %momentum.1) | copy-start | bytes 86020
  102.5 5.0 %collective-permute-start.9 = (bf16[256,256]{1,0:T(8,128)(2,1)S(1)}, bf16[256,256]{1,0:T(8,128)(2,1)S(1)}, u32[]{:S(2)}, u32[]{:S(2)}) collective-permute-start(bf16[256,256]{1,0:T(8,128)(2,1)S(1)} %get-tuple-element.23), channel_id=1, source_target_pairs={{0,8},{8,0},{1,9},{9,1},{2,10},{10,2},{3,11},{11,3},{4,12},{12,4},... | collective-permute-start | bytes 393224 | tf_op jit(solution)/shard_map/ppermute | solution.py:296

commit v3 on v2

v3 whole, which is shorter than its diff:
```python
import functools

import jax
import jax.numpy as jnp
from jax import lax
from jax.experimental import pallas as pl
from jax.experimental.pallas import tpu as pltpu
from jax.sharding import Mesh, PartitionSpec as P

D = 7168
KV = 512

OUTER_LR = 0.7
MOMENTUM_DECAY = 0.9
CLIP_RATIO = 0.25

NAMES = ("z_lo", "x", "core", "y", "z_hi")
SIZES = (8, 4, 2, 4, 2)
N_REPLICA = 64
SHARE = 14
ROWS = 896
PIECE = 112
LANES = 128
F32 = jnp.float32
BF16 = jnp.bfloat16
VMEM = pl.BlockSpec(memory_space=pltpu.VMEM)
PARAMS = pltpu.CompilerParams(vmem_limit_bytes=20 * 1024 * 1024)


LONG = pl.CostEstimate(flops=0, bytes_accessed=2**32, transcendentals=0)
TOKEN = jax.ShapeDtypeStruct((8, LANES), F32)


def call(body, name, out, args, after=(), scratch=(), first=VMEM, cost=None, through=None):
    anywhere = pl.BlockSpec(memory_space=pl.ANY)
    out, out_specs, aliases = tuple(out), [VMEM] * len(out), {}
    if through is not None:
        after, aliases = (*after, through), {len(args) + len(after): len(out)}
        out, out_specs = (*out, jax.ShapeDtypeStruct(through.shape, through.dtype)), out_specs + [anywhere]
    return pl.pallas_call(
        body,
        name=name,
        out_shape=out,
        in_specs=[first] + [VMEM] * (len(args) - 1) + [anywhere] * len(after),
        out_specs=out_specs,
        scratch_shapes=list(scratch),
        input_output_aliases=aliases,
        compiler_params=PARAMS,
        cost_estimate=cost,
    )(*args, *after)


def regroup_body(src, out, token, wide, grouped):
    token[...] = jnp.zeros_like(token)
    wide[...] = src[...].astype(F32)
    for xc in range(8):
        for z in range(8):
            first = PIECE * z + SHARE * xc
            grouped[xc, SHARE * z : SHARE * (z + 1), :] = wide[first : first + SHARE, :]
        out[xc] = grouped[xc].astype(BF16)


def cut_body(place, weight, after, own, mine):
    rows, cols = mine.shape
    own[...] = weight[:, pl.ds(pl.multiple_of(place[0] * cols, cols), cols)]
    mine[...] = own[pl.ds(pl.multiple_of(place[1] * rows, rows), rows), :]


def first_sum_body(parts, *rest):
    out, token, total = rest[-3:]
    token[...] = jnp.zeros_like(token)
    total[...] = functools.reduce(lambda a, b: a + b, [parts[i].astype(F32) for i in range(8)])
    for z in range(8):
        for j in range(4):
            out[z, SHARE * j : SHARE * (j + 1), :] = total[SHARE * z : SHARE * (z + 1), LANES * j : LANES * (j + 1)]


def lay_body(*refs):
    count = refs[-1].shape[0]
    for i in range(count):
        refs[-1][i] = refs[i][...]


def hold_body(given, after, out):
    out[...] = given[...]


def second_sum_body(parts, outer, *rest):
    delta, squares, token, through, total = rest[-5:]
    token[...] = jnp.zeros_like(token)
    total[...] = functools.reduce(lambda a, b: a + b, [parts[i] for i in range(8)])
    for j in range(4):
        cols = slice(LANES * j, LANES * (j + 1))
        delta[:, cols] = outer[:, cols] - total[SHARE * j : SHARE * (j + 1), :] / N_REPLICA
    d = delta[...]
    line = jnp.sum(d * d, axis=0, keepdims=True)
    line = line[:, :128] + line[:, 128:256] + line[:, 256:384] + line[:, 384:]
    squares[...] = jnp.broadcast_to(line[None], squares.shape)


def spread_sum_body(parts, *rest):
    out, token = rest[-2:]
    token[...] = jnp.zeros_like(token)
    out[...] = jnp.broadcast_to(jnp.sum(parts[...], axis=0, keepdims=True), out.shape)


def update_body(parts, delta, outer, momentum, new_outer, new_momentum):
    lanes = jnp.sum(parts[...], axis=0)[:1]
    length = jnp.sqrt(jnp.sum(lanes, axis=1, keepdims=True))
    limit = CLIP_RATIO * jnp.sqrt(jnp.full((1, 1), D * KV, F32))
    factor = jnp.minimum(1.0, limit / (length + 1e-06))
    clipped = factor * delta[...]
    moved = MOMENTUM_DECAY * momentum[...] + clipped
    new_momentum[...] = moved
    new_outer[...] = outer[...] - OUTER_LR * (clipped + MOMENTUM_DECAY * moved)


def norm_body(hidden, gain, after, out):
    for top in range(0, hidden.shape[0], 16):
        rows = slice(top, top + 16)
        squares = jnp.zeros((16, LANES), F32)
        for first in range(0, D, LANES):
            values = hidden[rows, first : first + LANES].astype(F32)
            squares += values * values
        scaled = lax.rsqrt(jnp.sum(squares, axis=1, keepdims=True) / D + 1e-05)
        scaled = jnp.broadcast_to(scaled, (16, LANES))
        for first in range(0, D, LANES):
            cols = slice(first, first + LANES)
            out[rows, cols] = (hidden[rows, cols].astype(F32) * scaled * gain[:, cols]).astype(BF16)


def norm(hidden, gain, after):
    rows, block = hidden.shape[0], 64
    return pl.pallas_call(
        norm_body,
        name="norm",
        grid=(rows // block,),
        out_shape=jax.ShapeDtypeStruct(hidden.shape, BF16),
        in_specs=[
            pl.BlockSpec((block, D), lambda i: (i, 0)),
            pl.BlockSpec((1, D), lambda i: (0, 0)),
            pl.BlockSpec(memory_space=pl.ANY),
        ],
        out_specs=pl.BlockSpec((block, D), lambda i: (i, 0)),
        compiler_params=PARAMS,
        cost_estimate=LONG,
    )(hidden, gain, after)


DOT = functools.partial(jnp.dot, preferred_element_type=F32)


def blocks(tokens, weights, order, first):
    cols = lambda k: pl.ds(pl.multiple_of(order[first + k] * ROWS, ROWS), ROWS)
    return functools.reduce(lambda a, b: a + b, [DOT(tokens[:, cols(k)], w[...]) for k, w in enumerate(weights)])


def project_own_body(order, near_in, far_in, early, late, after, near, far):
    parts = [early.at[0], early.at[1], late.at[0], late.at[1]]
    near[...] = blocks(near_in, parts, order, 0)
    far[...] = blocks(far_in, parts, order, 0)


def project_other_body(order, near_in, far_in, quad, quad_next, quad_late, near_own, far_own, near, far, weights):
    rows = quad.shape[1]
    for k in range(4):
        place = pl.ds(pl.multiple_of(order[8 + k] * rows, rows), rows)
        for j in range(4):
            weights[j, place, :] = (quad[j], quad_next[j], quad_late[0, j], quad_late[1, j])[k]
    parts = [weights.at[j] for j in range(4)]
    near[...] = (near_own[...] + blocks(near_in, parts, order, 4)).astype(BF16)
    far[...] = (far_own[...] + blocks(far_in, parts, order, 4)).astype(BF16)


def join_body(core, near, far, out):
    cols = near.shape[1]

    @pl.when(core[0] == 0)
    def _():
        out[:, :cols] = near[...]
        out[:, cols:] = far[...]

    @pl.when(core[0] == 1)
    def _():
        out[:, :cols] = far[...]
        out[:, cols:] = near[...]


def join(core, near, far):
    rows, cols = near.shape
    return pl.pallas_call(
        join_body,
        name="join",
        out_shape=jax.ShapeDtypeStruct((rows, 2 * cols), BF16),
        in_specs=[pl.BlockSpec(memory_space=pltpu.SMEM), VMEM, VMEM],
        out_specs=VMEM,
        compiler_params=PARAMS,
    )(core, near, far)


def exchange(array, axis, second):
    flips = (3, 1) if second else (1, 3)
    names = tuple(name for name in NAMES if name in (axis, "core"))
    number = lambda i, c: 2 * i + c if names[1] == "core" else 4 * c + i
    pairs = [(number(i, c), number(i ^ flips[c], c)) for i in range(4) for c in range(2)]
    return lax.ppermute(array, names, pairs)


SHIFTS = (1, 3, 2)


def spread(array, axis):
    return [lax.ppermute(array, axis, [(i, (i + s) % 4) for i in range(4)]) for s in SHIFTS]


def order_of(place, core):
    near = place ^ (1 + 2 * core)
    return [place, near, near ^ 2, place ^ 2]


def on_device(hidden_in, norm_gain, proj_weight, replica_params, outer_params, momentum):
    share, rows, cols = outer_params.shape, proj_weight.shape[0], KV // 2
    array = lambda dtype, *dims: jax.ShapeDtypeStruct(dims, dtype)
    x, y, core, half = [lax.axis_index(name).astype(jnp.int32) for name in ("x", "y", "core", "z_hi")]
    swap = [(0, 1), (1, 0)]

    scalars = pl.BlockSpec(memory_space=pltpu.SMEM)
    grouped, token = call(
        regroup_body, "regroup", (array(BF16, 8, PIECE, KV), TOKEN), (replica_params[0],),
        scratch=[pltpu.VMEM((ROWS, KV), F32), pltpu.VMEM((8, PIECE, KV), F32)],
    )
    own, mine = call(
        cut_body, "cut", (array(BF16, rows, cols), array(BF16, rows // 4, cols)),
        (jnp.stack([core, x]), proj_weight), (token,), first=scalars,
    )
    grouped = lax.all_to_all(grouped, ("x", "core"), 0, 0)
    mirror = [(2 * z + h, 2 * (7 - z) + 1 - h) for z in range(8) for h in range(2)]
    other = lax.ppermute(mine, ("z_lo", "z_hi"), mirror)
    own_next = exchange(own, "y", False)
    pieces, token = call(
        first_sum_body, "first_sum", (array(F32, 8, 56, LANES), TOKEN), (grouped,), (other, own_next),
        scratch=[pltpu.VMEM((PIECE, KV), F32)],
    )
    pieces = lax.all_to_all(pieces, "z_lo", 0, 0)
    gain = norm_gain.reshape(1, -1)
    normed = norm(hidden_in, gain, token)
    (early,) = call(lay_body, "pair", (array(BF16, 2, rows, cols),), (own, own_next), (token,))
    late = exchange(early, "y", True)
    (other,) = call(hold_body, "hold", (array(BF16, *other.shape),), (other,), (token,), cost=LONG)
    others = [other] + spread(other, "y")
    delta, squares, token, normed = call(
        second_sum_body, "second_sum", (array(F32, *share), array(F32, 32, 8, LANES), TOKEN),
        (pieces, outer_params), others[1:], [pltpu.VMEM((56, LANES), F32)], through=normed,
    )
    squares = lax.all_to_all(squares, ("y", "x", "core"), 0, 0)
    ys, other_ys, xs = order_of(y, core), [(y - s) % 4 for s in (0,) + SHIFTS], order_of(x, core)
    order = jnp.stack([2 * k + half for k in ys] + [2 * k + 1 - half for k in other_ys] + xs)
    quad = call(lay_body, "lay", (array(BF16, 4, rows // 4, cols),), others, (token,), cost=LONG)[0]
    quad_next = exchange(quad, "x", False)
    far_normed = lax.ppermute(normed, "core", swap)
    tokens = normed.shape[0]
    squares, token = call(
        spread_sum_body, "spread_sum", (array(F32, 16, 8, LANES), TOKEN), (squares,), (quad_next,)
    )
    squares = lax.all_to_all(squares, ("z_lo", "z_hi"), 0, 0)
    quads = call(lay_body, "pair", (array(BF16, 2, 4, rows // 4, cols),), (quad, quad_next), (token,))[0]
    quad_late = exchange(quads, "x", True)
    near, far = call(
        project_own_body, "project_own", (array(F32, tokens, cols),) * 2, (order, normed, far_normed, early, late), (token,),
        first=scalars, cost=LONG,
    )
    near, far = call(
        project_other_body, "project_other", (array(BF16, tokens, cols),) * 2,
        (order, normed, far_normed, quad, quad_next, quad_late, near, far),
        first=scalars, scratch=[pltpu.VMEM((4, rows, cols), BF16)], cost=LONG,
    )
    far = lax.ppermute(far, "core", swap)
    new_outer, new_momentum = call(
        update_body, "update", (array(F32, *share), array(F32, *share)), (squares, delta, outer_params, momentum)
    )
    projected = join(core.reshape(1), near, far)
    return (projected, new_outer, new_momentum)


def solution(mesh):
    inner = Mesh(mesh.devices.reshape(SIZES), NAMES)
    replica, fsdp = NAMES[:3], NAMES[3:]
    in_specs = (
        P(replica + fsdp, None),
        P(),
        P(fsdp, None),
        P(replica, fsdp, None),
        P(fsdp + replica, None),
        P(fsdp + replica, None),
    )
    out_specs = (
        P(replica + fsdp, None),
        P(fsdp + replica, None),
        P(fsdp + replica, None),
    )
    return jax.shard_map(
        on_device, mesh=inner, in_specs=in_specs, out_specs=out_specs, check_vma=False
    )
```

time: 110 us -> 109 us (level)
  local copies, waits for them, and re-layouts: 3.31 us -> 4.49 us
  other arithmetic: 1.18 us -> 0.07 us
    pallas_call x3 -> x1, Pallas kernels: 14.5 us -> 3.24 us  [norm(): pl.pallas_call(norm_body, name='norm', grid=(rows // block,), out_shape=j...]
    pallas_call x9 -> x12, Pallas kernels: 5.01 us -> 15.2 us  [call(): pl.pallas_call(body, name=name, out_shape=out, in_specs=[first] + [VMEM]...]
    all_to_all x1, waiting for transfers between devices: 0.92 us -> 4.26 us  [on_device(): squares = lax.all_to_all(squares, ('y', 'x', 'core'), 0, 0)]
    ppermute x4, waiting for transfers between devices: 2.57 us -> 0.01 us  [exchange(): return lax.ppermute(array, names, pairs)]
    ppermute x4, starting transfers between devices: 11.2 us -> 13 us  [exchange(): return lax.ppermute(array, names, pairs)]
    ppermute x1, starting transfers between devices: 2.3 us -> 3.81 us  [on_device(): far_normed = lax.ppermute(normed, 'core', swap)]
    ppermute x3, waiting for transfers between devices: 1.47 us -> 0.11 us  [spread(): lax.ppermute(array, axis, [(i, (i + s) % 4) for i in range(4)])]
    unnamed x12, local copies, waits for them, and re-layouts: 3.22 us -> 4.4 us
  transfers between devices with their start and end apart: 14 -> 14, of which waited for: 5 -> 4; matrix products, arithmetic and copies ran while one was open for 1% -> 0% of each run, Pallas kernels for 15% -> 14%
where the time goes in v3:
time: 109 us; the launch traced here: 108 us
  starting transfers between devices  68.7 us (63%)
  Pallas kernels  19.2 us (18%)
  waiting for transfers between devices  14.4 us (13%)
  local copies, waits for them, and re-layouts  4.49 us (4%)
    pallas_call x12, Pallas kernels, call(): pl.pallas_call(body, name=name, out_shape=out, in_specs=[first] + [VMEM]...  15.2 us
    ppermute x4, starting transfers between devices, exchange(): return lax.ppermute(array, names, pairs)  13 us
    all_to_all x1, starting transfers between devices, on_device(): grouped = lax.all_to_all(grouped, ('x', 'core'), 0, 0)  10.3 us
    ppermute x1, waiting for transfers between devices, on_device(): other = lax.ppermute(mine, ('z_lo', 'z_hi'), mirror)  9.8 us
    all_to_all x1, starting transfers between devices, on_device(): squares = lax.all_to_all(squares, ('z_lo', 'z_hi'), 0, 0)  9.74 us
    ppermute x1, starting transfers between devices, on_device(): other = lax.ppermute(mine, ('z_lo', 'z_hi'), mirror)  9.31 us
    ppermute x3, starting transfers between devices, spread(): lax.ppermute(array, axis, [(i, (i + s) % 4) for i in range(4)])  8.41 us
    all_to_all x1, starting transfers between devices, on_device(): pieces = lax.all_to_all(pieces, 'z_lo', 0, 0)  5.98 us
  transfers between devices with their start and end apart: 14, of which 4 were waited for; matrix products, arithmetic and copies ran while one was open for 0% of the time, Pallas kernels for 14%

profile of v3, /device:TPU:1, one launch (start us, length us, event | category | flops | bytes accessed | tf_op | source)
XLA Modules:
  0.0 107.7 jit_solution(16201165840943949678)
XLA Ops:
  0.6 1.2 %copy-done.1 = bf16[1,896,512]{2,1,0:T(8,128)(2,1)S(1)} copy-done((bf16[1,896,512]{2,1,0:T(8,128)(2,1)S(1)}, bf16[1,896,512]{2,1,0:T(8,128)(2,1)}, u32[]{:S(2)}) %copy-start.1) | copy-done | bytes 917528
  1.8 1.3 %regroup.1 = (bf16[8,112,512]{2,1,0:T(8,128)(2,1)}, f32[8,128]{1,0:T(8,128)S(1)}) custom-call(bf16[896,512]{1,0:T(8,128)(2,1)S(1)} %bitcast.15), custom_call_target="tpu_custom_call" | custom-call | tf_op jit(solution)/shard_map/regroup/pallas_call | solution.py:40
  3.1 10.3 %all-to-all-start = ((bf16[8,112,512]{2,1,0:T(8,128)(2,1)}), bf16[8,112,512]{2,1,0:T(8,128)(2,1)S(1)}, u32[]{:S(2)}, u32[]{:S(2)}) async-start(bf16[8,112,512]{2,1,0:T(8,128)(2,1)} %get-tuple-element.21), calls=%async_computation | async-start | bytes 1835008 | tf_op jit(solution)/shard_map/all_to_all | solution.py:236
  13.5 1.2 %copy-done.2 = bf16[896,512]{1,0:T(8,128)(2,1)S(1)} copy-done((bf16[896,512]{1,0:T(8,128)(2,1)S(1)}, bf16[896,512]{1,0:T(8,128)(2,1)}, u32[]{:S(2)}) %copy-start.2) | copy-done | bytes 917528
  14.7 0.6 cut.1
  15.3 1.9 %collective-permute-start.1 = (bf16[896,256]{1,0:T(8,128)(2,1)S(1)}, bf16[896,256]{1,0:T(8,128)(2,1)S(1)}, u32[]{:S(2)}, u32[]{:S(2)}) collective-permute-start(bf16[896,256]{1,0:T(8,128)(2,1)S(1)} %get-tuple-element.24.refs_0_), channel_id=1, source_target_pairs={{0,2},{8,14},{2,0},{10,12},{4,6},{12,10},{6,4},{14,8},{1,3},{9,15}... | collective-permute-start | bytes 1376264 | tf_op jit(solution)/shard_map/ppermute | solution.py:206
  17.2 9.3 %collective-permute-start = (bf16[224,256]{1,0:T(8,128)(2,1)S(1)}, bf16[224,256]{1,0:T(8,128)(2,1)S(1)}, u32[]{:S(2)}, u32[]{:S(2)}) collective-permute-start(bf16[224,256]{1,0:T(8,128)(2,1)S(1)} %get-tuple-element.23), channel_id=1, source_target_pairs={{0,449},{1,448},{64,385},{65,384},{128,321},{129,320},{192,257},{1... | collective-permute-start | bytes 344072 | tf_op jit(solution)/shard_map/ppermute | solution.py:238
  26.5 9.8 %collective-permute-done.rest_0_.given = bf16[224,256]{1,0:T(8,128)(2,1)S(1)} collective-permute-done((bf16[224,256]{1,0:T(8,128)(2,1)S(1)}, bf16[224,256]{1,0:T(8,128)(2,1)S(1)}, u32[]{:S(2)}, u32[]{:S(2)}) %collective-permute-start) | collective-permute-done | bytes 114720 | tf_op jit(solution)/shard_map/ppermute | solution.py:238
  36.3 0.9 first_sum.1
  37.2 6.0 %all-to-all-start.1 = ((f32[8,56,128]{2,1,0:T(8,128)}), f32[8,56,128]{2,1,0:T(8,128)S(1)}, u32[]{:S(2)}, u32[]{:S(2)}) async-start(f32[8,56,128]{2,1,0:T(8,128)} %get-tuple-element.25), calls=%async_computation.1 | async-start | bytes 458752 | tf_op jit(solution)/shard_map/all_to_all | solution.py:244
  43.2 2.1 %collective-permute-start.2 = (bf16[224,256]{1,0:T(8,128)(2,1)S(1)}, bf16[224,256]{1,0:T(8,128)(2,1)S(1)}, u32[]{:S(2)}, u32[]{:S(2)}) collective-permute-start(bf16[224,256]{1,0:T(8,128)(2,1)S(1)} %hold.1.refs_0_), channel_id=1, source_target_pairs={{0,2},{2,4},{4,6},{6,0},{1,3},{3,5},{5,7},{7,1},{8,10},{10,12},{12... | collective-permute-start | bytes 344072 | tf_op jit(solution)/shard_map/ppermute | solution.py:213
  45.3 4.4 %collective-permute-start.3 = (bf16[224,256]{1,0:T(8,128)(2,1)S(1)}, bf16[224,256]{1,0:T(8,128)(2,1)S(1)}, u32[]{:S(2)}, u32[]{:S(2)}) collective-permute-start(bf16[224,256]{1,0:T(8,128)(2,1)S(1)} %hold.1.refs_0_), channel_id=1, source_target_pairs={{0,6},{2,0},{4,2},{6,4},{1,7},{3,1},{5,3},{7,5},{8,14},{10,8},{12,... | collective-permute-start | bytes 344072 | tf_op jit(solution)/shard_map/ppermute | solution.py:213
  49.7 1.9 %collective-permute-start.4 = (bf16[224,256]{1,0:T(8,128)(2,1)S(1)}, bf16[224,256]{1,0:T(8,128)(2,1)S(1)}, u32[]{:S(2)}, u32[]{:S(2)}) collective-permute-start(bf16[224,256]{1,0:T(8,128)(2,1)S(1)} %hold.1.refs_0_), channel_id=1, source_target_pairs={{0,4},{2,6},{4,0},{6,2},{1,5},{3,7},{5,1},{7,3},{8,12},{10,14},{12... | collective-permute-start | bytes 344072 | tf_op jit(solution)/shard_map/ppermute | solution.py:213
  51.7 2.0 %copy-done = bf16[256,7168]{1,0:T(8,128)(2,1)S(1)} copy-done((bf16[256,7168]{1,0:T(8,128)(2,1)S(1)}, bf16[256,7168]{1,0:T(8,128)(2,1)}, u32[]{:S(2)}) %copy-start) | copy-done | bytes 3670040
  53.7 3.2 %norm.1.rest_3_ = bf16[256,7168]{1,0:T(8,128)(2,1)} custom-call(bf16[256,7168]{1,0:T(8,128)(2,1)S(1)} %copy-done, f32[1,7168]{1,0:T(1,128)S(1)} %bitcast.16, f32[8,128]{1,0:T(8,128)S(1)} %get-tuple-element.26.after.refs_2_), custom_call_target="tpu_custom_call" | custom-call | bytes 4294967296 | tf_op jit(solution)/shard_map/norm/pallas_call | solution.py:134
  57.0 0.1 collective-permute-done.4.rest_2_.refs_3_
  57.1 0.7 second_sum.1
  57.8 3.8 %collective-permute-start.5 = (bf16[256,7168]{1,0:T(8,128)(2,1)}, bf16[256,7168]{1,0:T(8,128)(2,1)}, u32[]{:S(2)}, u32[]{:S(2)}) collective-permute-start(bf16[256,7168]{1,0:T(8,128)(2,1)} %get-tuple-element.27.near_in), channel_id=1, source_target_pairs={{0,8},{8,0},{1,9},{9,1},{2,10},{10,2},{3,11},{11,3},{4,12},{12,4},... | collective-permute-start | bytes 11010056 | tf_op jit(solution)/shard_map/ppermute | solution.py:260
  61.6 5.5 %collective-permute-start.6 = (bf16[4,224,256]{2,1,0:T(8,128)(2,1)S(1)}, bf16[4,224,256]{2,1,0:T(8,128)(2,1)S(1)}, u32[]{:S(2)}, u32[]{:S(2)}) collective-permute-start(bf16[4,224,256]{2,1,0:T(8,128)(2,1)S(1)} %lay.1.refs_0_.quad), channel_id=1, source_target_pairs={{0,16},{8,56},{16,0},{24,40},{32,48},{40,24},{48,32},{56,8},{1,17}... | collective-permute-start | bytes 1376264 | tf_op jit(solution)/shard_map/ppermute | solution.py:206
  67.1 4.6 %all-to-all-start.2 = ((f32[32,8,128]{2,1,0:T(8,128)}), f32[32,8,128]{2,1,0:T(8,128)S(1)}, u32[]{:S(2)}, u32[]{:S(2)}) async-start(f32[32,8,128]{2,1,0:T(8,128)} %get-tuple-element.29), calls=%async_computation.2 | async-start | bytes 262144 | tf_op jit(solution)/shard_map/all_to_all | solution.py:255
  71.8 3.3 %collective-permute-start.8 = (bf16[2,896,256]{2,1,0:T(8,128)(2,1)S(1)}, bf16[2,896,256]{2,1,0:T(8,128)(2,1)S(1)}, u32[]{:S(2)}, u32[]{:S(2)}) collective-permute-start(bf16[2,896,256]{2,1,0:T(8,128)(2,1)S(1)} %pair.3.early), channel_id=1, source_target_pairs={{0,6},{8,10},{2,4},{10,8},{4,2},{12,14},{6,0},{14,12},{1,7},{9,11}... | collective-permute-start | bytes 2752520 | tf_op jit(solution)/shard_map/ppermute | solution.py:206
  75.1 4.3 %all-to-all-done.2.parts = f32[32,8,128]{2,1,0:T(8,128)S(1)} async-done(((f32[32,8,128]{2,1,0:T(8,128)}), f32[32,8,128]{2,1,0:T(8,128)S(1)}, u32[]{:S(2)}, u32[]{:S(2)}) %all-to-all-start.2) | async-done | bytes 131104 | tf_op jit(solution)/shard_map/all_to_all | solution.py:255
  79.4 0.7 spread_sum.1
  80.1 1.1 pair.2
  81.1 2.3 %collective-permute-start.7 = (bf16[2,4,224,256]{3,2,1,0:T(8,128)(2,1)}, bf16[2,4,224,256]{3,2,1,0:T(8,128)(2,1)}, u32[]{:S(2)}, u32[]{:S(2)}) collective-permute-start(bf16[2,4,224,256]{3,2,1,0:T(8,128)(2,1)} %pair.2), channel_id=1, source_target_pairs={{0,48},{8,24},{16,32},{24,8},{32,16},{40,56},{48,0},{56,40},{1,49}... | collective-permute-start | bytes 2752520 | tf_op jit(solution)/shard_map/ppermute | solution.py:206
  83.4 9.7 %all-to-all-start.3 = ((f32[16,8,128]{2,1,0:T(8,128)}), f32[16,8,128]{2,1,0:T(8,128)S(1)}, u32[]{:S(2)}, u32[]{:S(2)}) async-start(f32[16,8,128]{2,1,0:T(8,128)} %get-tuple-element.35), calls=%async_computation.3 | async-start | bytes 131072 | tf_op jit(solution)/shard_map/all_to_all | solution.py:265
  93.4 4.4 %project_own.1 = (f32[256,256]{1,0:T(8,128)S(1)}, f32[256,256]{1,0:T(8,128)S(1)}) custom-call(s32[12]{0:T(128)S(1)} %stack.56.order, bf16[256,7168]{1,0:T(8,128)(2,1)} %get-tuple-element.27.near_in, bf16[256,7168]{1,0:T(8,128)(2,1)} %collective-permute-done.5.far_in, bf16[2,896,256]{2,1,0:T(8,128)(2,1)S(1)} %pair.3.early, ...), custom_call_target="tpu_custom_call" | custom-call | bytes 4294967296 | tf_op jit(solution)/shard_map/project_own/pallas_call | solution.py:40
  97.8 4.7 %project_other.1 = (bf16[256,256]{1,0:T(8,128)(2,1)S(1)}, bf16[256,256]{1,0:T(8,128)(2,1)S(1)}) custom-call(s32[12]{0:T(128)S(1)} %stack.56.order, bf16[256,7168]{1,0:T(8,128)(2,1)} %get-tuple-element.27.near_in, bf16[256,7168]{1,0:T(8,128)(2,1)} %collective-permute-done.5.far_in, bf16[4,224,256]{2,1,0:T(8,128)(2,1)S(1)} %lay.1.refs_0_.quad, ...), custom_call_target="tpu_custom_call" | custom-call | bytes 4294967296 | tf_op jit(solution)/shard_map/project_other/pallas_call | solution.py:40
  102.5 3.5 %collective-permute-start.9 = (bf16[256,256]{1,0:T(8,128)(2,1)S(1)}, bf16[256,256]{1,0:T(8,128)(2,1)S(1)}, u32[]{:S(2)}, u32[]{:S(2)}) collective-permute-start(bf16[256,256]{1,0:T(8,128)(2,1)S(1)} %get-tuple-element.34), channel_id=1, source_target_pairs={{0,8},{8,0},{1,9},{9,1},{2,10},{10,2},{3,11},{11,3},{4,12},{12,4},... | collective-permute-start | bytes 393224 | tf_op jit(solution)/shard_map/ppermute | solution.py:277
  106.1 0.7 update.1
  106.8 0.2 collective-permute-done.9.far
  107.0 0.7 join.1
  (24 shorter events, 0.3 us)
Async XLA Ops:
  0.6 1.2 %copy-start.1 = (bf16[1,896,512]{2,1,0:T(8,128)(2,1)S(1)}, bf16[1,896,512]{2,1,0:T(8,128)(2,1)}, u32[]{:S(2)}) copy-start(bf16[1,896,512]{2,1,0:T(8,128)(2,1)} %param.9) | copy-start | bytes 2752516
  1.8 49.8 %copy-start.5 = (f32[7168]{0:T(1024)S(1)}, f32[7168]{0:T(1024)}, u32[]{:S(2)}) copy-start(f32[7168]{0:T(1024)} %param.7) | copy-start | bytes 86020
  3.1 33.2 %all-to-all-start = ((bf16[8,112,512]{2,1,0:T(8,128)(2,1)}), bf16[8,112,512]{2,1,0:T(8,128)(2,1)S(1)}, u32[]{:S(2)}, u32[]{:S(2)}) async-start(bf16[8,112,512]{2,1,0:T(8,128)(2,1)} %get-tuple-element.21), calls=%async_computation | async-start | bytes 1835008 | tf_op jit(solution)/shard_map/all_to_all | solution.py:236
  13.5 1.2 %copy-start.2 = (bf16[896,512]{1,0:T(8,128)(2,1)S(1)}, bf16[896,512]{1,0:T(8,128)(2,1)}, u32[]{:S(2)}) copy-start(bf16[896,512]{1,0:T(8,128)(2,1)} %weight.1) | copy-start | bytes 2752516
  15.3 21.0 %collective-permute-start.1 = (bf16[896,256]{1,0:T(8,128)(2,1)S(1)}, bf16[896,256]{1,0:T(8,128)(2,1)S(1)}, u32[]{:S(2)}, u32[]{:S(2)}) collective-permute-start(bf16[896,256]{1,0:T(8,128)(2,1)S(1)} %get-tuple-element.24.refs_0_), channel_id=1, source_target_pairs={{0,2},{8,14},{2,0},{10,12},{4,6},{12,10},{6,4},{14,8},{1,3},{9,15}... | collective-permute-start | bytes 1376264 | tf_op jit(solution)/shard_map/ppermute | solution.py:206
  17.2 19.1 %collective-permute-start = (bf16[224,256]{1,0:T(8,128)(2,1)S(1)}, bf16[224,256]{1,0:T(8,128)(2,1)S(1)}, u32[]{:S(2)}, u32[]{:S(2)}) collective-permute-start(bf16[224,256]{1,0:T(8,128)(2,1)S(1)} %get-tuple-element.23), channel_id=1, source_target_pairs={{0,449},{1,448},{64,385},{65,384},{128,321},{129,320},{192,257},{1... | collective-permute-start | bytes 344072 | tf_op jit(solution)/shard_map/ppermute | solution.py:238
  37.2 19.8 %all-to-all-start.1 = ((f32[8,56,128]{2,1,0:T(8,128)}), f32[8,56,128]{2,1,0:T(8,128)S(1)}, u32[]{:S(2)}, u32[]{:S(2)}) async-start(f32[8,56,128]{2,1,0:T(8,128)} %get-tuple-element.25), calls=%async_computation.1 | async-start | bytes 458752 | tf_op jit(solution)/shard_map/all_to_all | solution.py:244
  43.2 13.7 %collective-permute-start.2 = (bf16[224,256]{1,0:T(8,128)(2,1)S(1)}, bf16[224,256]{1,0:T(8,128)(2,1)S(1)}, u32[]{:S(2)}, u32[]{:S(2)}) collective-permute-start(bf16[224,256]{1,0:T(8,128)(2,1)S(1)} %hold.1.refs_0_), channel_id=1, source_target_pairs={{0,2},{2,4},{4,6},{6,0},{1,3},{3,5},{5,7},{7,1},{8,10},{10,12},{12... | collective-permute-start | bytes 344072 | tf_op jit(solution)/shard_map/ppermute | solution.py:213
  45.3 11.7 %collective-permute-start.3 = (bf16[224,256]{1,0:T(8,128)(2,1)S(1)}, bf16[224,256]{1,0:T(8,128)(2,1)S(1)}, u32[]{:S(2)}, u32[]{:S(2)}) collective-permute-start(bf16[224,256]{1,0:T(8,128)(2,1)S(1)} %hold.1.refs_0_), channel_id=1, source_target_pairs={{0,6},{2,0},{4,2},{6,4},{1,7},{3,1},{5,3},{7,5},{8,14},{10,8},{12,... | collective-permute-start | bytes 344072 | tf_op jit(solution)/shard_map/ppermute | solution.py:213
  49.7 7.3 %collective-permute-start.4 = (bf16[224,256]{1,0:T(8,128)(2,1)S(1)}, bf16[224,256]{1,0:T(8,128)(2,1)S(1)}, u32[]{:S(2)}, u32[]{:S(2)}) collective-permute-start(bf16[224,256]{1,0:T(8,128)(2,1)S(1)} %hold.1.refs_0_), channel_id=1, source_target_pairs={{0,4},{2,6},{4,0},{6,2},{1,5},{3,7},{5,1},{7,3},{8,12},{10,14},{12... | collective-permute-start | bytes 344072 | tf_op jit(solution)/shard_map/ppermute | solution.py:213
  51.7 2.0 %copy-start = (bf16[256,7168]{1,0:T(8,128)(2,1)S(1)}, bf16[256,7168]{1,0:T(8,128)(2,1)}, u32[]{:S(2)}) copy-start(bf16[256,7168]{1,0:T(8,128)(2,1)} %hidden.1) | copy-start | bytes 11010052
  53.7 3.4 %copy-start.3 = (f32[14,512]{1,0:T(8,128)S(1)}, f32[14,512]{1,0:T(8,128)}, u32[]{:S(2)}) copy-start(f32[14,512]{1,0:T(8,128)} %outer.3) | copy-start | bytes 86020
  57.8 35.6 %collective-permute-start.5 = (bf16[256,7168]{1,0:T(8,128)(2,1)}, bf16[256,7168]{1,0:T(8,128)(2,1)}, u32[]{:S(2)}, u32[]{:S(2)}) collective-permute-start(bf16[256,7168]{1,0:T(8,128)(2,1)} %get-tuple-element.27.near_in), channel_id=1, source_target_pairs={{0,8},{8,0},{1,9},{9,1},{2,10},{10,2},{3,11},{11,3},{4,12},{12,4},... | collective-permute-start | bytes 11010056 | tf_op jit(solution)/shard_map/ppermute | solution.py:260
  61.6 17.8 %collective-permute-start.6 = (bf16[4,224,256]{2,1,0:T(8,128)(2,1)S(1)}, bf16[4,224,256]{2,1,0:T(8,128)(2,1)S(1)}, u32[]{:S(2)}, u32[]{:S(2)}) collective-permute-start(bf16[4,224,256]{2,1,0:T(8,128)(2,1)S(1)} %lay.1.refs_0_.quad), channel_id=1, source_target_pairs={{0,16},{8,56},{16,0},{24,40},{32,48},{40,24},{48,32},{56,8},{1,17}... | collective-permute-start | bytes 1376264 | tf_op jit(solution)/shard_map/ppermute | solution.py:206
  67.1 12.2 %all-to-all-start.2 = ((f32[32,8,128]{2,1,0:T(8,128)}), f32[32,8,128]{2,1,0:T(8,128)S(1)}, u32[]{:S(2)}, u32[]{:S(2)}) async-start(f32[32,8,128]{2,1,0:T(8,128)} %get-tuple-element.29), calls=%async_computation.2 | async-start | bytes 262144 | tf_op jit(solution)/shard_map/all_to_all | solution.py:255
  71.8 21.5 %collective-permute-start.8 = (bf16[2,896,256]{2,1,0:T(8,128)(2,1)S(1)}, bf16[2,896,256]{2,1,0:T(8,128)(2,1)S(1)}, u32[]{:S(2)}, u32[]{:S(2)}) collective-permute-start(bf16[2,896,256]{2,1,0:T(8,128)(2,1)S(1)} %pair.3.early), channel_id=1, source_target_pairs={{0,6},{8,10},{2,4},{10,8},{4,2},{12,14},{6,0},{14,12},{1,7},{9,11}... | collective-permute-start | bytes 2752520 | tf_op jit(solution)/shard_map/ppermute | solution.py:206
  81.1 16.7 %collective-permute-start.7 = (bf16[2,4,224,256]{3,2,1,0:T(8,128)(2,1)}, bf16[2,4,224,256]{3,2,1,0:T(8,128)(2,1)}, u32[]{:S(2)}, u32[]{:S(2)}) collective-permute-start(bf16[2,4,224,256]{3,2,1,0:T(8,128)(2,1)} %pair.2), channel_id=1, source_target_pairs={{0,48},{8,24},{16,32},{24,8},{32,16},{40,56},{48,0},{56,40},{1,49}... | collective-permute-start | bytes 2752520 | tf_op jit(solution)/shard_map/ppermute | solution.py:206
  83.4 22.6 %all-to-all-start.3 = ((f32[16,8,128]{2,1,0:T(8,128)}), f32[16,8,128]{2,1,0:T(8,128)S(1)}, u32[]{:S(2)}, u32[]{:S(2)}) async-start(f32[16,8,128]{2,1,0:T(8,128)} %get-tuple-element.35), calls=%async_computation.3 | async-start | bytes 131072 | tf_op jit(solution)/shard_map/all_to_all | solution.py:265
  97.8 8.3 %copy-start.4 = (f32[14,512]{1,0:T(8,128)S(1)}, f32[14,512]{1,0:T(8,128)}, u32[]{:S(2)}) copy-start(f32[14,512]{1,0:T(8,128)} %momentum.1) | copy-start | bytes 86020
  102.5 4.5 %collective-permute-start.9 = (bf16[256,256]{1,0:T(8,128)(2,1)S(1)}, bf16[256,256]{1,0:T(8,128)(2,1)S(1)}, u32[]{:S(2)}, u32[]{:S(2)}) collective-permute-start(bf16[256,256]{1,0:T(8,128)(2,1)S(1)} %get-tuple-element.34), channel_id=1, source_target_pairs={{0,8},{8,0},{1,9},{9,1},{2,10},{10,2},{3,11},{11,3},{4,12},{12,4},... | collective-permute-start | bytes 393224 | tf_op jit(solution)/shard_map/ppermute | solution.py:277

commit v4 on v3

--- a/solution.py
+++ b/solution.py
@@ -41,7 +41,7 @@
         body,
         name=name,
         out_shape=out,
-        in_specs=[first] + [VMEM] * (len(args) - 1) + [anywhere] * len(after),
+        in_specs=[first] + [VMEM] * (len(args) - 1 + len(after) - len(aliases)) + [anywhere] * len(aliases),
         out_specs=out_specs,
         scratch_shapes=list(scratch),
         input_output_aliases=aliases,
@@ -150,26 +150,52 @@
 DOT = functools.partial(jnp.dot, preferred_element_type=F32)
 
 
-def blocks(tokens, weights, order, first):
-    cols = lambda k: pl.ds(pl.multiple_of(order[first + k] * ROWS, ROWS), ROWS)
-    return functools.reduce(lambda a, b: a + b, [DOT(tokens[:, cols(k)], w[...]) for k, w in enumerate(weights)])
-
-
-def project_own_body(order, near_in, far_in, early, late, after, near, far):
-    parts = [early.at[0], early.at[1], late.at[0], late.at[1]]
-    near[...] = blocks(near_in, parts, order, 0)
-    far[...] = blocks(far_in, parts, order, 0)
-
-
-def project_other_body(order, near_in, far_in, quad, quad_next, quad_late, near_own, far_own, near, far, weights):
+def project_body(order, normed, far_normed, early, late, quad, quad_next, quad_late, near, far, held, weights, sums, arrived):
+    copies = [
+        [
+            pltpu.make_async_copy(
+                tokens.at[:, pl.ds(pl.multiple_of(order[k] * ROWS, ROWS), ROWS)], held.at[t, k], arrived.at[t, k]
+            )
+            for t, tokens in enumerate((normed, far_normed))
+        ]
+        for k in range(8)
+    ]
+    for pair in copies:
+        for copy in pair:
+            copy.start()
     rows = quad.shape[1]
     for k in range(4):
         place = pl.ds(pl.multiple_of(order[8 + k] * rows, rows), rows)
         for j in range(4):
             weights[j, place, :] = (quad[j], quad_next[j], quad_late[0, j], quad_late[1, j])[k]
-    parts = [weights.at[j] for j in range(4)]
-    near[...] = (near_own[...] + blocks(near_in, parts, order, 4)).astype(BF16)
-    far[...] = (far_own[...] + blocks(far_in, parts, order, 4)).astype(BF16)
+    parts = [early.at[0], early.at[1], late.at[0], late.at[1]] + [weights.at[j] for j in range(4)]
+    for k in range(8):
+        for t in range(2):
+            copies[k][t].wait()
+            term = DOT(held[t, k], parts[k][...])
+            sums[t] = term if k == 0 else sums[t] + term
+    near[...] = sums[0].astype(BF16)
+    far[...] = sums[1].astype(BF16)
+
+
+def project(order, normed, far_normed, early, late, quad, quad_next, quad_late):
+    rows, cols = normed.shape[0], early.shape[2]
+    anywhere = pl.BlockSpec(memory_space=pl.ANY)
+    return pl.pallas_call(
+        project_body,
+        name="project",
+        out_shape=(jax.ShapeDtypeStruct((rows, cols), BF16),) * 2,
+        in_specs=[pl.BlockSpec(memory_space=pltpu.SMEM), anywhere, anywhere] + [VMEM] * 5,
+        out_specs=(VMEM, VMEM),
+        scratch_shapes=[
+            pltpu.VMEM((2, 8, rows, ROWS), BF16),
+            pltpu.VMEM((4, ROWS, cols), BF16),
+            pltpu.VMEM((2, rows, cols), F32),
+            pltpu.SemaphoreType.DMA((2, 8)),
+        ],
+        compiler_params=PARAMS,
+        cost_estimate=LONG,
+    )(order, normed, far_normed, early, late, quad, quad_next, quad_late)
 
 
 def join_body(core, near, far, out):
@@ -258,22 +284,13 @@
     quad = call(lay_body, "lay", (array(BF16, 4, rows // 4, cols),), others, (token,), cost=LONG)[0]
     quad_next = exchange(quad, "x", False)
     far_normed = lax.ppermute(normed, "core", swap)
-    tokens = normed.shape[0]
     squares, token = call(
         spread_sum_body, "spread_sum", (array(F32, 16, 8, LANES), TOKEN), (squares,), (quad_next,)
     )
     squares = lax.all_to_all(squares, ("z_lo", "z_hi"), 0, 0)
     quads = call(lay_body, "pair", (array(BF16, 2, 4, rows // 4, cols),), (quad, quad_next), (token,))[0]
     quad_late = exchange(quads, "x", True)
-    near, far = call(
-        project_own_body, "project_own", (array(F32, tokens, cols),) * 2, (order, normed, far_normed, early, late), (token,),
-        first=scalars, cost=LONG,
-    )
-    near, far = call(
-        project_other_body, "project_other", (array(BF16, tokens, cols),) * 2,
-        (order, normed, far_normed, quad, quad_next, quad_late, near, far),
-        first=scalars, scratch=[pltpu.VMEM((4, rows, cols), BF16)], cost=LONG,
-    )
+    near, far = project(order, normed, far_normed, early, late, quad, quad_next, quad_late)
     far = lax.ppermute(far, "core", swap)
     new_outer, new_momentum = call(
         update_body, "update", (array(F32, *share), array(F32, *share)), (squares, delta, outer_params, momentum)

time: 109 us -> 109 us (level)
  Pallas kernels: 19.2 us -> 16.7 us
  waiting for transfers between devices: 14.4 us -> 16.6 us
    pallas_call x12 -> x10, Pallas kernels: 15.2 us -> 5.06 us  [call(): pl.pallas_call(body, name=name, out_shape=out, in_specs=[first] + [VMEM]...]
    pallas_call x0 -> x1, Pallas kernels: none -> 7.73 us  [project(): pl.pallas_call(project_body, name='project', out_shape=(jax.ShapeDtypeStr...]
    ppermute x4, waiting for transfers between devices: 0.01 us -> 2.31 us  [exchange(): return lax.ppermute(array, names, pairs)]
  transfers between devices with their start and end apart: 14 -> 14, of which waited for: 4 -> 4; matrix products, arithmetic and copies ran while one was open for 0% -> 0% of each run, Pallas kernels for 14% -> 12%
where the time goes in v4:
time: 109 us; the launch traced here: 108 us
  starting transfers between devices  69.5 us (64%)
  Pallas kernels  16.7 us (15%)
  waiting for transfers between devices  16.6 us (15%)
  local copies, waits for them, and re-layouts  4.49 us (4%)
    ppermute x4, starting transfers between devices, exchange(): return lax.ppermute(array, names, pairs)  13 us
    all_to_all x1, starting transfers between devices, on_device(): grouped = lax.all_to_all(grouped, ('x', 'core'), 0, 0)  10.3 us
    ppermute x1, waiting for transfers between devices, on_device(): other = lax.ppermute(mine, ('z_lo', 'z_hi'), mirror)  9.8 us
    all_to_all x1, starting transfers between devices, on_device(): squares = lax.all_to_all(squares, ('z_lo', 'z_hi'), 0, 0)  9.74 us
    ppermute x1, starting transfers between devices, on_device(): other = lax.ppermute(mine, ('z_lo', 'z_hi'), mirror)  9.31 us
    ppermute x3, starting transfers between devices, spread(): lax.ppermute(array, axis, [(i, (i + s) % 4) for i in range(4)])  8.3 us
    pallas_call x1, Pallas kernels, project(): pl.pallas_call(project_body, name='project', out_shape=(jax.ShapeDtypeStr...  7.73 us
    all_to_all x1, starting transfers between devices, on_device(): pieces = lax.all_to_all(pieces, 'z_lo', 0, 0)  5.98 us
  transfers between devices with their start and end apart: 14, of which 4 were waited for; matrix products, arithmetic and copies ran while one was open for 0% of the time, Pallas kernels for 12%

profile of v4, /device:TPU:1, one launch (start us, length us, event | category | flops | bytes accessed | tf_op | source)
XLA Modules:
  0.0 108.3 jit_solution(1027753873621640695)
XLA Ops:
  0.6 1.2 %copy-done.1 = bf16[1,896,512]{2,1,0:T(8,128)(2,1)S(1)} copy-done((bf16[1,896,512]{2,1,0:T(8,128)(2,1)S(1)}, bf16[1,896,512]{2,1,0:T(8,128)(2,1)}, u32[]{:S(2)}) %copy-start.1) | copy-done | bytes 917528
  1.8 1.3 %regroup.1 = (bf16[8,112,512]{2,1,0:T(8,128)(2,1)}, f32[8,128]{1,0:T(8,128)S(1)}) custom-call(bf16[896,512]{1,0:T(8,128)(2,1)S(1)} %bitcast.15), custom_call_target="tpu_custom_call" | custom-call | tf_op jit(solution)/shard_map/regroup/pallas_call | solution.py:40
  3.1 10.3 %all-to-all-start = ((bf16[8,112,512]{2,1,0:T(8,128)(2,1)}), bf16[8,112,512]{2,1,0:T(8,128)(2,1)S(1)}, u32[]{:S(2)}, u32[]{:S(2)}) async-start(bf16[8,112,512]{2,1,0:T(8,128)(2,1)} %get-tuple-element.19), calls=%async_computation | async-start | bytes 1835008 | tf_op jit(solution)/shard_map/all_to_all | solution.py:262
  13.5 0.1 pad_add_fusion.place
  13.5 1.2 %copy-done.2 = bf16[896,512]{1,0:T(8,128)(2,1)S(1)} copy-done((bf16[896,512]{1,0:T(8,128)(2,1)S(1)}, bf16[896,512]{1,0:T(8,128)(2,1)}, u32[]{:S(2)}) %copy-start.2) | copy-done | bytes 917528
  14.7 0.6 cut.1
  15.3 1.9 %collective-permute-start.1 = (bf16[896,256]{1,0:T(8,128)(2,1)S(1)}, bf16[896,256]{1,0:T(8,128)(2,1)S(1)}, u32[]{:S(2)}, u32[]{:S(2)}) collective-permute-start(bf16[896,256]{1,0:T(8,128)(2,1)S(1)} %get-tuple-element.22.refs_0_), channel_id=1, source_target_pairs={{0,2},{8,14},{2,0},{10,12},{4,6},{12,10},{6,4},{14,8},{1,3},{9,15}... | collective-permute-start | bytes 1376264 | tf_op jit(solution)/shard_map/ppermute | solution.py:232
  17.2 9.3 %collective-permute-start = (bf16[224,256]{1,0:T(8,128)(2,1)S(1)}, bf16[224,256]{1,0:T(8,128)(2,1)S(1)}, u32[]{:S(2)}, u32[]{:S(2)}) collective-permute-start(bf16[224,256]{1,0:T(8,128)(2,1)S(1)} %get-tuple-element.21), channel_id=1, source_target_pairs={{0,449},{1,448},{64,385},{65,384},{128,321},{129,320},{192,257},{1... | collective-permute-start | bytes 344072 | tf_op jit(solution)/shard_map/ppermute | solution.py:264
  26.5 9.8 %collective-permute-done.rest_0_.given = bf16[224,256]{1,0:T(8,128)(2,1)S(1)} collective-permute-done((bf16[224,256]{1,0:T(8,128)(2,1)S(1)}, bf16[224,256]{1,0:T(8,128)(2,1)S(1)}, u32[]{:S(2)}, u32[]{:S(2)}) %collective-permute-start) | collective-permute-done | bytes 114720 | tf_op jit(solution)/shard_map/ppermute | solution.py:264
  36.4 0.9 first_sum.1
  37.2 6.0 %all-to-all-start.1 = ((f32[8,56,128]{2,1,0:T(8,128)}), f32[8,56,128]{2,1,0:T(8,128)S(1)}, u32[]{:S(2)}, u32[]{:S(2)}) async-start(f32[8,56,128]{2,1,0:T(8,128)} %get-tuple-element.23), calls=%async_computation.1 | async-start | bytes 458752 | tf_op jit(solution)/shard_map/all_to_all | solution.py:270
  43.2 2.8 %collective-permute-start.4 = (bf16[224,256]{1,0:T(8,128)(2,1)S(1)}, bf16[224,256]{1,0:T(8,128)(2,1)S(1)}, u32[]{:S(2)}, u32[]{:S(2)}) collective-permute-start(bf16[224,256]{1,0:T(8,128)(2,1)S(1)} %hold.1.refs_0_), channel_id=1, source_target_pairs={{0,4},{2,6},{4,0},{6,2},{1,5},{3,7},{5,1},{7,3},{8,12},{10,14},{12... | collective-permute-start | bytes 344072 | tf_op jit(solution)/shard_map/ppermute | solution.py:239
  46.1 3.6 %collective-permute-start.3 = (bf16[224,256]{1,0:T(8,128)(2,1)S(1)}, bf16[224,256]{1,0:T(8,128)(2,1)S(1)}, u32[]{:S(2)}, u32[]{:S(2)}) collective-permute-start(bf16[224,256]{1,0:T(8,128)(2,1)S(1)} %hold.1.refs_0_), channel_id=1, source_target_pairs={{0,6},{2,0},{4,2},{6,4},{1,7},{3,1},{5,3},{7,5},{8,14},{10,8},{12,... | collective-permute-start | bytes 344072 | tf_op jit(solution)/shard_map/ppermute | solution.py:239
  49.6 1.9 %collective-permute-start.2 = (bf16[224,256]{1,0:T(8,128)(2,1)S(1)}, bf16[224,256]{1,0:T(8,128)(2,1)S(1)}, u32[]{:S(2)}, u32[]{:S(2)}) collective-permute-start(bf16[224,256]{1,0:T(8,128)(2,1)S(1)} %hold.1.refs_0_), channel_id=1, source_target_pairs={{0,2},{2,4},{4,6},{6,0},{1,3},{3,5},{5,7},{7,1},{8,10},{10,12},{12... | collective-permute-start | bytes 344072 | tf_op jit(solution)/shard_map/ppermute | solution.py:239
  51.6 2.0 %copy-done = bf16[256,7168]{1,0:T(8,128)(2,1)S(1)} copy-done((bf16[256,7168]{1,0:T(8,128)(2,1)S(1)}, bf16[256,7168]{1,0:T(8,128)(2,1)}, u32[]{:S(2)}) %copy-start) | copy-done | bytes 3670040
  53.6 3.2 %norm.1.rest_3_ = bf16[256,7168]{1,0:T(8,128)(2,1)} custom-call(bf16[256,7168]{1,0:T(8,128)(2,1)S(1)} %copy-done, f32[1,7168]{1,0:T(1,128)S(1)} %bitcast.16, f32[8,128]{1,0:T(8,128)S(1)} %get-tuple-element.24.after.refs_2_), custom_call_target="tpu_custom_call" | custom-call | bytes 4294967296 | tf_op jit(solution)/shard_map/norm/pallas_call | solution.py:134
  56.9 0.7 second_sum.1
  57.6 4.0 %collective-permute-start.5 = (bf16[256,7168]{1,0:T(8,128)(2,1)}, bf16[256,7168]{1,0:T(8,128)(2,1)}, u32[]{:S(2)}, u32[]{:S(2)}) collective-permute-start(bf16[256,7168]{1,0:T(8,128)(2,1)} %get-tuple-element.25.normed), channel_id=1, source_target_pairs={{0,8},{8,0},{1,9},{9,1},{2,10},{10,2},{3,11},{11,3},{4,12},{12,4},... | collective-permute-start | bytes 11010056 | tf_op jit(solution)/shard_map/ppermute | solution.py:286
  61.6 5.5 %collective-permute-start.7 = (bf16[4,224,256]{2,1,0:T(8,128)(2,1)S(1)}, bf16[4,224,256]{2,1,0:T(8,128)(2,1)S(1)}, u32[]{:S(2)}, u32[]{:S(2)}) collective-permute-start(bf16[4,224,256]{2,1,0:T(8,128)(2,1)S(1)} %lay.1.refs_0_.quad), channel_id=1, source_target_pairs={{0,16},{8,56},{16,0},{24,40},{32,48},{40,24},{48,32},{56,8},{1,17}... | collective-permute-start | bytes 1376264 | tf_op jit(solution)/shard_map/ppermute | solution.py:232
  67.2 4.4 %all-to-all-start.2 = ((f32[32,8,128]{2,1,0:T(8,128)}), f32[32,8,128]{2,1,0:T(8,128)S(1)}, u32[]{:S(2)}, u32[]{:S(2)}) async-start(f32[32,8,128]{2,1,0:T(8,128)} %get-tuple-element.27), calls=%async_computation.2 | async-start | bytes 262144 | tf_op jit(solution)/shard_map/all_to_all | solution.py:281
  71.7 3.3 %collective-permute-start.6 = (bf16[2,896,256]{2,1,0:T(8,128)(2,1)S(1)}, bf16[2,896,256]{2,1,0:T(8,128)(2,1)}, u32[]{:S(2)}, u32[]{:S(2)}) collective-permute-start(bf16[2,896,256]{2,1,0:T(8,128)(2,1)S(1)} %pair.2.early), channel_id=1, source_target_pairs={{0,6},{8,10},{2,4},{10,8},{4,2},{12,14},{6,0},{14,12},{1,7},{9,11}... | collective-permute-start | bytes 2752520 | tf_op jit(solution)/shard_map/ppermute | solution.py:232
  75.0 4.3 %all-to-all-done.2.parts = f32[32,8,128]{2,1,0:T(8,128)S(1)} async-done(((f32[32,8,128]{2,1,0:T(8,128)}), f32[32,8,128]{2,1,0:T(8,128)S(1)}, u32[]{:S(2)}, u32[]{:S(2)}) %all-to-all-start.2) | async-done | bytes 131104 | tf_op jit(solution)/shard_map/all_to_all | solution.py:281
  79.2 0.7 spread_sum.1
  80.0 2.3 %collective-permute-start.8 = (bf16[2,4,224,256]{3,2,1,0:T(8,128)(2,1)S(1)}, bf16[2,4,224,256]{3,2,1,0:T(8,128)(2,1)}, u32[]{:S(2)}, u32[]{:S(2)}) collective-permute-start(bf16[2,4,224,256]{3,2,1,0:T(8,128)(2,1)S(1)} %pair.3), channel_id=1, source_target_pairs={{0,48},{8,24},{16,32},{24,8},{32,16},{40,56},{48,0},{56,40},{1,49}... | collective-permute-start | bytes 2752520 | tf_op jit(solution)/shard_map/ppermute | solution.py:232
  82.3 9.7 %all-to-all-start.3 = ((f32[16,8,128]{2,1,0:T(8,128)}), f32[16,8,128]{2,1,0:T(8,128)S(1)}, u32[]{:S(2)}, u32[]{:S(2)}) async-start(f32[16,8,128]{2,1,0:T(8,128)} %get-tuple-element.31), calls=%async_computation.3 | async-start | bytes 131072 | tf_op jit(solution)/shard_map/all_to_all | solution.py:290
  92.1 0.1 stack.56.order
  92.2 2.3 %collective-permute-done.8.quad_late = bf16[2,4,224,256]{3,2,1,0:T(8,128)(2,1)} collective-permute-done((bf16[2,4,224,256]{3,2,1,0:T(8,128)(2,1)S(1)}, bf16[2,4,224,256]{3,2,1,0:T(8,128)(2,1)}, u32[]{:S(2)}, u32[]{:S(2)}) %collective-permute-start.8) | collective-permute-done | bytes 917536 | tf_op jit(solution)/shard_map/ppermute | solution.py:232
  94.5 7.7 %project.1 = (bf16[256,256]{1,0:T(8,128)(2,1)S(1)}, bf16[256,256]{1,0:T(8,128)(2,1)S(1)}) custom-call(s32[12]{0:T(128)S(1)} %stack.56.order, bf16[256,7168]{1,0:T(8,128)(2,1)} %get-tuple-element.25.normed, bf16[256,7168]{1,0:T(8,128)(2,1)} %collective-permute-done.5.far_normed, bf16[2,896,256]{2,1,0:T(8,128)(2,1)S(1)} %pair.2.early, ...), custom_call_target="tpu_custom_call" | custom-call | bytes 4294967296 | tf_op jit(solution)/shard_map/project/pallas_call | solution.py:184
  102.2 4.4 %collective-permute-start.9 = (bf16[256,256]{1,0:T(8,128)(2,1)S(1)}, bf16[256,256]{1,0:T(8,128)(2,1)S(1)}, u32[]{:S(2)}, u32[]{:S(2)}) collective-permute-start(bf16[256,256]{1,0:T(8,128)(2,1)S(1)} %get-tuple-element.30), channel_id=1, source_target_pairs={{0,8},{8,0},{1,9},{9,1},{2,10},{10,2},{3,11},{11,3},{4,12},{12,4},... | collective-permute-start | bytes 393224 | tf_op jit(solution)/shard_map/ppermute | solution.py:294
  106.6 0.7 update.1
  107.4 0.2 collective-permute-done.9.far
  107.6 0.7 join.1
  (23 shorter events, 0.2 us)
Async XLA Ops:
  0.6 1.2 %copy-start.1 = (bf16[1,896,512]{2,1,0:T(8,128)(2,1)S(1)}, bf16[1,896,512]{2,1,0:T(8,128)(2,1)}, u32[]{:S(2)}) copy-start(bf16[1,896,512]{2,1,0:T(8,128)(2,1)} %param.9) | copy-start | bytes 2752516
  1.8 49.7 %copy-start.5 = (f32[7168]{0:T(1024)S(1)}, f32[7168]{0:T(1024)}, u32[]{:S(2)}) copy-start(f32[7168]{0:T(1024)} %param.7) | copy-start | bytes 86020
  3.1 33.2 %all-to-all-start = ((bf16[8,112,512]{2,1,0:T(8,128)(2,1)}), bf16[8,112,512]{2,1,0:T(8,128)(2,1)S(1)}, u32[]{:S(2)}, u32[]{:S(2)}) async-start(bf16[8,112,512]{2,1,0:T(8,128)(2,1)} %get-tuple-element.19), calls=%async_computation | async-start | bytes 1835008 | tf_op jit(solution)/shard_map/all_to_all | solution.py:262
  13.5 1.2 %copy-start.2 = (bf16[896,512]{1,0:T(8,128)(2,1)S(1)}, bf16[896,512]{1,0:T(8,128)(2,1)}, u32[]{:S(2)}) copy-start(bf16[896,512]{1,0:T(8,128)(2,1)} %weight.1) | copy-start | bytes 2752516
  15.3 21.0 %collective-permute-start.1 = (bf16[896,256]{1,0:T(8,128)(2,1)S(1)}, bf16[896,256]{1,0:T(8,128)(2,1)S(1)}, u32[]{:S(2)}, u32[]{:S(2)}) collective-permute-start(bf16[896,256]{1,0:T(8,128)(2,1)S(1)} %get-tuple-element.22.refs_0_), channel_id=1, source_target_pairs={{0,2},{8,14},{2,0},{10,12},{4,6},{12,10},{6,4},{14,8},{1,3},{9,15}... | collective-permute-start | bytes 1376264 | tf_op jit(solution)/shard_map/ppermute | solution.py:232
  17.2 19.1 %collective-permute-start = (bf16[224,256]{1,0:T(8,128)(2,1)S(1)}, bf16[224,256]{1,0:T(8,128)(2,1)S(1)}, u32[]{:S(2)}, u32[]{:S(2)}) collective-permute-start(bf16[224,256]{1,0:T(8,128)(2,1)S(1)} %get-tuple-element.21), channel_id=1, source_target_pairs={{0,449},{1,448},{64,385},{65,384},{128,321},{129,320},{192,257},{1... | collective-permute-start | bytes 344072 | tf_op jit(solution)/shard_map/ppermute | solution.py:264
  37.2 19.6 %all-to-all-start.1 = ((f32[8,56,128]{2,1,0:T(8,128)}), f32[8,56,128]{2,1,0:T(8,128)S(1)}, u32[]{:S(2)}, u32[]{:S(2)}) async-start(f32[8,56,128]{2,1,0:T(8,128)} %get-tuple-element.23), calls=%async_computation.1 | async-start | bytes 458752 | tf_op jit(solution)/shard_map/all_to_all | solution.py:270
  43.2 13.6 %collective-permute-start.4 = (bf16[224,256]{1,0:T(8,128)(2,1)S(1)}, bf16[224,256]{1,0:T(8,128)(2,1)S(1)}, u32[]{:S(2)}, u32[]{:S(2)}) collective-permute-start(bf16[224,256]{1,0:T(8,128)(2,1)S(1)} %hold.1.refs_0_), channel_id=1, source_target_pairs={{0,4},{2,6},{4,0},{6,2},{1,5},{3,7},{5,1},{7,3},{8,12},{10,14},{12... | collective-permute-start | bytes 344072 | tf_op jit(solution)/shard_map/ppermute | solution.py:239
  46.1 10.8 %collective-permute-start.3 = (bf16[224,256]{1,0:T(8,128)(2,1)S(1)}, bf16[224,256]{1,0:T(8,128)(2,1)S(1)}, u32[]{:S(2)}, u32[]{:S(2)}) collective-permute-start(bf16[224,256]{1,0:T(8,128)(2,1)S(1)} %hold.1.refs_0_), channel_id=1, source_target_pairs={{0,6},{2,0},{4,2},{6,4},{1,7},{3,1},{5,3},{7,5},{8,14},{10,8},{12,... | collective-permute-start | bytes 344072 | tf_op jit(solution)/shard_map/ppermute | solution.py:239
  49.6 7.2 %collective-permute-start.2 = (bf16[224,256]{1,0:T(8,128)(2,1)S(1)}, bf16[224,256]{1,0:T(8,128)(2,1)S(1)}, u32[]{:S(2)}, u32[]{:S(2)}) collective-permute-start(bf16[224,256]{1,0:T(8,128)(2,1)S(1)} %hold.1.refs_0_), channel_id=1, source_target_pairs={{0,2},{2,4},{4,6},{6,0},{1,3},{3,5},{5,7},{7,1},{8,10},{10,12},{12... | collective-permute-start | bytes 344072 | tf_op jit(solution)/shard_map/ppermute | solution.py:239
  51.6 2.0 %copy-start = (bf16[256,7168]{1,0:T(8,128)(2,1)S(1)}, bf16[256,7168]{1,0:T(8,128)(2,1)}, u32[]{:S(2)}) copy-start(bf16[256,7168]{1,0:T(8,128)(2,1)} %hidden.1) | copy-start | bytes 11010052
  53.6 3.3 %copy-start.3 = (f32[14,512]{1,0:T(8,128)S(1)}, f32[14,512]{1,0:T(8,128)}, u32[]{:S(2)}) copy-start(f32[14,512]{1,0:T(8,128)} %outer.3) | copy-start | bytes 86020
  57.6 36.9 %collective-permute-start.5 = (bf16[256,7168]{1,0:T(8,128)(2,1)}, bf16[256,7168]{1,0:T(8,128)(2,1)}, u32[]{:S(2)}, u32[]{:S(2)}) collective-permute-start(bf16[256,7168]{1,0:T(8,128)(2,1)} %get-tuple-element.25.normed), channel_id=1, source_target_pairs={{0,8},{8,0},{1,9},{9,1},{2,10},{10,2},{3,11},{11,3},{4,12},{12,4},... | collective-permute-start | bytes 11010056 | tf_op jit(solution)/shard_map/ppermute | solution.py:286
  61.6 17.6 %collective-permute-start.7 = (bf16[4,224,256]{2,1,0:T(8,128)(2,1)S(1)}, bf16[4,224,256]{2,1,0:T(8,128)(2,1)S(1)}, u32[]{:S(2)}, u32[]{:S(2)}) collective-permute-start(bf16[4,224,256]{2,1,0:T(8,128)(2,1)S(1)} %lay.1.refs_0_.quad), channel_id=1, source_target_pairs={{0,16},{8,56},{16,0},{24,40},{32,48},{40,24},{48,32},{56,8},{1,17}... | collective-permute-start | bytes 1376264 | tf_op jit(solution)/shard_map/ppermute | solution.py:232
  67.2 12.1 %all-to-all-start.2 = ((f32[32,8,128]{2,1,0:T(8,128)}), f32[32,8,128]{2,1,0:T(8,128)S(1)}, u32[]{:S(2)}, u32[]{:S(2)}) async-start(f32[32,8,128]{2,1,0:T(8,128)} %get-tuple-element.27), calls=%async_computation.2 | async-start | bytes 262144 | tf_op jit(solution)/shard_map/all_to_all | solution.py:281
  71.7 20.5 %collective-permute-start.6 = (bf16[2,896,256]{2,1,0:T(8,128)(2,1)S(1)}, bf16[2,896,256]{2,1,0:T(8,128)(2,1)}, u32[]{:S(2)}, u32[]{:S(2)}) collective-permute-start(bf16[2,896,256]{2,1,0:T(8,128)(2,1)S(1)} %pair.2.early), channel_id=1, source_target_pairs={{0,6},{8,10},{2,4},{10,8},{4,2},{12,14},{6,0},{14,12},{1,7},{9,11}... | collective-permute-start | bytes 2752520 | tf_op jit(solution)/shard_map/ppermute | solution.py:232
  80.0 14.5 %collective-permute-start.8 = (bf16[2,4,224,256]{3,2,1,0:T(8,128)(2,1)S(1)}, bf16[2,4,224,256]{3,2,1,0:T(8,128)(2,1)}, u32[]{:S(2)}, u32[]{:S(2)}) collective-permute-start(bf16[2,4,224,256]{3,2,1,0:T(8,128)(2,1)S(1)} %pair.3), channel_id=1, source_target_pairs={{0,48},{8,24},{16,32},{24,8},{32,16},{40,56},{48,0},{56,40},{1,49}... | collective-permute-start | bytes 2752520 | tf_op jit(solution)/shard_map/ppermute | solution.py:232
  82.3 24.4 %all-to-all-start.3 = ((f32[16,8,128]{2,1,0:T(8,128)}), f32[16,8,128]{2,1,0:T(8,128)S(1)}, u32[]{:S(2)}, u32[]{:S(2)}) async-start(f32[16,8,128]{2,1,0:T(8,128)} %get-tuple-element.31), calls=%async_computation.3 | async-start | bytes 131072 | tf_op jit(solution)/shard_map/all_to_all | solution.py:290
  92.2 14.5 %copy-start.4 = (f32[14,512]{1,0:T(8,128)S(1)}, f32[14,512]{1,0:T(8,128)}, u32[]{:S(2)}) copy-start(f32[14,512]{1,0:T(8,128)} %momentum.1) | copy-start | bytes 86020
  102.2 5.4 %collective-permute-start.9 = (bf16[256,256]{1,0:T(8,128)(2,1)S(1)}, bf16[256,256]{1,0:T(8,128)(2,1)S(1)}, u32[]{:S(2)}, u32[]{:S(2)}) collective-permute-start(bf16[256,256]{1,0:T(8,128)(2,1)S(1)} %get-tuple-element.30), channel_id=1, source_target_pairs={{0,8},{8,0},{1,9},{9,1},{2,10},{10,2},{3,11},{11,3},{4,12},{12,4},... | collective-permute-start | bytes 393224 | tf_op jit(solution)/shard_map/ppermute | solution.py:294

commit v5 on v3

--- a/solution.py
+++ b/solution.py
@@ -41,7 +41,7 @@
         body,
         name=name,
         out_shape=out,
-        in_specs=[first] + [VMEM] * (len(args) - 1) + [anywhere] * len(after),
+        in_specs=[first] + [VMEM] * (len(args) - 1 + len(after) - len(aliases)) + [anywhere] * len(aliases),
         out_specs=out_specs,
         scratch_shapes=list(scratch),
         input_output_aliases=aliases,
@@ -150,26 +150,54 @@
 DOT = functools.partial(jnp.dot, preferred_element_type=F32)
 
 
-def blocks(tokens, weights, order, first):
-    cols = lambda k: pl.ds(pl.multiple_of(order[first + k] * ROWS, ROWS), ROWS)
-    return functools.reduce(lambda a, b: a + b, [DOT(tokens[:, cols(k)], w[...]) for k, w in enumerate(weights)])
-
-
-def project_own_body(order, near_in, far_in, early, late, after, near, far):
-    parts = [early.at[0], early.at[1], late.at[0], late.at[1]]
-    near[...] = blocks(near_in, parts, order, 0)
-    far[...] = blocks(far_in, parts, order, 0)
-
-
-def project_other_body(order, near_in, far_in, quad, quad_next, quad_late, near_own, far_own, near, far, weights):
-    rows = quad.shape[1]
+def blocks(tokens, weights):
+    return functools.reduce(lambda a, b: a + b, [DOT(tokens[k], w[...]) for k, w in enumerate(weights)])
+
+
+def project_own_body(order, normed, far_normed, early, late, token, sums, kept, held, arrived):
+    count = normed.shape[0]
+    copies = [
+        pltpu.make_async_copy(
+            tokens.at[:, pl.ds(pl.multiple_of(order[k] * ROWS, ROWS), ROWS)],
+            (held if k < 4 else kept).at[k % 4, pl.ds(t * count, count)],
+            arrived.at[t, k],
+        )
+        for k in range(8)
+        for t, tokens in enumerate((normed, far_normed))
+    ]
+    for copy in copies:
+        copy.start()
+    for copy in copies[:8]:
+        copy.wait()
+    sums[...] = blocks(held, [early.at[0], early.at[1], late.at[0], late.at[1]])
+    for copy in copies[8:]:
+        copy.wait()
+
+
+def project_own(order, normed, far_normed, early, late, token):
+    count, cols = 2 * normed.shape[0], early.shape[2]
+    anywhere = pl.BlockSpec(memory_space=pl.ANY)
+    return pl.pallas_call(
+        project_own_body,
+        name="project_own",
+        out_shape=(jax.ShapeDtypeStruct((count, cols), F32), jax.ShapeDtypeStruct((4, count, ROWS), BF16)),
+        in_specs=[pl.BlockSpec(memory_space=pltpu.SMEM), anywhere, anywhere] + [VMEM] * 3,
+        out_specs=(VMEM, VMEM),
+        scratch_shapes=[pltpu.VMEM((4, count, ROWS), BF16), pltpu.SemaphoreType.DMA((2, 8))],
+        compiler_params=PARAMS,
+        cost_estimate=LONG,
+    )(order, normed, far_normed, early, late, token)
+
+
+def project_other_body(order, kept, quad, quad_next, quad_late, sums, near, far, weights):
+    rows, count = quad.shape[1], near.shape[0]
     for k in range(4):
         place = pl.ds(pl.multiple_of(order[8 + k] * rows, rows), rows)
         for j in range(4):
             weights[j, place, :] = (quad[j], quad_next[j], quad_late[0, j], quad_late[1, j])[k]
-    parts = [weights.at[j] for j in range(4)]
-    near[...] = (near_own[...] + blocks(near_in, parts, order, 4)).astype(BF16)
-    far[...] = (far_own[...] + blocks(far_in, parts, order, 4)).astype(BF16)
+    total = sums[...] + blocks(kept, [weights.at[j] for j in range(4)])
+    near[...] = total[:count].astype(BF16)
+    far[...] = total[count:].astype(BF16)
 
 
 def join_body(core, near, far, out):
@@ -258,20 +286,16 @@
     quad = call(lay_body, "lay", (array(BF16, 4, rows // 4, cols),), others, (token,), cost=LONG)[0]
     quad_next = exchange(quad, "x", False)
     far_normed = lax.ppermute(normed, "core", swap)
-    tokens = normed.shape[0]
     squares, token = call(
         spread_sum_body, "spread_sum", (array(F32, 16, 8, LANES), TOKEN), (squares,), (quad_next,)
     )
     squares = lax.all_to_all(squares, ("z_lo", "z_hi"), 0, 0)
     quads = call(lay_body, "pair", (array(BF16, 2, 4, rows // 4, cols),), (quad, quad_next), (token,))[0]
     quad_late = exchange(quads, "x", True)
+    sums, kept = project_own(order, normed, far_normed, early, late, token)
     near, far = call(
-        project_own_body, "project_own", (array(F32, tokens, cols),) * 2, (order, normed, far_normed, early, late), (token,),
-        first=scalars, cost=LONG,
-    )
-    near, far = call(
-        project_other_body, "project_other", (array(BF16, tokens, cols),) * 2,
-        (order, normed, far_normed, quad, quad_next, quad_late, near, far),
+        project_other_body, "project_other", (array(BF16, normed.shape[0], cols),) * 2,
+        (order, kept, quad, quad_next, quad_late, sums),
         first=scalars, scratch=[pltpu.VMEM((4, rows, cols), BF16)], cost=LONG,
     )
     far = lax.ppermute(far, "core", swap)

time: 109 us -> 108 us (level)
  Pallas kernels: 19.2 us -> 16.5 us
  waiting for transfers between devices: 14.4 us -> 16.1 us
    pallas_call x12 -> x11, Pallas kernels: 15.2 us -> 8.63 us  [call(): pl.pallas_call(body, name=name, out_shape=out, in_specs=[first] + [VMEM]...]
    pallas_call x0 -> x1, Pallas kernels: none -> 3.94 us  [project_own(): pl.pallas_call(project_own_body, name='project_own', out_shape=(jax.Shape...]
    all_to_all x1, waiting for transfers between devices: 0.01 us -> 1.87 us  [on_device(): squares = lax.all_to_all(squares, ('z_lo', 'z_hi'), 0, 0)]
  transfers between devices with their start and end apart: 14 -> 14, of which waited for: 4 -> 4; matrix products, arithmetic and copies ran while one was open for 0% -> 0% of each run, Pallas kernels for 14% -> 12%
where the time goes in v5:
time: 108 us; the launch traced here: 107 us
  starting transfers between devices  68.7 us (64%)
  Pallas kernels  16.5 us (15%)
  waiting for transfers between devices  16.1 us (15%)
  local copies, waits for them, and re-layouts  4.49 us (4%)
    ppermute x4, starting transfers between devices, exchange(): return lax.ppermute(array, names, pairs)  13 us
    all_to_all x1, starting transfers between devices, on_device(): grouped = lax.all_to_all(grouped, ('x', 'core'), 0, 0)  10.3 us
    ppermute x1, waiting for transfers between devices, on_device(): other = lax.ppermute(mine, ('z_lo', 'z_hi'), mirror)  9.8 us
    all_to_all x1, starting transfers between devices, on_device(): squares = lax.all_to_all(squares, ('z_lo', 'z_hi'), 0, 0)  9.74 us
    ppermute x1, starting transfers between devices, on_device(): other = lax.ppermute(mine, ('z_lo', 'z_hi'), mirror)  9.31 us
    pallas_call x11, Pallas kernels, call(): pl.pallas_call(body, name=name, out_shape=out, in_specs=[first] + [VMEM]...  8.63 us
    ppermute x3, starting transfers between devices, spread(): lax.ppermute(array, axis, [(i, (i + s) % 4) for i in range(4)])  8.41 us
    all_to_all x1, starting transfers between devices, on_device(): pieces = lax.all_to_all(pieces, 'z_lo', 0, 0)  5.98 us
  transfers between devices with their start and end apart: 14, of which 4 were waited for; matrix products, arithmetic and copies ran while one was open for 0% of the time, Pallas kernels for 12%

profile of v5, /device:TPU:1, one launch (start us, length us, event | category | flops | bytes accessed | tf_op | source)
XLA Modules:
  0.0 106.7 jit_solution(6188560921071920362)
XLA Ops:
  0.6 1.2 %copy-done.1 = bf16[1,896,512]{2,1,0:T(8,128)(2,1)S(1)} copy-done((bf16[1,896,512]{2,1,0:T(8,128)(2,1)S(1)}, bf16[1,896,512]{2,1,0:T(8,128)(2,1)}, u32[]{:S(2)}) %copy-start.1) | copy-done | bytes 917528
  1.8 1.3 %regroup.1 = (bf16[8,112,512]{2,1,0:T(8,128)(2,1)}, f32[8,128]{1,0:T(8,128)S(1)}) custom-call(bf16[896,512]{1,0:T(8,128)(2,1)S(1)} %bitcast.15), custom_call_target="tpu_custom_call" | custom-call | tf_op jit(solution)/shard_map/regroup/pallas_call | solution.py:40
  3.1 10.3 %all-to-all-start = ((bf16[8,112,512]{2,1,0:T(8,128)(2,1)}), bf16[8,112,512]{2,1,0:T(8,128)(2,1)S(1)}, u32[]{:S(2)}, u32[]{:S(2)}) async-start(bf16[8,112,512]{2,1,0:T(8,128)(2,1)} %get-tuple-element.21), calls=%async_computation | async-start | bytes 1835008 | tf_op jit(solution)/shard_map/all_to_all | solution.py:264
  13.5 1.2 %copy-done.2 = bf16[896,512]{1,0:T(8,128)(2,1)S(1)} copy-done((bf16[896,512]{1,0:T(8,128)(2,1)S(1)}, bf16[896,512]{1,0:T(8,128)(2,1)}, u32[]{:S(2)}) %copy-start.2) | copy-done | bytes 917528
  14.7 0.6 cut.1
  15.3 1.9 %collective-permute-start.1 = (bf16[896,256]{1,0:T(8,128)(2,1)S(1)}, bf16[896,256]{1,0:T(8,128)(2,1)S(1)}, u32[]{:S(2)}, u32[]{:S(2)}) collective-permute-start(bf16[896,256]{1,0:T(8,128)(2,1)S(1)} %get-tuple-element.24.refs_0_), channel_id=1, source_target_pairs={{0,2},{8,14},{2,0},{10,12},{4,6},{12,10},{6,4},{14,8},{1,3},{9,15}... | collective-permute-start | bytes 1376264 | tf_op jit(solution)/shard_map/ppermute | solution.py:234
  17.2 9.3 %collective-permute-start = (bf16[224,256]{1,0:T(8,128)(2,1)S(1)}, bf16[224,256]{1,0:T(8,128)(2,1)S(1)}, u32[]{:S(2)}, u32[]{:S(2)}) collective-permute-start(bf16[224,256]{1,0:T(8,128)(2,1)S(1)} %get-tuple-element.23), channel_id=1, source_target_pairs={{0,449},{1,448},{64,385},{65,384},{128,321},{129,320},{192,257},{1... | collective-permute-start | bytes 344072 | tf_op jit(solution)/shard_map/ppermute | solution.py:266
  26.5 9.8 %collective-permute-done.rest_0_.given = bf16[224,256]{1,0:T(8,128)(2,1)S(1)} collective-permute-done((bf16[224,256]{1,0:T(8,128)(2,1)S(1)}, bf16[224,256]{1,0:T(8,128)(2,1)S(1)}, u32[]{:S(2)}, u32[]{:S(2)}) %collective-permute-start) | collective-permute-done | bytes 114720 | tf_op jit(solution)/shard_map/ppermute | solution.py:266
  36.3 0.9 first_sum.1
  37.2 6.0 %all-to-all-start.1 = ((f32[8,56,128]{2,1,0:T(8,128)}), f32[8,56,128]{2,1,0:T(8,128)S(1)}, u32[]{:S(2)}, u32[]{:S(2)}) async-start(f32[8,56,128]{2,1,0:T(8,128)} %get-tuple-element.25), calls=%async_computation.1 | async-start | bytes 458752 | tf_op jit(solution)/shard_map/all_to_all | solution.py:272
  43.2 2.1 %collective-permute-start.2 = (bf16[224,256]{1,0:T(8,128)(2,1)S(1)}, bf16[224,256]{1,0:T(8,128)(2,1)S(1)}, u32[]{:S(2)}, u32[]{:S(2)}) collective-permute-start(bf16[224,256]{1,0:T(8,128)(2,1)S(1)} %hold.1.refs_0_), channel_id=1, source_target_pairs={{0,2},{2,4},{4,6},{6,0},{1,3},{3,5},{5,7},{7,1},{8,10},{10,12},{12... | collective-permute-start | bytes 344072 | tf_op jit(solution)/shard_map/ppermute | solution.py:241
  45.3 4.4 %collective-permute-start.3 = (bf16[224,256]{1,0:T(8,128)(2,1)S(1)}, bf16[224,256]{1,0:T(8,128)(2,1)S(1)}, u32[]{:S(2)}, u32[]{:S(2)}) collective-permute-start(bf16[224,256]{1,0:T(8,128)(2,1)S(1)} %hold.1.refs_0_), channel_id=1, source_target_pairs={{0,6},{2,0},{4,2},{6,4},{1,7},{3,1},{5,3},{7,5},{8,14},{10,8},{12,... | collective-permute-start | bytes 344072 | tf_op jit(solution)/shard_map/ppermute | solution.py:241
  49.7 1.9 %collective-permute-start.4 = (bf16[224,256]{1,0:T(8,128)(2,1)S(1)}, bf16[224,256]{1,0:T(8,128)(2,1)S(1)}, u32[]{:S(2)}, u32[]{:S(2)}) collective-permute-start(bf16[224,256]{1,0:T(8,128)(2,1)S(1)} %hold.1.refs_0_), channel_id=1, source_target_pairs={{0,4},{2,6},{4,0},{6,2},{1,5},{3,7},{5,1},{7,3},{8,12},{10,14},{12... | collective-permute-start | bytes 344072 | tf_op jit(solution)/shard_map/ppermute | solution.py:241
  51.7 2.0 %copy-done = bf16[256,7168]{1,0:T(8,128)(2,1)S(1)} copy-done((bf16[256,7168]{1,0:T(8,128)(2,1)S(1)}, bf16[256,7168]{1,0:T(8,128)(2,1)}, u32[]{:S(2)}) %copy-start) | copy-done | bytes 3670040
  53.7 3.2 %norm.1.rest_3_ = bf16[256,7168]{1,0:T(8,128)(2,1)} custom-call(bf16[256,7168]{1,0:T(8,128)(2,1)S(1)} %copy-done, f32[1,7168]{1,0:T(1,128)S(1)} %bitcast.16, f32[8,128]{1,0:T(8,128)S(1)} %get-tuple-element.26.after.refs_2_), custom_call_target="tpu_custom_call" | custom-call | bytes 4294967296 | tf_op jit(solution)/shard_map/norm/pallas_call | solution.py:134
  57.0 0.1 collective-permute-done.4.rest_2_.refs_3_
  57.1 0.7 second_sum.1
  57.8 3.8 %collective-permute-start.5 = (bf16[256,7168]{1,0:T(8,128)(2,1)}, bf16[256,7168]{1,0:T(8,128)(2,1)}, u32[]{:S(2)}, u32[]{:S(2)}) collective-permute-start(bf16[256,7168]{1,0:T(8,128)(2,1)} %get-tuple-element.27.normed), channel_id=1, source_target_pairs={{0,8},{8,0},{1,9},{9,1},{2,10},{10,2},{3,11},{11,3},{4,12},{12,4},... | collective-permute-start | bytes 11010056 | tf_op jit(solution)/shard_map/ppermute | solution.py:288
  61.6 5.5 %collective-permute-start.7 = (bf16[4,224,256]{2,1,0:T(8,128)(2,1)S(1)}, bf16[4,224,256]{2,1,0:T(8,128)(2,1)S(1)}, u32[]{:S(2)}, u32[]{:S(2)}) collective-permute-start(bf16[4,224,256]{2,1,0:T(8,128)(2,1)S(1)} %lay.1.refs_0_.quad), channel_id=1, source_target_pairs={{0,16},{8,56},{16,0},{24,40},{32,48},{40,24},{48,32},{56,8},{1,17}... | collective-permute-start | bytes 1376264 | tf_op jit(solution)/shard_map/ppermute | solution.py:234
  67.1 4.6 %all-to-all-start.2 = ((f32[32,8,128]{2,1,0:T(8,128)}), f32[32,8,128]{2,1,0:T(8,128)S(1)}, u32[]{:S(2)}, u32[]{:S(2)}) async-start(f32[32,8,128]{2,1,0:T(8,128)} %get-tuple-element.28), calls=%async_computation.2 | async-start | bytes 262144 | tf_op jit(solution)/shard_map/all_to_all | solution.py:283
  71.8 3.3 %collective-permute-start.6 = (bf16[2,896,256]{2,1,0:T(8,128)(2,1)S(1)}, bf16[2,896,256]{2,1,0:T(8,128)(2,1)S(1)}, u32[]{:S(2)}, u32[]{:S(2)}) collective-permute-start(bf16[2,896,256]{2,1,0:T(8,128)(2,1)S(1)} %pair.2.early), channel_id=1, source_target_pairs={{0,6},{8,10},{2,4},{10,8},{4,2},{12,14},{6,0},{14,12},{1,7},{9,11}... | collective-permute-start | bytes 2752520 | tf_op jit(solution)/shard_map/ppermute | solution.py:234
  75.1 4.3 %all-to-all-done.2.parts = f32[32,8,128]{2,1,0:T(8,128)S(1)} async-done(((f32[32,8,128]{2,1,0:T(8,128)}), f32[32,8,128]{2,1,0:T(8,128)S(1)}, u32[]{:S(2)}, u32[]{:S(2)}) %all-to-all-start.2) | async-done | bytes 131104 | tf_op jit(solution)/shard_map/all_to_all | solution.py:283
  79.4 0.7 spread_sum.1
  80.1 1.1 %pair.3 = bf16[2,4,224,256]{3,2,1,0:T(8,128)(2,1)} custom-call(bf16[4,224,256]{2,1,0:T(8,128)(2,1)S(1)} %lay.1.refs_0_.quad, bf16[4,224,256]{2,1,0:T(8,128)(2,1)S(1)} %collective-permute-done.7.rest_0_.refs_1_.quad_next, f32[8,128]{1,0:T(8,128)S(1)} %get-tuple-element.30.token.refs_2_), custom_call_target="tpu_custom_call" | custom-call | tf_op jit(solution)/shard_map/pair/pallas_call | solution.py:40
  81.1 2.3 %collective-permute-start.8 = (bf16[2,4,224,256]{3,2,1,0:T(8,128)(2,1)}, bf16[2,4,224,256]{3,2,1,0:T(8,128)(2,1)}, u32[]{:S(2)}, u32[]{:S(2)}) collective-permute-start(bf16[2,4,224,256]{3,2,1,0:T(8,128)(2,1)} %pair.3), channel_id=1, source_target_pairs={{0,48},{8,24},{16,32},{24,8},{32,16},{40,56},{48,0},{56,40},{1,49}... | collective-permute-start | bytes 2752520 | tf_op jit(solution)/shard_map/ppermute | solution.py:234
  83.4 9.7 %all-to-all-start.3 = ((f32[16,8,128]{2,1,0:T(8,128)}), f32[16,8,128]{2,1,0:T(8,128)S(1)}, u32[]{:S(2)}, u32[]{:S(2)}) async-start(f32[16,8,128]{2,1,0:T(8,128)} %get-tuple-element.35), calls=%async_computation.3 | async-start | bytes 131072 | tf_op jit(solution)/shard_map/all_to_all | solution.py:292
  93.4 3.9 %project_own.1 = (f32[512,256]{1,0:T(8,128)S(1)}, bf16[4,512,896]{2,1,0:T(8,128)(2,1)S(1)}) custom-call(s32[12]{0:T(128)S(1)} %stack.56.order, bf16[256,7168]{1,0:T(8,128)(2,1)} %get-tuple-element.27.normed, bf16[256,7168]{1,0:T(8,128)(2,1)} %collective-permute-done.5.far_normed, bf16[2,896,256]{2,1,0:T(8,128)(2,1)S(1)} %pair.2.early, ...), custom_call_target="tpu_custom_call" | custom-call | bytes 4294967296 | tf_op jit(solution)/shard_map/project_own/pallas_call | solution.py:180
  97.3 2.6 %project_other.1 = (bf16[256,256]{1,0:T(8,128)(2,1)S(1)}, bf16[256,256]{1,0:T(8,128)(2,1)S(1)}) custom-call(s32[12]{0:T(128)S(1)} %stack.56.order, bf16[4,512,896]{2,1,0:T(8,128)(2,1)S(1)} %get-tuple-element.31.kept, bf16[4,224,256]{2,1,0:T(8,128)(2,1)S(1)} %lay.1.refs_0_.quad, bf16[4,224,256]{2,1,0:T(8,128)(2,1)S(1)} %collective-permute-done.7.rest_0_.refs_1_.quad_next, ...), custom_call_target="tpu_custom_call" | custom-call | bytes 4294967296 | tf_op jit(solution)/shard_map/project_other/pallas_call | solution.py:40
  99.9 3.5 %collective-permute-start.9 = (bf16[256,256]{1,0:T(8,128)(2,1)S(1)}, bf16[256,256]{1,0:T(8,128)(2,1)S(1)}, u32[]{:S(2)}, u32[]{:S(2)}) collective-permute-start(bf16[256,256]{1,0:T(8,128)(2,1)S(1)} %get-tuple-element.34), channel_id=1, source_target_pairs={{0,8},{8,0},{1,9},{9,1},{2,10},{10,2},{3,11},{11,3},{4,12},{12,4},... | collective-permute-start | bytes 393224 | tf_op jit(solution)/shard_map/ppermute | solution.py:301
  103.4 1.9 %all-to-all-done.3.parts = f32[16,8,128]{2,1,0:T(8,128)S(1)} async-done(((f32[16,8,128]{2,1,0:T(8,128)}), f32[16,8,128]{2,1,0:T(8,128)S(1)}, u32[]{:S(2)}, u32[]{:S(2)}) %all-to-all-start.3) | async-done | bytes 65568 | tf_op jit(solution)/shard_map/all_to_all | solution.py:292
  105.3 0.7 update.1
  106.0 0.7 join.1
  (24 shorter events, 0.3 us)
Async XLA Ops:
  0.6 1.2 %copy-start.1 = (bf16[1,896,512]{2,1,0:T(8,128)(2,1)S(1)}, bf16[1,896,512]{2,1,0:T(8,128)(2,1)}, u32[]{:S(2)}) copy-start(bf16[1,896,512]{2,1,0:T(8,128)(2,1)} %param.9) | copy-start | bytes 2752516
  1.8 49.8 %copy-start.5 = (f32[7168]{0:T(1024)S(1)}, f32[7168]{0:T(1024)}, u32[]{:S(2)}) copy-start(f32[7168]{0:T(1024)} %param.7) | copy-start | bytes 86020
  3.1 33.2 %all-to-all-start = ((bf16[8,112,512]{2,1,0:T(8,128)(2,1)}), bf16[8,112,512]{2,1,0:T(8,128)(2,1)S(1)}, u32[]{:S(2)}, u32[]{:S(2)}) async-start(bf16[8,112,512]{2,1,0:T(8,128)(2,1)} %get-tuple-element.21), calls=%async_computation | async-start | bytes 1835008 | tf_op jit(solution)/shard_map/all_to_all | solution.py:264
  13.5 1.2 %copy-start.2 = (bf16[896,512]{1,0:T(8,128)(2,1)S(1)}, bf16[896,512]{1,0:T(8,128)(2,1)}, u32[]{:S(2)}) copy-start(bf16[896,512]{1,0:T(8,128)(2,1)} %weight.1) | copy-start | bytes 2752516
  15.3 21.0 %collective-permute-start.1 = (bf16[896,256]{1,0:T(8,128)(2,1)S(1)}, bf16[896,256]{1,0:T(8,128)(2,1)S(1)}, u32[]{:S(2)}, u32[]{:S(2)}) collective-permute-start(bf16[896,256]{1,0:T(8,128)(2,1)S(1)} %get-tuple-element.24.refs_0_), channel_id=1, source_target_pairs={{0,2},{8,14},{2,0},{10,12},{4,6},{12,10},{6,4},{14,8},{1,3},{9,15}... | collective-permute-start | bytes 1376264 | tf_op jit(solution)/shard_map/ppermute | solution.py:234
  17.2 19.1 %collective-permute-start = (bf16[224,256]{1,0:T(8,128)(2,1)S(1)}, bf16[224,256]{1,0:T(8,128)(2,1)S(1)}, u32[]{:S(2)}, u32[]{:S(2)}) collective-permute-start(bf16[224,256]{1,0:T(8,128)(2,1)S(1)} %get-tuple-element.23), channel_id=1, source_target_pairs={{0,449},{1,448},{64,385},{65,384},{128,321},{129,320},{192,257},{1... | collective-permute-start | bytes 344072 | tf_op jit(solution)/shard_map/ppermute | solution.py:266
  37.2 19.8 %all-to-all-start.1 = ((f32[8,56,128]{2,1,0:T(8,128)}), f32[8,56,128]{2,1,0:T(8,128)S(1)}, u32[]{:S(2)}, u32[]{:S(2)}) async-start(f32[8,56,128]{2,1,0:T(8,128)} %get-tuple-element.25), calls=%async_computation.1 | async-start | bytes 458752 | tf_op jit(solution)/shard_map/all_to_all | solution.py:272
  43.2 13.7 %collective-permute-start.2 = (bf16[224,256]{1,0:T(8,128)(2,1)S(1)}, bf16[224,256]{1,0:T(8,128)(2,1)S(1)}, u32[]{:S(2)}, u32[]{:S(2)}) collective-permute-start(bf16[224,256]{1,0:T(8,128)(2,1)S(1)} %hold.1.refs_0_), channel_id=1, source_target_pairs={{0,2},{2,4},{4,6},{6,0},{1,3},{3,5},{5,7},{7,1},{8,10},{10,12},{12... | collective-permute-start | bytes 344072 | tf_op jit(solution)/shard_map/ppermute | solution.py:241
  45.3 11.7 %collective-permute-start.3 = (bf16[224,256]{1,0:T(8,128)(2,1)S(1)}, bf16[224,256]{1,0:T(8,128)(2,1)S(1)}, u32[]{:S(2)}, u32[]{:S(2)}) collective-permute-start(bf16[224,256]{1,0:T(8,128)(2,1)S(1)} %hold.1.refs_0_), channel_id=1, source_target_pairs={{0,6},{2,0},{4,2},{6,4},{1,7},{3,1},{5,3},{7,5},{8,14},{10,8},{12,... | collective-permute-start | bytes 344072 | tf_op jit(solution)/shard_map/ppermute | solution.py:241
  49.7 7.3 %collective-permute-start.4 = (bf16[224,256]{1,0:T(8,128)(2,1)S(1)}, bf16[224,256]{1,0:T(8,128)(2,1)S(1)}, u32[]{:S(2)}, u32[]{:S(2)}) collective-permute-start(bf16[224,256]{1,0:T(8,128)(2,1)S(1)} %hold.1.refs_0_), channel_id=1, source_target_pairs={{0,4},{2,6},{4,0},{6,2},{1,5},{3,7},{5,1},{7,3},{8,12},{10,14},{12... | collective-permute-start | bytes 344072 | tf_op jit(solution)/shard_map/ppermute | solution.py:241
  51.7 2.0 %copy-start = (bf16[256,7168]{1,0:T(8,128)(2,1)S(1)}, bf16[256,7168]{1,0:T(8,128)(2,1)}, u32[]{:S(2)}) copy-start(bf16[256,7168]{1,0:T(8,128)(2,1)} %hidden.1) | copy-start | bytes 11010052
  53.7 3.4 %copy-start.3 = (f32[14,512]{1,0:T(8,128)S(1)}, f32[14,512]{1,0:T(8,128)}, u32[]{:S(2)}) copy-start(f32[14,512]{1,0:T(8,128)} %outer.3) | copy-start | bytes 86020
  57.8 35.6 %collective-permute-start.5 = (bf16[256,7168]{1,0:T(8,128)(2,1)}, bf16[256,7168]{1,0:T(8,128)(2,1)}, u32[]{:S(2)}, u32[]{:S(2)}) collective-permute-start(bf16[256,7168]{1,0:T(8,128)(2,1)} %get-tuple-element.27.normed), channel_id=1, source_target_pairs={{0,8},{8,0},{1,9},{9,1},{2,10},{10,2},{3,11},{11,3},{4,12},{12,4},... | collective-permute-start | bytes 11010056 | tf_op jit(solution)/shard_map/ppermute | solution.py:288
  61.6 17.8 %collective-permute-start.7 = (bf16[4,224,256]{2,1,0:T(8,128)(2,1)S(1)}, bf16[4,224,256]{2,1,0:T(8,128)(2,1)S(1)}, u32[]{:S(2)}, u32[]{:S(2)}) collective-permute-start(bf16[4,224,256]{2,1,0:T(8,128)(2,1)S(1)} %lay.1.refs_0_.quad), channel_id=1, source_target_pairs={{0,16},{8,56},{16,0},{24,40},{32,48},{40,24},{48,32},{56,8},{1,17}... | collective-permute-start | bytes 1376264 | tf_op jit(solution)/shard_map/ppermute | solution.py:234
  67.1 12.2 %all-to-all-start.2 = ((f32[32,8,128]{2,1,0:T(8,128)}), f32[32,8,128]{2,1,0:T(8,128)S(1)}, u32[]{:S(2)}, u32[]{:S(2)}) async-start(f32[32,8,128]{2,1,0:T(8,128)} %get-tuple-element.28), calls=%async_computation.2 | async-start | bytes 262144 | tf_op jit(solution)/shard_map/all_to_all | solution.py:283
  71.8 21.5 %collective-permute-start.6 = (bf16[2,896,256]{2,1,0:T(8,128)(2,1)S(1)}, bf16[2,896,256]{2,1,0:T(8,128)(2,1)S(1)}, u32[]{:S(2)}, u32[]{:S(2)}) collective-permute-start(bf16[2,896,256]{2,1,0:T(8,128)(2,1)S(1)} %pair.2.early), channel_id=1, source_target_pairs={{0,6},{8,10},{2,4},{10,8},{4,2},{12,14},{6,0},{14,12},{1,7},{9,11}... | collective-permute-start | bytes 2752520 | tf_op jit(solution)/shard_map/ppermute | solution.py:234
  81.1 16.2 %collective-permute-start.8 = (bf16[2,4,224,256]{3,2,1,0:T(8,128)(2,1)}, bf16[2,4,224,256]{3,2,1,0:T(8,128)(2,1)}, u32[]{:S(2)}, u32[]{:S(2)}) collective-permute-start(bf16[2,4,224,256]{3,2,1,0:T(8,128)(2,1)} %pair.3), channel_id=1, source_target_pairs={{0,48},{8,24},{16,32},{24,8},{32,16},{40,56},{48,0},{56,40},{1,49}... | collective-permute-start | bytes 2752520 | tf_op jit(solution)/shard_map/ppermute | solution.py:234
  83.4 21.9 %all-to-all-start.3 = ((f32[16,8,128]{2,1,0:T(8,128)}), f32[16,8,128]{2,1,0:T(8,128)S(1)}, u32[]{:S(2)}, u32[]{:S(2)}) async-start(f32[16,8,128]{2,1,0:T(8,128)} %get-tuple-element.35), calls=%async_computation.3 | async-start | bytes 131072 | tf_op jit(solution)/shard_map/all_to_all | solution.py:292
  97.3 8.0 %copy-start.4 = (f32[14,512]{1,0:T(8,128)S(1)}, f32[14,512]{1,0:T(8,128)}, u32[]{:S(2)}) copy-start(f32[14,512]{1,0:T(8,128)} %momentum.1) | copy-start | bytes 86020
  99.9 6.1 %collective-permute-start.9 = (bf16[256,256]{1,0:T(8,128)(2,1)S(1)}, bf16[256,256]{1,0:T(8,128)(2,1)S(1)}, u32[]{:S(2)}, u32[]{:S(2)}) collective-permute-start(bf16[256,256]{1,0:T(8,128)(2,1)S(1)} %get-tuple-element.34), channel_id=1, source_target_pairs={{0,8},{8,0},{1,9},{9,1},{2,10},{10,2},{3,11},{11,3},{4,12},{12,4},... | collective-permute-start | bytes 393224 | tf_op jit(solution)/shard_map/ppermute | solution.py:301

commit v6 on v5

--- a/solution.py
+++ b/solution.py
@@ -50,7 +50,7 @@
     )(*args, *after)
 
 
-def regroup_body(src, out, token, wide, grouped):
+def regroup_body(src, after, out, token, wide, grouped):
     token[...] = jnp.zeros_like(token)
     wide[...] = src[...].astype(F32)
     for xc in range(8):
@@ -60,14 +60,14 @@
         out[xc] = grouped[xc].astype(BF16)
 
 
-def cut_body(place, weight, after, own, mine):
+def cut_body(place, weight, own, mine):
     rows, cols = mine.shape
     own[...] = weight[:, pl.ds(pl.multiple_of(place[0] * cols, cols), cols)]
     mine[...] = own[pl.ds(pl.multiple_of(place[1] * rows, rows), rows), :]
 
 
 def first_sum_body(parts, *rest):
-    out, token, total = rest[-3:]
+    out, token, through, total = rest[-4:]
     token[...] = jnp.zeros_like(token)
     total[...] = functools.reduce(lambda a, b: a + b, [parts[i].astype(F32) for i in range(8)])
     for z in range(8):
@@ -104,7 +104,7 @@
     out[...] = jnp.broadcast_to(jnp.sum(parts[...], axis=0, keepdims=True), out.shape)
 
 
-def update_body(parts, delta, outer, momentum, new_outer, new_momentum):
+def finish_body(core, parts, delta, outer, momentum, near, far, new_outer, new_momentum, projected):
     lanes = jnp.sum(parts[...], axis=0)[:1]
     length = jnp.sqrt(jnp.sum(lanes, axis=1, keepdims=True))
     limit = CLIP_RATIO * jnp.sqrt(jnp.full((1, 1), D * KV, F32))
@@ -113,6 +113,13 @@
     moved = MOMENTUM_DECAY * momentum[...] + clipped
     new_momentum[...] = moved
     new_outer[...] = outer[...] - OUTER_LR * (clipped + MOMENTUM_DECAY * moved)
+    cols = near.shape[1]
+    for c in range(2):
+
+        @pl.when(core[0] == c)
+        def _(c=c):
+            projected[:, c * cols : (c + 1) * cols] = near[...]
+            projected[:, (1 - c) * cols : (2 - c) * cols] = far[...]
 
 
 def norm_body(hidden, gain, after, out):
@@ -200,32 +207,6 @@
     far[...] = total[count:].astype(BF16)
 
 
-def join_body(core, near, far, out):
-    cols = near.shape[1]
-
-    @pl.when(core[0] == 0)
-    def _():
-        out[:, :cols] = near[...]
-        out[:, cols:] = far[...]
-
-    @pl.when(core[0] == 1)
-    def _():
-        out[:, :cols] = far[...]
-        out[:, cols:] = near[...]
-
-
-def join(core, near, far):
-    rows, cols = near.shape
-    return pl.pallas_call(
-        join_body,
-        name="join",
-        out_shape=jax.ShapeDtypeStruct((rows, 2 * cols), BF16),
-        in_specs=[pl.BlockSpec(memory_space=pltpu.SMEM), VMEM, VMEM],
-        out_specs=VMEM,
-        compiler_params=PARAMS,
-    )(core, near, far)
-
-
 def exchange(array, axis, second):
     flips = (3, 1) if second else (1, 3)
     names = tuple(name for name in NAMES if name in (axis, "core"))
@@ -253,25 +234,23 @@
     swap = [(0, 1), (1, 0)]
 
     scalars = pl.BlockSpec(memory_space=pltpu.SMEM)
+    own, mine = call(
+        cut_body, "cut", (array(BF16, rows, cols), array(BF16, rows // 4, cols)), (jnp.stack([core, x]), proj_weight), first=scalars
+    )
     grouped, token = call(
-        regroup_body, "regroup", (array(BF16, 8, PIECE, KV), TOKEN), (replica_params[0],),
+        regroup_body, "regroup", (array(BF16, 8, PIECE, KV), TOKEN), (replica_params[0],), (mine,),
         scratch=[pltpu.VMEM((ROWS, KV), F32), pltpu.VMEM((8, PIECE, KV), F32)],
-    )
-    own, mine = call(
-        cut_body, "cut", (array(BF16, rows, cols), array(BF16, rows // 4, cols)),
-        (jnp.stack([core, x]), proj_weight), (token,), first=scalars,
     )
     grouped = lax.all_to_all(grouped, ("x", "core"), 0, 0)
     mirror = [(2 * z + h, 2 * (7 - z) + 1 - h) for z in range(8) for h in range(2)]
     other = lax.ppermute(mine, ("z_lo", "z_hi"), mirror)
     own_next = exchange(own, "y", False)
-    pieces, token = call(
+    normed = norm(hidden_in, norm_gain.reshape(1, -1), token)
+    pieces, token, normed = call(
         first_sum_body, "first_sum", (array(F32, 8, 56, LANES), TOKEN), (grouped,), (other, own_next),
-        scratch=[pltpu.VMEM((PIECE, KV), F32)],
+        scratch=[pltpu.VMEM((PIECE, KV), F32)], through=normed,
     )
     pieces = lax.all_to_all(pieces, "z_lo", 0, 0)
-    gain = norm_gain.reshape(1, -1)
-    normed = norm(hidden_in, gain, token)
     (early,) = call(lay_body, "pair", (array(BF16, 2, rows, cols),), (own, own_next), (token,))
     late = exchange(early, "y", True)
     (other,) = call(hold_body, "hold", (array(BF16, *other.shape),), (other,), (token,), cost=LONG)
@@ -299,10 +278,10 @@
         first=scalars, scratch=[pltpu.VMEM((4, rows, cols), BF16)], cost=LONG,
     )
     far = lax.ppermute(far, "core", swap)
-    new_outer, new_momentum = call(
-        update_body, "update", (array(F32, *share), array(F32, *share)), (squares, delta, outer_params, momentum)
-    )
-    projected = join(core.reshape(1), near, far)
+    new_outer, new_momentum, projected = call(
+        finish_body, "finish", (array(F32, *share), array(F32, *share), array(BF16, near.shape[0], KV)),
+        (core.reshape(1), squares, delta, outer_params, momentum, near, far), first=scalars,
+    )
     return (projected, new_outer, new_momentum)
 
 

time: 108 us -> 105 us (0.972)
  starting transfers between devices: 68.7 us -> 66.7 us
    ppermute x1, waiting for transfers between devices: 9.8 us -> 4.5 us  [on_device(): other = lax.ppermute(mine, ('z_lo', 'z_hi'), mirror)]
    ppermute x3, waiting for transfers between devices: 0.11 us -> 5.39 us  [spread(): lax.ppermute(array, axis, [(i, (i + s) % 4) for i in range(4)])]
  transfers between devices with their start and end apart: 14 -> 14, of which waited for: 4 -> 4; matrix products, arithmetic and copies ran while one was open for 0% -> 0% of each run, Pallas kernels for 12% -> 11%
where the time goes in v6:
time: 105 us; the launch traced here: 104 us
  starting transfers between devices  66.7 us (64%)
  waiting for transfers between devices  16 us (15%)
  Pallas kernels  15.9 us (15%)
  local copies, waits for them, and re-layouts  4.49 us (4%)
    ppermute x4, starting transfers between devices, exchange(): return lax.ppermute(array, names, pairs)  12.5 us
    all_to_all x1, starting transfers between devices, on_device(): grouped = lax.all_to_all(grouped, ('x', 'core'), 0, 0)  10.3 us
    ppermute x1, starting transfers between devices, on_device(): other = lax.ppermute(mine, ('z_lo', 'z_hi'), mirror)  9.31 us
    all_to_all x1, starting transfers between devices, on_device(): squares = lax.all_to_all(squares, ('z_lo', 'z_hi'), 0, 0)  9.14 us
    pallas_call x11, Pallas kernels, call(): pl.pallas_call(body, name=name, out_shape=out, in_specs=[first] + [VMEM]...  8.75 us
    ppermute x3, starting transfers between devices, spread(): lax.ppermute(array, axis, [(i, (i + s) % 4) for i in range(4)])  8.41 us
    all_to_all x1, starting transfers between devices, on_device(): pieces = lax.all_to_all(pieces, 'z_lo', 0, 0)  5.98 us
    ppermute x3, waiting for transfers between devices, spread(): lax.ppermute(array, axis, [(i, (i + s) % 4) for i in range(4)])  5.39 us
  transfers between devices with their start and end apart: 14, of which 4 were waited for; matrix products, arithmetic and copies ran while one was open for 0% of the time, Pallas kernels for 11%

profile of v6, /device:TPU:1, one launch (start us, length us, event | category | flops | bytes accessed | tf_op | source)
XLA Modules:
  0.0 104.1 jit_solution(10614636192878719192)
XLA Ops:
  0.7 1.2 %copy-done.1 = bf16[896,512]{1,0:T(8,128)(2,1)S(1)} copy-done((bf16[896,512]{1,0:T(8,128)(2,1)S(1)}, bf16[896,512]{1,0:T(8,128)(2,1)}, u32[]{:S(2)}) %copy-start.1) | copy-done | bytes 917528
  1.9 0.6 cut.1
  2.5 1.2 %copy-done.2 = bf16[1,896,512]{2,1,0:T(8,128)(2,1)S(1)} copy-done((bf16[1,896,512]{2,1,0:T(8,128)(2,1)S(1)}, bf16[1,896,512]{2,1,0:T(8,128)(2,1)}, u32[]{:S(2)}) %copy-start.2) | copy-done | bytes 917528
  3.7 1.3 %regroup.1 = (bf16[8,112,512]{2,1,0:T(8,128)(2,1)}, f32[8,128]{1,0:T(8,128)S(1)}) custom-call(bf16[896,512]{1,0:T(8,128)(2,1)S(1)} %bitcast.15, bf16[224,256]{1,0:T(8,128)(2,1)S(1)} %get-tuple-element.23.after), custom_call_target="tpu_custom_call" | custom-call | tf_op jit(solution)/shard_map/regroup/pallas_call | solution.py:40
  5.0 10.3 %all-to-all-start = ((bf16[8,112,512]{2,1,0:T(8,128)(2,1)}), bf16[8,112,512]{2,1,0:T(8,128)(2,1)S(1)}, u32[]{:S(2)}, u32[]{:S(2)}) async-start(bf16[8,112,512]{2,1,0:T(8,128)(2,1)} %get-tuple-element.24), calls=%async_computation | async-start | bytes 1835008 | tf_op jit(solution)/shard_map/all_to_all | solution.py:244
  15.3 1.9 %collective-permute-start.1 = (bf16[896,256]{1,0:T(8,128)(2,1)S(1)}, bf16[896,256]{1,0:T(8,128)(2,1)S(1)}, u32[]{:S(2)}, u32[]{:S(2)}) collective-permute-start(bf16[896,256]{1,0:T(8,128)(2,1)S(1)} %get-tuple-element.25.refs_0_), channel_id=1, source_target_pairs={{0,2},{8,14},{2,0},{10,12},{4,6},{12,10},{6,4},{14,8},{1,3},{9,15}... | collective-permute-start | bytes 1376264 | tf_op jit(solution)/shard_map/ppermute | solution.py:215
  17.2 9.3 %collective-permute-start = (bf16[224,256]{1,0:T(8,128)(2,1)S(1)}, bf16[224,256]{1,0:T(8,128)(2,1)S(1)}, u32[]{:S(2)}, u32[]{:S(2)}) collective-permute-start(bf16[224,256]{1,0:T(8,128)(2,1)S(1)} %get-tuple-element.23.after), channel_id=1, source_target_pairs={{0,449},{1,448},{64,385},{65,384},{128,321},{129,320},{192,257},{1... | collective-permute-start | bytes 344072 | tf_op jit(solution)/shard_map/ppermute | solution.py:246
  26.6 2.0 %copy-done = bf16[256,7168]{1,0:T(8,128)(2,1)S(1)} copy-done((bf16[256,7168]{1,0:T(8,128)(2,1)S(1)}, bf16[256,7168]{1,0:T(8,128)(2,1)}, u32[]{:S(2)}) %copy-start) | copy-done | bytes 3670040
  28.6 3.2 %norm.1.rest_2_ = bf16[256,7168]{1,0:T(8,128)(2,1)} custom-call(bf16[256,7168]{1,0:T(8,128)(2,1)S(1)} %copy-done, f32[1,7168]{1,0:T(1,128)S(1)} %bitcast.16, f32[8,128]{1,0:T(8,128)S(1)} %get-tuple-element.26.after), custom_call_target="tpu_custom_call" | custom-call | bytes 4294967296 | tf_op jit(solution)/shard_map/norm/pallas_call | solution.py:141
  31.8 4.5 %collective-permute-done.rest_0_.given = bf16[224,256]{1,0:T(8,128)(2,1)S(1)} collective-permute-done((bf16[224,256]{1,0:T(8,128)(2,1)S(1)}, bf16[224,256]{1,0:T(8,128)(2,1)S(1)}, u32[]{:S(2)}, u32[]{:S(2)}) %collective-permute-start) | collective-permute-done | bytes 114720 | tf_op jit(solution)/shard_map/ppermute | solution.py:246
  36.3 0.9 first_sum.1
  37.2 6.0 %all-to-all-start.1 = ((f32[8,56,128]{2,1,0:T(8,128)}), f32[8,56,128]{2,1,0:T(8,128)S(1)}, u32[]{:S(2)}, u32[]{:S(2)}) async-start(f32[8,56,128]{2,1,0:T(8,128)} %get-tuple-element.27), calls=%async_computation.1 | async-start | bytes 458752 | tf_op jit(solution)/shard_map/all_to_all | solution.py:253
  43.2 2.1 %collective-permute-start.2 = (bf16[224,256]{1,0:T(8,128)(2,1)S(1)}, bf16[224,256]{1,0:T(8,128)(2,1)S(1)}, u32[]{:S(2)}, u32[]{:S(2)}) collective-permute-start(bf16[224,256]{1,0:T(8,128)(2,1)S(1)} %hold.1.refs_0_), channel_id=1, source_target_pairs={{0,2},{2,4},{4,6},{6,0},{1,3},{3,5},{5,7},{7,1},{8,10},{10,12},{12... | collective-permute-start | bytes 344072 | tf_op jit(solution)/shard_map/ppermute | solution.py:222
  45.3 4.4 %collective-permute-start.3 = (bf16[224,256]{1,0:T(8,128)(2,1)S(1)}, bf16[224,256]{1,0:T(8,128)(2,1)S(1)}, u32[]{:S(2)}, u32[]{:S(2)}) collective-permute-start(bf16[224,256]{1,0:T(8,128)(2,1)S(1)} %hold.1.refs_0_), channel_id=1, source_target_pairs={{0,6},{2,0},{4,2},{6,4},{1,7},{3,1},{5,3},{7,5},{8,14},{10,8},{12,... | collective-permute-start | bytes 344072 | tf_op jit(solution)/shard_map/ppermute | solution.py:222
  49.7 1.9 %collective-permute-start.4 = (bf16[224,256]{1,0:T(8,128)(2,1)S(1)}, bf16[224,256]{1,0:T(8,128)(2,1)S(1)}, u32[]{:S(2)}, u32[]{:S(2)}) collective-permute-start(bf16[224,256]{1,0:T(8,128)(2,1)S(1)} %hold.1.refs_0_), channel_id=1, source_target_pairs={{0,4},{2,6},{4,0},{6,2},{1,5},{3,7},{5,1},{7,3},{8,12},{10,14},{12... | collective-permute-start | bytes 344072 | tf_op jit(solution)/shard_map/ppermute | solution.py:222
  51.7 5.4 %collective-permute-done.4.rest_2_.refs_3_ = bf16[224,256]{1,0:T(8,128)(2,1)S(1)} collective-permute-done((bf16[224,256]{1,0:T(8,128)(2,1)S(1)}, bf16[224,256]{1,0:T(8,128)(2,1)S(1)}, u32[]{:S(2)}, u32[]{:S(2)}) %collective-permute-start.4) | collective-permute-done | bytes 114720 | tf_op jit(solution)/shard_map/ppermute | solution.py:222
  57.1 0.7 second_sum.1
  57.8 3.8 %collective-permute-start.6 = (bf16[256,7168]{1,0:T(8,128)(2,1)}, bf16[256,7168]{1,0:T(8,128)(2,1)}, u32[]{:S(2)}, u32[]{:S(2)}) collective-permute-start(bf16[256,7168]{1,0:T(8,128)(2,1)} %get-tuple-element.34.normed), channel_id=1, source_target_pairs={{0,8},{8,0},{1,9},{9,1},{2,10},{10,2},{3,11},{11,3},{4,12},{12,4},... | collective-permute-start | bytes 11010056 | tf_op jit(solution)/shard_map/ppermute | solution.py:267
  61.6 5.5 %collective-permute-start.5 = (bf16[4,224,256]{2,1,0:T(8,128)(2,1)S(1)}, bf16[4,224,256]{2,1,0:T(8,128)(2,1)S(1)}, u32[]{:S(2)}, u32[]{:S(2)}) collective-permute-start(bf16[4,224,256]{2,1,0:T(8,128)(2,1)S(1)} %lay.1.refs_0_.quad), channel_id=1, source_target_pairs={{0,16},{8,56},{16,0},{24,40},{32,48},{40,24},{48,32},{56,8},{1,17}... | collective-permute-start | bytes 1376264 | tf_op jit(solution)/shard_map/ppermute | solution.py:215
  67.1 3.7 %all-to-all-start.2 = ((f32[32,8,128]{2,1,0:T(8,128)}), f32[32,8,128]{2,1,0:T(8,128)S(1)}, u32[]{:S(2)}, u32[]{:S(2)}) async-start(f32[32,8,128]{2,1,0:T(8,128)} %get-tuple-element.30), calls=%async_computation.2 | async-start | bytes 262144 | tf_op jit(solution)/shard_map/all_to_all | solution.py:262
  70.9 2.8 %collective-permute-start.7 = (bf16[2,896,256]{2,1,0:T(8,128)(2,1)S(1)}, bf16[2,896,256]{2,1,0:T(8,128)(2,1)S(1)}, u32[]{:S(2)}, u32[]{:S(2)}) collective-permute-start(bf16[2,896,256]{2,1,0:T(8,128)(2,1)S(1)} %pair.2.early), channel_id=1, source_target_pairs={{0,6},{8,10},{2,4},{10,8},{4,2},{12,14},{6,0},{14,12},{1,7},{9,11}... | collective-permute-start | bytes 2752520 | tf_op jit(solution)/shard_map/ppermute | solution.py:215
  73.7 4.3 %all-to-all-done.2.parts = f32[32,8,128]{2,1,0:T(8,128)S(1)} async-done(((f32[32,8,128]{2,1,0:T(8,128)}), f32[32,8,128]{2,1,0:T(8,128)S(1)}, u32[]{:S(2)}, u32[]{:S(2)}) %all-to-all-start.2) | async-done | bytes 131104 | tf_op jit(solution)/shard_map/all_to_all | solution.py:262
  78.0 0.7 spread_sum.1
  78.6 1.1 %pair.3 = bf16[2,4,224,256]{3,2,1,0:T(8,128)(2,1)} custom-call(bf16[4,224,256]{2,1,0:T(8,128)(2,1)S(1)} %lay.1.refs_0_.quad, bf16[4,224,256]{2,1,0:T(8,128)(2,1)S(1)} %collective-permute-done.5.rest_0_.refs_1_.quad_next, f32[8,128]{1,0:T(8,128)S(1)} %get-tuple-element.35.token.refs_2_), custom_call_target="tpu_custom_call" | custom-call | tf_op jit(solution)/shard_map/pair/pallas_call | solution.py:40
  79.7 2.3 %collective-permute-start.8 = (bf16[2,4,224,256]{3,2,1,0:T(8,128)(2,1)}, bf16[2,4,224,256]{3,2,1,0:T(8,128)(2,1)}, u32[]{:S(2)}, u32[]{:S(2)}) collective-permute-start(bf16[2,4,224,256]{3,2,1,0:T(8,128)(2,1)} %pair.3), channel_id=1, source_target_pairs={{0,48},{8,24},{16,32},{24,8},{32,16},{40,56},{48,0},{56,40},{1,49}... | collective-permute-start | bytes 2752520 | tf_op jit(solution)/shard_map/ppermute | solution.py:215
  82.0 9.1 %all-to-all-start.3 = ((f32[16,8,128]{2,1,0:T(8,128)}), f32[16,8,128]{2,1,0:T(8,128)S(1)}, u32[]{:S(2)}, u32[]{:S(2)}) async-start(f32[16,8,128]{2,1,0:T(8,128)} %get-tuple-element.32), calls=%async_computation.3 | async-start | bytes 131072 | tf_op jit(solution)/shard_map/all_to_all | solution.py:271
  91.2 0.1 stack.57.order
  91.3 3.9 %project_own.1 = (f32[512,256]{1,0:T(8,128)S(1)}, bf16[4,512,896]{2,1,0:T(8,128)(2,1)S(1)}) custom-call(s32[12]{0:T(128)S(1)} %stack.57.order, bf16[256,7168]{1,0:T(8,128)(2,1)} %get-tuple-element.34.normed, bf16[256,7168]{1,0:T(8,128)(2,1)} %collective-permute-done.6.far_normed, bf16[2,896,256]{2,1,0:T(8,128)(2,1)S(1)} %pair.2.early, ...), custom_call_target="tpu_custom_call" | custom-call | bytes 4294967296 | tf_op jit(solution)/shard_map/project_own/pallas_call | solution.py:187
  95.3 2.6 %project_other.1 = (bf16[256,256]{1,0:T(8,128)(2,1)S(1)}, bf16[256,256]{1,0:T(8,128)(2,1)S(1)}) custom-call(s32[12]{0:T(128)S(1)} %stack.57.order, bf16[4,512,896]{2,1,0:T(8,128)(2,1)S(1)} %get-tuple-element.36.kept, bf16[4,224,256]{2,1,0:T(8,128)(2,1)S(1)} %lay.1.refs_0_.quad, bf16[4,224,256]{2,1,0:T(8,128)(2,1)S(1)} %collective-permute-done.5.rest_0_.refs_1_.quad_next, ...), custom_call_target="tpu_custom_call" | custom-call | bytes 4294967296 | tf_op jit(solution)/shard_map/project_other/pallas_call | solution.py:40
  97.9 3.5 %collective-permute-start.9 = (bf16[256,256]{1,0:T(8,128)(2,1)S(1)}, bf16[256,256]{1,0:T(8,128)(2,1)S(1)}, u32[]{:S(2)}, u32[]{:S(2)}) collective-permute-start(bf16[256,256]{1,0:T(8,128)(2,1)S(1)} %get-tuple-element.39), channel_id=1, source_target_pairs={{0,8},{8,0},{1,9},{9,1},{2,10},{10,2},{3,11},{11,3},{4,12},{12,4},... | collective-permute-start | bytes 393224 | tf_op jit(solution)/shard_map/ppermute | solution.py:280
  101.4 1.8 %all-to-all-done.3.parts = f32[16,8,128]{2,1,0:T(8,128)S(1)} async-done(((f32[16,8,128]{2,1,0:T(8,128)}), f32[16,8,128]{2,1,0:T(8,128)S(1)}, u32[]{:S(2)}, u32[]{:S(2)}) %all-to-all-start.3) | async-done | bytes 65568 | tf_op jit(solution)/shard_map/all_to_all | solution.py:271
  103.3 0.9 finish.1
  (23 shorter events, 0.2 us)
Async XLA Ops:
  0.7 1.2 %copy-start.1 = (bf16[896,512]{1,0:T(8,128)(2,1)S(1)}, bf16[896,512]{1,0:T(8,128)(2,1)}, u32[]{:S(2)}) copy-start(bf16[896,512]{1,0:T(8,128)(2,1)} %weight.1) | copy-start | bytes 2752516
  1.9 24.6 %copy-start.5 = (f32[7168]{0:T(1024)S(1)}, f32[7168]{0:T(1024)}, u32[]{:S(2)}) copy-start(f32[7168]{0:T(1024)} %param.7) | copy-start | bytes 86020
  2.5 1.2 %copy-start.2 = (bf16[1,896,512]{2,1,0:T(8,128)(2,1)S(1)}, bf16[1,896,512]{2,1,0:T(8,128)(2,1)}, u32[]{:S(2)}) copy-start(bf16[1,896,512]{2,1,0:T(8,128)(2,1)} %param.9) | copy-start | bytes 2752516
  5.0 31.4 %all-to-all-start = ((bf16[8,112,512]{2,1,0:T(8,128)(2,1)}), bf16[8,112,512]{2,1,0:T(8,128)(2,1)S(1)}, u32[]{:S(2)}, u32[]{:S(2)}) async-start(bf16[8,112,512]{2,1,0:T(8,128)(2,1)} %get-tuple-element.24), calls=%async_computation | async-start | bytes 1835008 | tf_op jit(solution)/shard_map/all_to_all | solution.py:244
  15.3 21.0 %collective-permute-start.1 = (bf16[896,256]{1,0:T(8,128)(2,1)S(1)}, bf16[896,256]{1,0:T(8,128)(2,1)S(1)}, u32[]{:S(2)}, u32[]{:S(2)}) collective-permute-start(bf16[896,256]{1,0:T(8,128)(2,1)S(1)} %get-tuple-element.25.refs_0_), channel_id=1, source_target_pairs={{0,2},{8,14},{2,0},{10,12},{4,6},{12,10},{6,4},{14,8},{1,3},{9,15}... | collective-permute-start | bytes 1376264 | tf_op jit(solution)/shard_map/ppermute | solution.py:215
  17.2 19.1 %collective-permute-start = (bf16[224,256]{1,0:T(8,128)(2,1)S(1)}, bf16[224,256]{1,0:T(8,128)(2,1)S(1)}, u32[]{:S(2)}, u32[]{:S(2)}) collective-permute-start(bf16[224,256]{1,0:T(8,128)(2,1)S(1)} %get-tuple-element.23.after), channel_id=1, source_target_pairs={{0,449},{1,448},{64,385},{65,384},{128,321},{129,320},{192,257},{1... | collective-permute-start | bytes 344072 | tf_op jit(solution)/shard_map/ppermute | solution.py:246
  26.5 2.0 %copy-start = (bf16[256,7168]{1,0:T(8,128)(2,1)S(1)}, bf16[256,7168]{1,0:T(8,128)(2,1)}, u32[]{:S(2)}) copy-start(bf16[256,7168]{1,0:T(8,128)(2,1)} %hidden.1) | copy-start | bytes 11010052
  31.8 25.2 %copy-start.3 = (f32[14,512]{1,0:T(8,128)S(1)}, f32[14,512]{1,0:T(8,128)}, u32[]{:S(2)}) copy-start(f32[14,512]{1,0:T(8,128)} %outer.3) | copy-start | bytes 86020
  37.2 19.8 %all-to-all-start.1 = ((f32[8,56,128]{2,1,0:T(8,128)}), f32[8,56,128]{2,1,0:T(8,128)S(1)}, u32[]{:S(2)}, u32[]{:S(2)}) async-start(f32[8,56,128]{2,1,0:T(8,128)} %get-tuple-element.27), calls=%async_computation.1 | async-start | bytes 458752 | tf_op jit(solution)/shard_map/all_to_all | solution.py:253
  43.2 8.4 %collective-permute-start.2 = (bf16[224,256]{1,0:T(8,128)(2,1)S(1)}, bf16[224,256]{1,0:T(8,128)(2,1)S(1)}, u32[]{:S(2)}, u32[]{:S(2)}) collective-permute-start(bf16[224,256]{1,0:T(8,128)(2,1)S(1)} %hold.1.refs_0_), channel_id=1, source_target_pairs={{0,2},{2,4},{4,6},{6,0},{1,3},{3,5},{5,7},{7,1},{8,10},{10,12},{12... | collective-permute-start | bytes 344072 | tf_op jit(solution)/shard_map/ppermute | solution.py:222
  45.3 6.4 %collective-permute-start.3 = (bf16[224,256]{1,0:T(8,128)(2,1)S(1)}, bf16[224,256]{1,0:T(8,128)(2,1)S(1)}, u32[]{:S(2)}, u32[]{:S(2)}) collective-permute-start(bf16[224,256]{1,0:T(8,128)(2,1)S(1)} %hold.1.refs_0_), channel_id=1, source_target_pairs={{0,6},{2,0},{4,2},{6,4},{1,7},{3,1},{5,3},{7,5},{8,14},{10,8},{12,... | collective-permute-start | bytes 344072 | tf_op jit(solution)/shard_map/ppermute | solution.py:222
  49.7 7.3 %collective-permute-start.4 = (bf16[224,256]{1,0:T(8,128)(2,1)S(1)}, bf16[224,256]{1,0:T(8,128)(2,1)S(1)}, u32[]{:S(2)}, u32[]{:S(2)}) collective-permute-start(bf16[224,256]{1,0:T(8,128)(2,1)S(1)} %hold.1.refs_0_), channel_id=1, source_target_pairs={{0,4},{2,6},{4,0},{6,2},{1,5},{3,7},{5,1},{7,3},{8,12},{10,14},{12... | collective-permute-start | bytes 344072 | tf_op jit(solution)/shard_map/ppermute | solution.py:222
  57.8 33.6 %collective-permute-start.6 = (bf16[256,7168]{1,0:T(8,128)(2,1)}, bf16[256,7168]{1,0:T(8,128)(2,1)}, u32[]{:S(2)}, u32[]{:S(2)}) collective-permute-start(bf16[256,7168]{1,0:T(8,128)(2,1)} %get-tuple-element.34.normed), channel_id=1, source_target_pairs={{0,8},{8,0},{1,9},{9,1},{2,10},{10,2},{3,11},{11,3},{4,12},{12,4},... | collective-permute-start | bytes 11010056 | tf_op jit(solution)/shard_map/ppermute | solution.py:267
  61.6 16.3 %collective-permute-start.5 = (bf16[4,224,256]{2,1,0:T(8,128)(2,1)S(1)}, bf16[4,224,256]{2,1,0:T(8,128)(2,1)S(1)}, u32[]{:S(2)}, u32[]{:S(2)}) collective-permute-start(bf16[4,224,256]{2,1,0:T(8,128)(2,1)S(1)} %lay.1.refs_0_.quad), channel_id=1, source_target_pairs={{0,16},{8,56},{16,0},{24,40},{32,48},{40,24},{48,32},{56,8},{1,17}... | collective-permute-start | bytes 1376264 | tf_op jit(solution)/shard_map/ppermute | solution.py:215
  67.1 10.8 %all-to-all-start.2 = ((f32[32,8,128]{2,1,0:T(8,128)}), f32[32,8,128]{2,1,0:T(8,128)S(1)}, u32[]{:S(2)}, u32[]{:S(2)}) async-start(f32[32,8,128]{2,1,0:T(8,128)} %get-tuple-element.30), calls=%async_computation.2 | async-start | bytes 262144 | tf_op jit(solution)/shard_map/all_to_all | solution.py:262
  70.9 20.5 %collective-permute-start.7 = (bf16[2,896,256]{2,1,0:T(8,128)(2,1)S(1)}, bf16[2,896,256]{2,1,0:T(8,128)(2,1)S(1)}, u32[]{:S(2)}, u32[]{:S(2)}) collective-permute-start(bf16[2,896,256]{2,1,0:T(8,128)(2,1)S(1)} %pair.2.early), channel_id=1, source_target_pairs={{0,6},{8,10},{2,4},{10,8},{4,2},{12,14},{6,0},{14,12},{1,7},{9,11}... | collective-permute-start | bytes 2752520 | tf_op jit(solution)/shard_map/ppermute | solution.py:215
  79.7 15.6 %collective-permute-start.8 = (bf16[2,4,224,256]{3,2,1,0:T(8,128)(2,1)}, bf16[2,4,224,256]{3,2,1,0:T(8,128)(2,1)}, u32[]{:S(2)}, u32[]{:S(2)}) collective-permute-start(bf16[2,4,224,256]{3,2,1,0:T(8,128)(2,1)} %pair.3), channel_id=1, source_target_pairs={{0,48},{8,24},{16,32},{24,8},{32,16},{40,56},{48,0},{56,40},{1,49}... | collective-permute-start | bytes 2752520 | tf_op jit(solution)/shard_map/ppermute | solution.py:215
  82.0 21.3 %all-to-all-start.3 = ((f32[16,8,128]{2,1,0:T(8,128)}), f32[16,8,128]{2,1,0:T(8,128)S(1)}, u32[]{:S(2)}, u32[]{:S(2)}) async-start(f32[16,8,128]{2,1,0:T(8,128)} %get-tuple-element.32), calls=%async_computation.3 | async-start | bytes 131072 | tf_op jit(solution)/shard_map/all_to_all | solution.py:271
  95.3 8.0 %copy-start.4 = (f32[14,512]{1,0:T(8,128)S(1)}, f32[14,512]{1,0:T(8,128)}, u32[]{:S(2)}) copy-start(f32[14,512]{1,0:T(8,128)} %momentum.1) | copy-start | bytes 86020
  97.9 5.4 %collective-permute-start.9 = (bf16[256,256]{1,0:T(8,128)(2,1)S(1)}, bf16[256,256]{1,0:T(8,128)(2,1)S(1)}, u32[]{:S(2)}, u32[]{:S(2)}) collective-permute-start(bf16[256,256]{1,0:T(8,128)(2,1)S(1)} %get-tuple-element.39), channel_id=1, source_target_pairs={{0,8},{8,0},{1,9},{9,1},{2,10},{10,2},{3,11},{11,3},{4,12},{12,4},... | collective-permute-start | bytes 393224 | tf_op jit(solution)/shard_map/ppermute | solution.py:280
